TPU v7x, 32 devices: a whole 2x2x4 slice. The times are simulated.
32 devices in a mesh: dp: 8 (over y, x, core), shard: 4 (over z).
Axes of the slice: x: 2, y: 2, z: 4, core: 2. Of those that a mesh axis runs over, the one named last changes fastest.
Arguments:
- tokens: bfloat16 [16384, 1024], P(('dp', 'shard')), may hold values from -6 to 6
- attn_gain: bfloat16 [1024], P('shard'), may hold values from 0.099609375 to 1.8984375
- w_query: bfloat16 [1024, 2048], P('shard'), may hold values from -0.1875 to 0.1875
- w_key: bfloat16 [1024, 1024], P('shard'), may hold values from -0.1875 to 0.1875
- w_value: bfloat16 [1024, 1024], P('shard'), may hold values from -0.1875 to 0.1875
- q_gain: bfloat16 [128], P('shard'), may hold values from 0.099609375 to 1.8984375
- k_gain: bfloat16 [128], P('shard'), may hold values from 0.099609375 to 1.8984375
- w_out: bfloat16 [2048, 1024], P('shard'), may hold values from -0.75 to 0.75
- mlp_gain: bfloat16 [1024], P('shard'), may hold values from 0.099609375 to 1.8984375
- w_gate: bfloat16 [1024, 3072], P('shard'), may hold values from -0.1875 to 0.1875
- w_up: bfloat16 [1024, 3072], P('shard'), may hold values from -0.1875 to 0.1875
- w_down: bfloat16 [3072, 1024], P('shard'), may hold values from -0.109375 to 0.109375
- segments: int32 [8, 2048], P('dp'), may hold values from 0 to 7, as said below
- spans: int32 [8, 4], P('dp'), may hold values from 0 to 3, each once within a row
- out_grad: bfloat16 [16384, 1024], P(('dp', 'shard')), may hold values from -6 to 6
Outputs:
- result: bfloat16 [16384, 1024], P(('dp', 'shard'))
- grad_tokens: float32 [16384, 1024], P(('dp', 'shard'))
- grad_attn_gain: float32 [1024], P('shard')
- grad_w_query: float32 [1024, 2048], P('shard')
- grad_w_key: float32 [1024, 1024], P('shard')
- grad_w_value: float32 [1024, 1024], P('shard')
- grad_q_gain: float32 [128], P('shard')
- grad_k_gain: float32 [128], P('shard')
- grad_w_out: float32 [2048, 1024], P('shard')
- grad_mlp_gain: float32 [1024], P('shard')
- grad_w_gate: float32 [1024, 3072], P('shard')
- grad_w_up: float32 [1024, 3072], P('shard')
- grad_w_down: float32 [3072, 1024], P('shard')
Inputs may be any that keep to these rules, and one draw needn't show every extreme that they name: `segments`: segment numbers never fall along a sequence; positions 0 to 1023 form one document and position 1024 begins another. Each row is a permutation: device j of group i holds sequence blocks spans[i, j] and 7 - spans[i, j].
All inputs are finite; a program needn't handle non-finite values.
Results may differ from a plain program's by a relative error of at most 0.024.
Values may be sent and summed in bfloat16 or wider, within the bound.
No kernel may reach another device: no remote copies, remote signals or barrier semaphores. Data moves between devices by JAX's collectives and lax.ppermute only.
A program may use at most 384 MiB of HBM per device.

v0:
```python
import jax
import jax.numpy as jnp
from jax import lax
from jax.sharding import PartitionSpec as P

HEADS = 16
KV_HEADS = 8
HEAD_WIDTH = 128
TOK_DEV = 512


EPS = 1e-06
THETA = 1000000.0
NEG = -1e30


def rms_norm(values, gain):
    return values * lax.rsqrt(jnp.mean(values * values, axis=-1, keepdims=True) + EPS) * gain


def rope_tables(positions):
    steps = jnp.arange(HEAD_WIDTH // 2, dtype=jnp.float32) * (2.0 / HEAD_WIDTH)
    inverse = jnp.power(jnp.float32(THETA), -steps)
    angles = positions.astype(jnp.float32)[:, None] * inverse[None, :]
    angles = jnp.concatenate([angles, angles], axis=1)[:, None, :]
    return (jnp.cos(angles), jnp.sin(angles))


def rotate(values, cosine, sine):
    first = values[..., : HEAD_WIDTH // 2]
    second = values[..., HEAD_WIDTH // 2 :]
    turned = jnp.concatenate([-second, first], axis=-1)
    return values * cosine + turned * sine


def layout(segment_row, span_row, shards):
    length = segment_row.shape[0]
    block_len = length // (2 * shards)
    mirror = 2 * shards - 1 - span_row
    blocks = jnp.stack([span_row, mirror], axis=1).reshape(2 * shards)
    offsets = jnp.arange(block_len, dtype=jnp.int32)
    place = (blocks[:, None] * block_len + offsets[None, :]).reshape(length)
    indices = jnp.arange(length, dtype=jnp.int32)
    fresh = jnp.concatenate([jnp.ones((1,), jnp.bool_), segment_row[1:] != segment_row[:-1]])
    doc_start = lax.cummax(jnp.where(fresh, indices, 0), axis=0)
    seg_blocks = segment_row.reshape(2 * shards, block_len)
    start_blocks = doc_start.reshape(2 * shards, block_len)
    seg_tok = jnp.take(seg_blocks, blocks, axis=0).reshape(length)
    rope_pos = place - jnp.take(start_blocks, blocks, axis=0).reshape(length)
    return (place, seg_tok, rope_pos)


def head_norms(queries, keys_pre, q_weight, k_weight, cosine, sine):
    q_rot = rotate(rms_norm(queries, q_weight), cosine, sine)
    k_rot = rotate(rms_norm(keys_pre, k_weight), cosine, sine)
    return (q_rot, k_rot)


def swiglu(gate, upward):
    return jax.nn.silu(gate) * upward


def key_mask(start, rows, q_place, q_seg, place_all, seg_all):
    key_place = lax.dynamic_slice_in_dim(place_all, start, rows)
    key_seg = lax.dynamic_slice_in_dim(seg_all, start, rows)
    return (q_seg[:, None] == key_seg[None, :]) & (key_place[None, :] <= q_place[:, None])


def attend_block(state, piece, start, query_block, q_place, q_seg, place_all, seg_all):
    rows = piece.shape[0]
    width = KV_HEADS * HEAD_WIDTH
    softmax_scale = HEAD_WIDTH ** (-0.5)
    allowed = key_mask(start, rows, q_place, q_seg, place_all, seg_all)
    top, total, summed = state
    partial_key_rows = piece[:, :width].reshape(rows, KV_HEADS, HEAD_WIDTH)
    partial_value_rows = piece[:, width:].reshape(rows, KV_HEADS, HEAD_WIDTH)
    score_matrix = (
        jnp.einsum(
            "micf,yif->icmy", query_block, partial_key_rows, preferred_element_type=jnp.float32
        )
        * softmax_scale
    )
    score_matrix = jnp.where(allowed, score_matrix, NEG)
    new_top = jnp.maximum(top, jnp.max(score_matrix, axis=-1))
    raised = jnp.where(allowed, jnp.exp(score_matrix - new_top[..., None]), 0.0)
    total = jnp.sum(raised, axis=-1)
    added = jnp.einsum(
        "xjvb,bxu->vxju",
        raised.astype(jnp.bfloat16),
        partial_value_rows,
        preferred_element_type=jnp.float32,
    )
    summed = added
    return (new_top, total, summed)


def body(
    tokens,
    attn_gain,
    w_query,
    w_key,
    w_value,
    q_gain,
    k_gain,
    w_out,
    mlp_gain,
    w_gate,
    w_up,
    w_down,
    segments,
    spans,
    out_grad,
):
    compute_dtype = jnp.float32
    half_type = jnp.bfloat16
    shards = lax.axis_size("shard")
    groups = HEADS // KV_HEADS
    width = KV_HEADS * HEAD_WIDTH
    softmax_scale = HEAD_WIDTH ** (-0.5)
    place_all, seg_all, rope_all = layout(segments[0], spans[0], shards)
    mine = lax.axis_index("shard") * TOK_DEV
    q_place = lax.dynamic_slice_in_dim(place_all, mine, TOK_DEV)
    q_seg = lax.dynamic_slice_in_dim(seg_all, mine, TOK_DEV)
    q_rope = lax.dynamic_slice_in_dim(rope_all, mine, TOK_DEV)
    cosine, sine = rope_tables(q_rope)
    inputs = tokens.astype(compute_dtype)
    attn_set = (
        lax.all_gather(attn_gain, "shard", axis=0, tiled=True),
        lax.all_gather(w_query, "shard", axis=0, tiled=True),
        lax.all_gather(w_key, "shard", axis=0, tiled=True),
        lax.all_gather(w_value, "shard", axis=0, tiled=True),
        lax.all_gather(q_gain, "shard", axis=0, tiled=True),
        lax.all_gather(k_gain, "shard", axis=0, tiled=True),
        lax.all_gather(w_out, "shard", axis=0, tiled=True),
    )
    normed, pull_attn_norm = jax.vjp(rms_norm, inputs, attn_set[0].astype(compute_dtype))
    normed_b = normed.astype(half_type)
    queries = jnp.dot(normed_b, attn_set[1], preferred_element_type=compute_dtype).reshape(
        TOK_DEV, HEADS, HEAD_WIDTH
    )
    keys_pre = jnp.dot(normed_b, attn_set[2], preferred_element_type=compute_dtype).reshape(
        TOK_DEV, KV_HEADS, HEAD_WIDTH
    )
    values_b = jnp.dot(normed_b, attn_set[3], preferred_element_type=compute_dtype).astype(
        half_type
    )

    def norms_here(query_in, key_in, q_weight, k_weight):
        return head_norms(query_in, key_in, q_weight, k_weight, cosine, sine)

    (q_rot, k_rot), pull_heads = jax.vjp(
        norms_here,
        queries,
        keys_pre,
        attn_set[4].astype(compute_dtype),
        attn_set[5].astype(compute_dtype),
    )
    query_block = q_rot.astype(half_type).reshape(TOK_DEV, KV_HEADS, groups, HEAD_WIDTH)
    k_b = k_rot.astype(half_type).reshape(TOK_DEV, width)
    key_values = jnp.concatenate([k_b, values_b], axis=1)
    begin = (
        jnp.full((KV_HEADS, groups, TOK_DEV), NEG, compute_dtype),
        jnp.zeros((KV_HEADS, groups, TOK_DEV), compute_dtype),
        jnp.zeros((TOK_DEV, KV_HEADS, groups, HEAD_WIDTH), compute_dtype),
    )
    top, total, summed = attend_block(
        begin,
        lax.all_gather(key_values, "shard", axis=0, tiled=True),
        jnp.int32(0),
        query_block,
        q_place,
        q_seg,
        place_all,
        seg_all,
    )
    attended = summed / jnp.transpose(total, (2, 0, 1))[..., None]
    log_total = top + jnp.log(total)
    attended_b = attended.astype(half_type).reshape(TOK_DEV, HEADS * HEAD_WIDTH)
    residual = inputs + jnp.dot(attended_b, attn_set[6], preferred_element_type=compute_dtype)
    mlp_set = (
        lax.all_gather(mlp_gain, "shard", axis=0, tiled=True),
        lax.all_gather(w_gate, "shard", axis=0, tiled=True),
        lax.all_gather(w_up, "shard", axis=0, tiled=True),
        lax.all_gather(w_down, "shard", axis=0, tiled=True),
    )
    mixed_heads, pull_mlp_norm = jax.vjp(rms_norm, residual, mlp_set[0].astype(compute_dtype))
    mixed_b = mixed_heads.astype(half_type)
    gate = jnp.dot(mixed_b, mlp_set[1], preferred_element_type=compute_dtype)
    upward = jnp.dot(mixed_b, mlp_set[2], preferred_element_type=compute_dtype)
    hidden, pull_swiglu = jax.vjp(swiglu, gate, upward)
    hidden_b = hidden.astype(half_type)
    result = (
        residual + jnp.dot(hidden_b, mlp_set[3], preferred_element_type=compute_dtype)
    ).astype(half_type)
    mlp_back = (
        lax.all_gather(mlp_gain, "shard", axis=0, tiled=True),
        lax.all_gather(w_gate, "shard", axis=0, tiled=True),
        lax.all_gather(w_up, "shard", axis=0, tiled=True),
        lax.all_gather(w_down, "shard", axis=0, tiled=True),
    )
    grad_down = jnp.einsum("tf,td->fd", hidden_b, out_grad, preferred_element_type=compute_dtype)
    grad_hidden = jnp.einsum(
        "td,fd->tf", out_grad, mlp_back[3], preferred_element_type=compute_dtype
    )
    grad_gate, grad_upward = pull_swiglu(grad_hidden)
    gate_b = grad_gate.astype(half_type)
    upward_b = grad_upward.astype(half_type)
    grad_wgate = jnp.einsum("td,tf->df", mixed_b, gate_b, preferred_element_type=compute_dtype)
    grad_wup = jnp.einsum("td,tf->df", mixed_b, upward_b, preferred_element_type=compute_dtype)
    grad_mixed = jnp.einsum("tf,df->td", gate_b, mlp_back[1], preferred_element_type=compute_dtype)
    grad_mixed = grad_mixed + jnp.einsum(
        "tf,df->td", upward_b, mlp_back[2], preferred_element_type=compute_dtype
    )
    grad_residual, grad_mgain = pull_mlp_norm(grad_mixed)
    grad_residual = grad_residual + out_grad.astype(compute_dtype)
    mlp_own = (
        lax.psum_scatter(
            grad_mgain.astype(jnp.bfloat16), "shard", scatter_dimension=0, tiled=True
        ).astype(jnp.float32),
        lax.psum_scatter(
            grad_wgate.astype(jnp.bfloat16), "shard", scatter_dimension=0, tiled=True
        ).astype(jnp.float32),
        lax.psum_scatter(
            grad_wup.astype(jnp.bfloat16), "shard", scatter_dimension=0, tiled=True
        ).astype(jnp.float32),
        lax.psum_scatter(
            grad_down.astype(jnp.bfloat16), "shard", scatter_dimension=0, tiled=True
        ).astype(jnp.float32),
    )
    attn_back = (
        lax.all_gather(attn_gain, "shard", axis=0, tiled=True),
        lax.all_gather(w_query, "shard", axis=0, tiled=True),
        lax.all_gather(w_key, "shard", axis=0, tiled=True),
        lax.all_gather(w_value, "shard", axis=0, tiled=True),
        lax.all_gather(q_gain, "shard", axis=0, tiled=True),
        lax.all_gather(k_gain, "shard", axis=0, tiled=True),
        lax.all_gather(w_out, "shard", axis=0, tiled=True),
    )
    grad_branch = grad_residual.astype(half_type)
    grad_wout = jnp.einsum(
        "tc,td->cd", attended_b, grad_branch, preferred_element_type=compute_dtype
    )
    grad_attended_rows = jnp.einsum(
        "td,cd->tc", grad_branch, attn_back[6], preferred_element_type=compute_dtype
    )
    grad_attended_rows = grad_attended_rows.astype(half_type).reshape(
        TOK_DEV, KV_HEADS, groups, HEAD_WIDTH
    )
    row_dots = jnp.transpose(
        jnp.sum(grad_attended_rows.astype(compute_dtype) * attended, axis=-1), (1, 2, 0)
    )
    every_kv = lax.all_gather(key_values, "shard", axis=0, tiled=True)
    pieces = every_kv.reshape(shards, TOK_DEV, 2 * width)
    starts = jnp.arange(shards, dtype=jnp.int32) * TOK_DEV

    def back_step(grad_query, item):
        piece, start = item
        allowed = key_mask(start, TOK_DEV, q_place, q_seg, place_all, seg_all)
        grad_now = grad_query
        partial_key_rows = piece[:, :width].reshape(TOK_DEV, KV_HEADS, HEAD_WIDTH)
        partial_value_rows = piece[:, width:].reshape(TOK_DEV, KV_HEADS, HEAD_WIDTH)
        score_matrix = (
            jnp.einsum(
                "micf,yif->icmy",
                query_block,
                partial_key_rows,
                preferred_element_type=compute_dtype,
            )
            * softmax_scale
        )
        probability_rows = jnp.where(allowed, jnp.exp(score_matrix - log_total[..., None]), 0.0)
        grad_shares = jnp.einsum(
            "micf,yif->icmy",
            grad_attended_rows,
            partial_value_rows,
            preferred_element_type=compute_dtype,
        )
        grad_score_matrix = (probability_rows * (grad_shares - row_dots[..., None])).astype(
            half_type
        )
        grad_now = (
            grad_now
            + jnp.einsum(
                "xjvb,bxu->vxju",
                grad_score_matrix,
                partial_key_rows,
                preferred_element_type=compute_dtype,
            )
            * softmax_scale
        )
        grad_keys = (
            jnp.einsum(
                "kcei,ekcv->ikv",
                grad_score_matrix,
                query_block,
                preferred_element_type=compute_dtype,
            )
            * softmax_scale
        )
        grad_values = jnp.einsum(
            "kcei,ekcv->ikv",
            probability_rows.astype(half_type),
            grad_attended_rows,
            preferred_element_type=compute_dtype,
        )
        joined = jnp.concatenate(
            [grad_keys.reshape(TOK_DEV, width), grad_values.reshape(TOK_DEV, width)], axis=1
        )
        return (grad_now, joined.astype(half_type))

    grad_query, kv_terms = lax.scan(
        back_step,
        jnp.zeros((TOK_DEV, KV_HEADS, groups, HEAD_WIDTH), compute_dtype),
        (pieces, starts),
    )
    grad_kv = lax.psum_scatter(
        kv_terms.reshape(shards * TOK_DEV, 2 * width).astype(compute_dtype).astype(jnp.bfloat16),
        "shard",
        scatter_dimension=0,
        tiled=True,
    ).astype(jnp.float32)
    grad_keys_rot = grad_kv[:, :width].reshape(TOK_DEV, KV_HEADS, HEAD_WIDTH)
    grad_values_b = grad_kv[:, width:].astype(half_type)
    grad_queries, grad_keys_pre, grad_qgain, grad_kgain = pull_heads(
        (grad_query.reshape(TOK_DEV, HEADS, HEAD_WIDTH), grad_keys_rot)
    )
    queries_b = grad_queries.reshape(TOK_DEV, HEADS * HEAD_WIDTH).astype(half_type)
    keys_b = grad_keys_pre.reshape(TOK_DEV, width).astype(half_type)
    grad_wquery = jnp.einsum("td,tc->dc", normed_b, queries_b, preferred_element_type=compute_dtype)
    grad_wkey = jnp.einsum("td,tc->dc", normed_b, keys_b, preferred_element_type=compute_dtype)
    grad_wvalue = jnp.einsum(
        "td,tc->dc", normed_b, grad_values_b, preferred_element_type=compute_dtype
    )
    grad_normed = jnp.einsum(
        "tc,dc->td", queries_b, attn_back[1], preferred_element_type=compute_dtype
    )
    grad_normed = grad_normed + jnp.einsum(
        "tc,dc->td", keys_b, attn_back[2], preferred_element_type=compute_dtype
    )
    grad_normed = grad_normed + jnp.einsum(
        "tc,dc->td", grad_values_b, attn_back[3], preferred_element_type=compute_dtype
    )
    grad_inputs, grad_again = pull_attn_norm(grad_normed)
    grad_inputs = grad_residual + grad_inputs
    attn_own = (
        lax.psum_scatter(
            grad_again.astype(jnp.bfloat16), "shard", scatter_dimension=0, tiled=True
        ).astype(jnp.float32),
        lax.psum_scatter(
            grad_wquery.astype(jnp.bfloat16), "shard", scatter_dimension=0, tiled=True
        ).astype(jnp.float32),
        lax.psum_scatter(
            grad_wkey.astype(jnp.bfloat16), "shard", scatter_dimension=0, tiled=True
        ).astype(jnp.float32),
        lax.psum_scatter(
            grad_wvalue.astype(jnp.bfloat16), "shard", scatter_dimension=0, tiled=True
        ).astype(jnp.float32),
        lax.psum_scatter(
            grad_qgain.astype(jnp.bfloat16), "shard", scatter_dimension=0, tiled=True
        ).astype(jnp.float32),
        lax.psum_scatter(
            grad_kgain.astype(jnp.bfloat16), "shard", scatter_dimension=0, tiled=True
        ).astype(jnp.float32),
        lax.psum_scatter(
            grad_wout.astype(jnp.bfloat16), "shard", scatter_dimension=0, tiled=True
        ).astype(jnp.float32),
    )
    summed_all = (
        lax.psum(attn_own[0].astype(jnp.bfloat16), "dp").astype(jnp.float32),
        lax.psum(attn_own[1].astype(jnp.bfloat16), "dp").astype(jnp.float32),
        lax.psum(attn_own[2].astype(jnp.bfloat16), "dp").astype(jnp.float32),
        lax.psum(attn_own[3].astype(jnp.bfloat16), "dp").astype(jnp.float32),
        lax.psum(attn_own[4].astype(jnp.bfloat16), "dp").astype(jnp.float32),
        lax.psum(attn_own[5].astype(jnp.bfloat16), "dp").astype(jnp.float32),
        lax.psum(attn_own[6].astype(jnp.bfloat16), "dp").astype(jnp.float32),
        lax.psum(mlp_own[0].astype(jnp.bfloat16), "dp").astype(jnp.float32),
        lax.psum(mlp_own[1].astype(jnp.bfloat16), "dp").astype(jnp.float32),
        lax.psum(mlp_own[2].astype(jnp.bfloat16), "dp").astype(jnp.float32),
        lax.psum(mlp_own[3].astype(jnp.bfloat16), "dp").astype(jnp.float32),
    )
    attn_final = summed_all[:7]
    mlp_final = summed_all[7:]
    return (
        result,
        grad_inputs,
        attn_final[0],
        attn_final[1],
        attn_final[2],
        attn_final[3],
        attn_final[4],
        attn_final[5],
        attn_final[6],
        mlp_final[0],
        mlp_final[1],
        mlp_final[2],
        mlp_final[3],
    )


def solution(mesh):
    placed = (
        P(("dp", "shard"), None),
        P("shard"),
        P("shard", None),
        P("shard", None),
        P("shard", None),
        P("shard"),
        P("shard"),
        P("shard", None),
        P("shard"),
        P("shard", None),
        P("shard", None),
        P("shard", None),
        P("dp", None),
        P("dp", None),
        P(("dp", "shard"), None),
    )
    return jax.shard_map(
        body,
        mesh=mesh,
        in_specs=placed,
        out_specs=(
            P(("dp", "shard"), None),
            P(("dp", "shard"), None),
            P("shard"),
            P("shard", None),
            P("shard", None),
            P("shard", None),
            P("shard"),
            P("shard"),
            P("shard", None),
            P("shard"),
            P("shard", None),
            P("shard", None),
            P("shard", None),
        ),
        check_vma=False,
    )
```

profile of v0, /device:TPU:0, one launch (start us, length us, event | category | flops | bytes accessed | tf_op | source)
XLA Modules:
  0.0 1932.9 jit_solution(6342382721476863069)
XLA Ops:
  10.1 12.6 all-gather
  38.1 20.5 %all-gather.11.cloned.1.call-done = bf16[1024,1024]{1,0:T(8,128)(2,1)} async-done(((bf16[256,1024]{1,0:T(8,128)(2,1)}), bf16[1024,1024]{1,0:T(8,128)(2,1)}) %all-gather.11.cloned.1.call-update) | async-done | bytes 2097168 | tf_op jit(solution)/shard_map/all_gather | solution.py:130
  65.9 38.9 %all-gather.13.cloned.1.call-done = bf16[1024,1024]{1,0:T(8,128)(2,1)} async-done(((bf16[256,1024]{1,0:T(8,128)(2,1)}), bf16[1024,1024]{1,0:T(8,128)(2,1)}) %all-gather.13.cloned.1.call-update) | async-done | bytes 2097168 | tf_op jit(solution)/shard_map/all_gather | solution.py:131
  127.3 58.6 %all-gather.17.cloned.1.call-done = bf16[1024,2048]{1,0:T(8,128)(2,1)} async-done(((bf16[256,2048]{1,0:T(8,128)(2,1)}), bf16[1024,2048]{1,0:T(8,128)(2,1)}) %all-gather.17.cloned.1.call-update) | async-done | bytes 4194320 | tf_op jit(solution)/shard_map/all_gather | solution.py:129
  201.7 134.4 %all-gather.15.cloned.1.call-done = bf16[2048,2048]{1,0:T(8,128)(2,1)} async-done(((bf16[512,2048]{1,0:T(8,128)(2,1)}), bf16[2048,2048]{1,0:T(8,128)(2,1)}) %all-gather.15.cloned.1.call-update) | async-done | bytes 8388624 | tf_op jit(solution)/shard_map/all_gather | solution.py:168
  344.7 28.1 %fusion.13 = (f32[8,2,512]{2,1,0:T(2,128)S(1)}, f32[8,2048,512,2]{2,1,3,0:T(8,128)}) fusion(pred[512,2048]{0,1:T(8,128)(4,1)S(1)} %compare_and_fusion.1, bf16[512,8,2,128]{0,3,2,1:T(8,128)(2,1)} %fusion.25, bf16[2048,8,128,1]{2,1,0,3:T(8,128)(2,1)} %bitcast.265), kind=kOutput, calls=%fused_computation.23 | convolution fusion | flops 4345290752 | bytes 74481664 | tf_op jit(solution)/shard_map/micf,yif->icmy/dot_general | solution.py:78
  372.7 22.2 %fusion.14 = f32[8,2,512]{2,1,0:T(2,128)S(1)} fusion(f32[8,2048,512,2]{2,1,3,0:T(8,128)} %get-tuple-element.258, f32[8,2,512]{2,1,0:T(2,128)S(1)} %broadcast_maximum_fusion, pred[512,2048]{0,1:T(8,128)(4,1)S(1)} %compare_and_fusion.1), kind=kLoop, calls=%fused_computation.24 | loop fusion | flops 83877888 | bytes 68222976 | tf_op jit(solution)/shard_map/reduce_sum | solution.py:86
  401.5 29.7 %fusion.76 = (bf16[512,8,2,128]{0,3,2,1:T(8,128)(2,1)}, f32[512,8,2,128]{0,3,2,1:T(8,128)}) fusion(f32[512,8,2]{0,2,1:T(2,128)S(1)} %bitcast.270, bf16[2048,8,128,1]{0,2,3,1:T(8,128)(2,1)} %bitcast.264, f32[8,2048,512,2]{2,1,3,0:T(8,128)} %get-tuple-element.258, f32[8,2,512]{2,1,0:T(2,128)S(1)} %broadcast_maximum_fusion, ...), kind=kOutput, calls=%fused_computation.162 | convolution fusion | flops 4380950528 | bytes 78708736 | tf_op jit(solution)/shard_map/xjvb,bxu->vxju/dot_general | solution.py:87
  436.8 95.1 %all-gather.21.cloned.1.call-done = bf16[1024,3072]{1,0:T(8,128)(2,1)} async-done(((bf16[256,3072]{1,0:T(8,128)(2,1)}), bf16[1024,3072]{1,0:T(8,128)(2,1)}) %all-gather.21.cloned.1.call-update) | async-done | bytes 6291472 | tf_op jit(solution)/shard_map/all_gather | solution.py:182
  540.0 107.1 %all-gather.23.cloned.1.call-done = bf16[1024,3072]{1,0:T(8,128)(2,1)} async-done(((bf16[256,3072]{1,0:T(8,128)(2,1)}), bf16[1024,3072]{1,0:T(8,128)(2,1)}) %all-gather.23.cloned.1.call-update) | async-done | bytes 6291472 | tf_op jit(solution)/shard_map/all_gather | solution.py:183
  655.2 107.0 %all-gather.25.cloned.1.call-done = bf16[3072,1024]{1,0:T(8,128)(2,1)} async-done(((bf16[768,1024]{1,0:T(8,128)(2,1)}), bf16[3072,1024]{1,0:T(8,128)(2,1)}) %all-gather.25.cloned.1.call-update) | async-done | bytes 6291472 | tf_op jit(solution)/shard_map/all_gather | solution.py:184
  762.3 12.0 multiply_convert_fusion
  798.6 252.0 %while.13 = (s32[]{:T(128)}, f32[512,8,2,128]{0,3,2,1:T(8,128)}, bf16[4,512,2048]{2,1,0:T(8,128)(2,1)}, bf16[4,512,2048]{2,1,0:T(8,128)(2,1)}, s32[512]{0:T(512)...) while((s32[]{:T(128)}, f32[512,8,2,128]{0,3,2,1:T(8,128)}, ...), condition=%wide.region_11.13_spmd.clone, body=%wide.region_10.12_spmd.clone.sunk | while | flops 5420351488 | bytes 157139696 | solution.py:311
  809.6 9.8 fusion.147
  836.0 10.9 bitcast_convert_fusion.2
  871.6 9.8 fusion.147
  898.0 10.9 bitcast_convert_fusion.2
  934.9 9.8 fusion.147
  961.3 10.9 bitcast_convert_fusion.2
  998.0 9.8 fusion.147
  1024.4 10.9 bitcast_convert_fusion.2
  1100.3 93.2 %reduce-scatter.9.cloned.1.call-done = bf16[512,2048]{1,0:T(8,128)(2,1)} async-done(((bf16[2048,2048]{1,0:T(8,128)(2,1)}), bf16[512,2048]{1,0:T(8,128)(2,1)}) %reduce-scatter.9.cloned.1.call-update) | async-done | bytes 2097168 | tf_op jit(solution)/shard_map/reduce_scatter | solution.py:316
  1215.2 57.9 %reduce-scatter.17.cloned.1.call-done = bf16[512,1024]{1,0:T(8,128)(2,1)} async-done(((bf16[2048,1024]{1,0:T(8,128)(2,1)}), bf16[512,1024]{1,0:T(8,128)(2,1)}) %reduce-scatter.17.cloned.1.call-update) | async-done | bytes 1048592 | tf_op jit(solution)/shard_map/reduce_scatter | solution.py:364
  1273.1 79.7 %reduce-scatter.11.cloned.1.call-done = bf16[256,2048]{1,0:T(8,128)(2,1)} async-done(((bf16[1024,2048]{1,0:T(8,128)(2,1)}), bf16[256,2048]{1,0:T(8,128)(2,1)}) %reduce-scatter.11.cloned.1.call-update) | async-done | bytes 1048592 | tf_op jit(solution)/shard_map/reduce_scatter | solution.py:349
  1352.8 113.4 %reduce-scatter.21.cloned.1.call-done = bf16[256,3072]{1,0:T(8,128)(2,1)} async-done(((bf16[1024,3072]{1,0:T(8,128)(2,1)}), bf16[256,3072]{1,0:T(8,128)(2,1)}) %reduce-scatter.21.cloned.1.call-update) | async-done | bytes 1572880 | tf_op jit(solution)/shard_map/reduce_scatter | solution.py:223
  1466.3 113.6 %reduce-scatter.19.cloned.1.call-done = bf16[256,3072]{1,0:T(8,128)(2,1)} async-done(((bf16[1024,3072]{1,0:T(8,128)(2,1)}), bf16[256,3072]{1,0:T(8,128)(2,1)}) %reduce-scatter.19.cloned.1.call-update) | async-done | bytes 1572880 | tf_op jit(solution)/shard_map/reduce_scatter | solution.py:220
  1579.9 113.5 %reduce-scatter.23.cloned.1.call-done = bf16[768,1024]{1,0:T(8,128)(2,1)} async-done(((bf16[3072,1024]{1,0:T(8,128)(2,1)}), bf16[768,1024]{1,0:T(8,128)(2,1)}) %reduce-scatter.23.cloned.1.call-update) | async-done | bytes 1572880 | tf_op jit(solution)/shard_map/reduce_scatter | solution.py:226
  1693.4 47.1 %reduce-scatter.13.cloned.1.call-done = bf16[256,1024]{1,0:T(8,128)(2,1)} async-done(((bf16[1024,1024]{1,0:T(8,128)(2,1)}), bf16[256,1024]{1,0:T(8,128)(2,1)}) %reduce-scatter.13.cloned.1.call-update) | async-done | bytes 524304 | tf_op jit(solution)/shard_map/reduce_scatter | solution.py:352
  1740.5 46.0 %reduce-scatter.15.cloned.1.call-done = bf16[256,1024]{1,0:T(8,128)(2,1)} async-done(((bf16[1024,1024]{1,0:T(8,128)(2,1)}), bf16[256,1024]{1,0:T(8,128)(2,1)}) %reduce-scatter.15.cloned.1.call-update) | async-done | bytes 524304 | tf_op jit(solution)/shard_map/reduce_scatter | solution.py:355
  1805.8 10.8 all-reduce.12
  1816.9 12.8 all-reduce.10
  1835.3 77.6 %all-reduce.16.cloned.1.call-done = (bf16[256,2048]{1,0:T(8,128)(2,1)}, bf16[256,1024]{1,0:T(8,128)(2,1)}, bf16[256,1024]{1,0:T(8,128)(2,1)}, bf16[512,1024]{1,0...) async-done(((bf16[256,2048]{1,0:T(8,128)(2,1)}, bf16[256,1024]{1,0:T(8,128)(2,1)}, bf16[256,1024]{1,0:T(8,128)(2,1)}, ...) | async-done | bytes 7864336 | tf_op jit(solution)/shard_map/psum | solution.py:370
  (391 shorter events, 392.4 us)
Async XLA Ops:
  7.2 30.6 %copy-start.20 = (bf16[512,1024]{1,0:T(8,128)(2,1)S(1)}, bf16[512,1024]{1,0:T(8,128)(2,1)}, u32[]{:S(2)}) copy-start(bf16[512,1024]{1,0:T(8,128)(2,1)} %param.19) | copy-start | bytes 3145732
  7.3 51.3 %all-gather.11.cloned.1.call-start = ((), (), s32[]{:S(2)}) async-start(), calls=%async_computation.8 | async-start | bytes 2621440 | tf_op jit(solution)/shard_map/all_gather | solution.py:130
  8.0 96.8 %all-gather.13.cloned.1.call-start = ((), (), s32[]{:S(2)}) async-start(), calls=%async_computation.9 | async-start | bytes 2621440 | tf_op jit(solution)/shard_map/all_gather | solution.py:131
  8.7 177.2 %all-gather.17.cloned.1.call-start = ((), (), s32[]{:S(2)}) async-start(), calls=%async_computation.11 | async-start | bytes 5242880 | tf_op jit(solution)/shard_map/all_gather | solution.py:129
  9.5 326.6 %all-gather.15.cloned.1.call-start = ((), (), s32[]{:S(2)}) async-start(), calls=%async_computation.10 | async-start | bytes 10485760 | tf_op jit(solution)/shard_map/all_gather | solution.py:168
  22.7 163.2 %copy-start.59 = (f32[4,1,256]{2,1,0:T(1,128)}, f32[4,1,256]{2,1,0:T(1,128)S(1)}, u32[]{:S(2)}) copy-start(f32[4,1,256]{2,1,0:T(1,128)S(1)} %convert_element_type.230) | copy-start | bytes 12292
  33.2 30.5 %copy-start.61 = (f32[128]{0:T(128)}, f32[128]{0:T(128)S(1)}, u32[]{:S(2)}) copy-start(f32[128]{0:T(128)S(1)} %convert_element_type.186) | copy-start | bytes 1540
  36.3 89.4 %copy-start.54 = (s32[1,2,8,128]{3,1,2,0:T(2,128)}, s32[1,2,8,128]{3,1,2,0:T(2,128)S(1)}, u32[]{:S(2)}) copy-start(s32[1,2,8,128]{3,1,2,0:T(2,128)S(1)} %copy.176) | copy-start | bytes 24580
  36.4 89.3 %copy-start.50 = (s32[512]{0:T(512)}, s32[512]{0:T(512)S(1)}, u32[]{:S(2)}) copy-start(s32[512]{0:T(512)S(1)} %get-tuple-element.356) | copy-start | bytes 6148
  37.5 159.8 %copy-start.16 = (f32[512,128]{0,1:T(8,128)}, f32[512,128]{0,1:T(8,128)S(1)}, u32[]{:S(2)}) copy-start(f32[512,128]{0,1:T(8,128)S(1)} %get-tuple-element.247) | copy-start | bytes 786436
  37.5 159.8 %copy-start.18 = (f32[512,128]{0,1:T(8,128)}, f32[512,128]{0,1:T(8,128)S(1)}, u32[]{:S(2)}) copy-start(f32[512,128]{0,1:T(8,128)S(1)} %get-tuple-element.248) | copy-start | bytes 786436
  37.8 70.2 %copy-start.24 = (f32[512,128]{1,0:T(8,128)}, f32[512,128]{1,0:T(8,128)S(1)}, u32[]{:S(2)}) copy-start(f32[512,128]{1,0:T(8,128)S(1)} %copy.136) | copy-start | bytes 786436
  38.1 147.8 %copy-start.63 = (f32[512]{0:T(512)}, f32[512]{0:T(512)S(1)}, u32[]{:S(2)}) copy-start(f32[512]{0:T(512)S(1)} %fusion.60) | copy-start | bytes 6148
  63.7 44.5 %copy-start.14 = (f32[512,8]{1,0:T(8,128)}, f32[512,8]{1,0:T(8,128)S(1)}, u32[]{:S(2)}) copy-start(f32[512,8]{1,0:T(8,128)S(1)} %copy.133) | copy-start | bytes 49156
  113.0 318.2 %all-gather.19.cloned.1.call-start = ((), (), s32[]{:S(2)}) async-start(), calls=%async_computation.12 | async-start | bytes 5242880 | tf_op jit(solution)/shard_map/all_gather | solution.py:134
  113.6 418.3 %all-gather.21.cloned.1.call-start = ((), (), s32[]{:S(2)}) async-start(), calls=%async_computation.13 | async-start | bytes 7864320 | tf_op jit(solution)/shard_map/all_gather | solution.py:182
  114.2 71.7 %copy-start.21 = (bf16[512,1024]{1,0:T(8,128)(2,1)S(1)}, bf16[512,1024]{1,0:T(8,128)(2,1)}, u32[]{:S(2)}) copy-start(bf16[512,1024]{1,0:T(8,128)(2,1)} %param.19) | copy-start | bytes 3145732
  114.2 532.9 %all-gather.23.cloned.1.call-start = ((), (), s32[]{:S(2)}) async-start(), calls=%async_computation.14 | async-start | bytes 7864320 | tf_op jit(solution)/shard_map/all_gather | solution.py:183
  115.0 647.3 %all-gather.25.cloned.1.call-start = ((), (), s32[]{:S(2)}) async-start(), calls=%async_computation.15 | async-start | bytes 7864320 | tf_op jit(solution)/shard_map/all_gather | solution.py:184
  115.7 1077.8 %reduce-scatter.9.cloned.1.call-start = ((), (), s32[]{:S(2)}) async-start(), calls=%async_computation.16 | async-start | bytes 10485760 | tf_op jit(solution)/shard_map/reduce_scatter | solution.py:316
  116.3 81.0 %copy-start.65 = (f32[128]{0:T(128)}, f32[128]{0:T(128)S(1)}, u32[]{:S(2)}) copy-start(f32[128]{0:T(128)S(1)} %convert_element_type.190) | copy-start | bytes 1540
  436.5 350.6 %copy-start.7 = (f32[512,1024]{1,0:T(8,128)}, f32[512,1024]{1,0:T(8,128)S(1)}, u32[]{:S(2)}) copy-start(f32[512,1024]{1,0:T(8,128)S(1)} %get-tuple-element.262) | copy-start | bytes 6291460
  436.8 210.3 %copy-start.34 = (bf16[512,1024]{1,0:T(8,128)(2,1)}, bf16[512,1024]{1,0:T(8,128)(2,1)S(1)}, u32[]{:S(2)}) copy-start(bf16[512,1024]{1,0:T(8,128)(2,1)S(1)} %multiply_convert_fusion.2) | copy-start | bytes 3145732
  1050.6 222.5 %reduce-scatter.17.cloned.1.call-start = ((), (), s32[]{:S(2)}) async-start(), calls=%async_computation.20 | async-start | bytes 5242880 | tf_op jit(solution)/shard_map/reduce_scatter | solution.py:364
  1058.1 294.7 %reduce-scatter.11.cloned.1.call-start = ((), (), s32[]{:S(2)}) async-start(), calls=%async_computation.17 | async-start | bytes 5242880 | tf_op jit(solution)/shard_map/reduce_scatter | solution.py:349
  1075.8 390.5 %reduce-scatter.21.cloned.1.call-start = ((), (), s32[]{:S(2)}) async-start(), calls=%async_computation.22 | async-start | bytes 7864320 | tf_op jit(solution)/shard_map/reduce_scatter | solution.py:223
  1084.3 495.6 %reduce-scatter.19.cloned.1.call-start = ((), (), s32[]{:S(2)}) async-start(), calls=%async_computation.21 | async-start | bytes 7864320 | tf_op jit(solution)/shard_map/reduce_scatter | solution.py:220
  1091.7 601.7 %reduce-scatter.23.cloned.1.call-start = ((), (), s32[]{:S(2)}) async-start(), calls=%async_computation.23 | async-start | bytes 7864320 | tf_op jit(solution)/shard_map/reduce_scatter | solution.py:226
  1100.2 640.2 %reduce-scatter.13.cloned.1.call-start = ((), (), s32[]{:S(2)}) async-start(), calls=%async_computation.18 | async-start | bytes 2621440 | tf_op jit(solution)/shard_map/reduce_scatter | solution.py:352
  1210.6 576.0 %reduce-scatter.15.cloned.1.call-start = ((), (), s32[]{:S(2)}) async-start(), calls=%async_computation.19 | async-start | bytes 2621440 | tf_op jit(solution)/shard_map/reduce_scatter | solution.py:355
  1214.9 698.0 %all-reduce.16.cloned.1.call-start = ((), (), s32[]{:S(2)}) async-start(), calls=%async_computation.24 | async-start | bytes 15728640 | tf_op jit(solution)/shard_map/psum | solution.py:370
  1801.6 30.3 %copy-start.13 = (f32[512,1024]{1,0:T(8,128)S(1)}, f32[512,1024]{1,0:T(8,128)}, u32[]{:S(2)}) copy-start(f32[512,1024]{1,0:T(8,128)} %copy-done.11) | copy-start | bytes 6291460
  (70 other events, 397.5 us)
Sparse Core Ops, SparseCore 0:
  9.7 48.8 all-gather.10
  60.2 44.5 all-gather.12
  106.4 79.5 all-gather.16
  187.9 148.1 all-gather.14
  337.5 78.9 all-gather.18
  418.0 113.8 all-gather.20
  533.5 113.5 all-gather.22
  648.6 113.5 all-gather.24
  1050.7 142.6 reduce-scatter.8
  1195.6 77.4 reduce-scatter.16
  1275.5 77.2 reduce-scatter.10
  1355.0 111.2 reduce-scatter.20
  1468.6 111.2 reduce-scatter.18
  1582.0 111.2 reduce-scatter.22
  1696.1 44.3 reduce-scatter.12
  1743.3 43.1 reduce-scatter.14
  1790.5 122.3 all-reduce.15
where the time goes:
time: 1940 us; the launch traced here: 1930 us
  waiting for transfers between devices  1310 us (68%)
  matrix products  352 us (18%)
  local copies, waits for them, and re-layouts  103 us (5%)
  other arithmetic  88 us (5%)
  blocking collectives  54.2 us (3%)
    all_gather x1, waiting for transfers between devices, body(): lax.all_gather(key_values, 'shard', axis=0, tiled=True)  134 us
    reduce_scatter x1, waiting for transfers between devices, body(): lax.psum_scatter(grad_wgate.astype(jnp.bfloat16), 'shard', scatter_dimens...  114 us
    reduce_scatter x1, waiting for transfers between devices, body(): lax.psum_scatter(grad_down.astype(jnp.bfloat16), 'shard', scatter_dimensi...  113 us
    reduce_scatter x1, waiting for transfers between devices, body(): lax.psum_scatter(grad_wup.astype(jnp.bfloat16), 'shard', scatter_dimensio...  113 us
    all_gather x1, waiting for transfers between devices, body(): lax.all_gather(w_up, 'shard', axis=0, tiled=True)  107 us
    all_gather x1, waiting for transfers between devices, body(): lax.all_gather(w_down, 'shard', axis=0, tiled=True)  107 us
    all_gather x1, waiting for transfers between devices, body(): lax.all_gather(w_gate, 'shard', axis=0, tiled=True)  95.1 us
    reduce_scatter x1, waiting for transfers between devices, body(): lax.psum_scatter(kv_terms.reshape(shards * TOK_DEV, 2 * width).astype(com...  93.2 us
  transfers between devices with their start and end apart: 17, of which 16 were waited for; matrix products, arithmetic and copies ran while one was open for 12% of the time, Pallas kernels for 0%

commit v1 on v0

v1 whole, which is shorter than its diff:
```python
import functools
import math

import jax
import jax.numpy as jnp
from jax import lax
from jax.experimental import pallas as pl
from jax.experimental.pallas import tpu as pltpu
from jax.sharding import PartitionSpec as P

HEADS = 16
KV_HEADS = 8
HEAD_WIDTH = 128
EPS = 1e-06
THETA = 1000000.0
F32 = jnp.float32
BF16 = jnp.bfloat16
SCALE = HEAD_WIDTH ** (-0.5)
EXP2_SCALE = SCALE * math.log2(math.e)
VMEM_LIMIT = 40 * 1024 * 1024


def dp_swap(x, bit):
    count = lax.axis_size("dp")
    return lax.ppermute(x, "dp", [(i, i ^ (1 << bit)) for i in range(count)])


def z_shift(x, step):
    count = lax.axis_size("shard")
    return lax.ppermute(x, "shard", [(i, (i + step) % count) for i in range(count)])


def bit_of(index, bit):
    return (index >> bit) & 1


def plane_order(flip):
    bits = list(range(1, lax.axis_size("dp").bit_length() - 1))
    return bits[::-1] if flip else bits


def column_piece(index, order):
    piece = bit_of(index, 0)
    for bit in order:
        piece = piece * 2 + bit_of(index, bit)
    return piece


def spread(arrays, bits):
    masks = [0]
    for bit in bits:
        arrays = arrays + [dp_swap(a, bit) for a in arrays]
        masks = masks + [m ^ (1 << bit) for m in masks]
    return arrays, masks


def place_kernel(shards, at_ref, own_ref, *refs):
    count = len(refs) - 2
    out_ref, sems = refs[-2], refs[-1]
    rows = own_ref.shape[0]
    cols = refs[0].shape[2]
    copies = [
        pltpu.make_async_copy(
            own_ref, out_ref.at[pl.ds(pl.multiple_of(at_ref[0] * rows, rows), rows), :], sems.at[0]
        )
    ]
    for i in range(count):
        column = pl.multiple_of(at_ref[shards + i] * cols, cols)
        for t in range(1, shards):
            row = pl.multiple_of(at_ref[t] * rows, rows)
            copies.append(
                pltpu.make_async_copy(
                    refs[i].at[t - 1],
                    out_ref.at[pl.ds(row, rows), pl.ds(column, cols)],
                    sems.at[1 + i * (shards - 1) + t - 1],
                )
            )
    for copy in copies:
        copy.start()
    for copy in copies:
        copy.wait()


def gather_weight(own, flip):
    shards = lax.axis_size("shard")
    z = lax.axis_index("shard")
    d = lax.axis_index("dp")
    order = plane_order(flip)
    rows, width = own.shape
    cols = width // lax.axis_size("dp")
    moving = lax.dynamic_slice_in_dim(own, column_piece(d, order) * cols, cols, axis=1)
    chunks = []
    for _ in range(shards - 1):
        moving = z_shift(moving, 1)
        chunks.append(moving)
    arrays, masks = spread([jnp.stack(chunks)], order + [0])
    row_at = [(z - t) % shards for t in range(shards)]
    col_at = [column_piece(d ^ m, order) for m in masks]
    if cols % 128 == 0 and rows % 16 == 0:
        at = jnp.stack(row_at + col_at).astype(jnp.int32)
        return pl.pallas_call(
            functools.partial(place_kernel, shards),
            out_shape=jax.ShapeDtypeStruct((shards * rows, width), own.dtype),
            grid_spec=pltpu.PrefetchScalarGridSpec(
                num_scalar_prefetch=1,
                grid=(1,),
                in_specs=[pl.BlockSpec(memory_space=pl.ANY)] * (1 + len(arrays)),
                out_specs=pl.BlockSpec((shards * rows, width), lambda i, at: (0, 0)),
                scratch_shapes=[pltpu.SemaphoreType.DMA((1 + len(arrays) * (shards - 1),))],
            ),
            compiler_params=pltpu.CompilerParams(vmem_limit_bytes=VMEM_LIMIT),
            name="place",
        )(at, own, *arrays)
    full = jnp.zeros((shards * rows, width), own.dtype)
    full = lax.dynamic_update_slice(full, own, (row_at[0] * rows, 0))
    for array, column in zip(arrays, col_at):
        for t in range(1, shards):
            full = lax.dynamic_update_slice(full, array[t - 1], (row_at[t] * rows, column * cols))
    return full


def widen_kernel(at_ref, *refs):
    out_ref = refs[-1]
    step = pl.program_id(0)
    for i in range(len(refs) - 1):

        @pl.when(step == i)
        def _():
            out_ref[...] = refs[i][...].astype(F32)


def reduce_weight(left, right, flip):
    shards = lax.axis_size("shard")
    z = lax.axis_index("shard")
    d = lax.axis_index("dp")
    order = plane_order(flip)
    width = right.shape[1]
    half = width // 2
    core = bit_of(d, 0)

    def product(columns):
        return lax.dot_general(left, columns, (((0,), (0,)), ((), ())), preferred_element_type=F32)

    theirs = product(lax.dynamic_slice_in_dim(right, (1 - core) * half, half, axis=1)).astype(BF16)
    arrived = dp_swap(theirs, 0)
    mine = product(lax.dynamic_slice_in_dim(right, core * half, half, axis=1))
    total = (mine + arrived.astype(F32)).astype(BF16)
    for bit in order:
        half = half // 2
        here = bit_of(d, bit)
        sent = lax.dynamic_slice_in_dim(total, (1 - here) * half, half, axis=1)
        kept = lax.dynamic_slice_in_dim(total, here * half, half, axis=1)
        total = (kept.astype(F32) + dp_swap(sent, bit).astype(F32)).astype(BF16)
    rows = total.shape[0] // shards

    def chunk(owner):
        return lax.dynamic_slice_in_dim(total, (owner % shards) * rows, rows, axis=0)

    moving = chunk(z - 1 + shards)
    for t in range(1, shards):
        moving = z_shift(moving, 1)
        moving = (moving.astype(F32) + chunk(z - 1 - t + shards).astype(F32)).astype(BF16)
    arrays, masks = spread([moving], order[::-1] + [0])
    col_at = [column_piece(d ^ m, order) for m in masks]
    cols = moving.shape[1]
    if cols % 128 == 0:
        return pl.pallas_call(
            widen_kernel,
            out_shape=jax.ShapeDtypeStruct((rows, width), F32),
            grid_spec=pltpu.PrefetchScalarGridSpec(
                num_scalar_prefetch=1,
                grid=(len(arrays),),
                in_specs=[pl.BlockSpec((rows, cols), lambda i, at: (0, 0))] * len(arrays),
                out_specs=pl.BlockSpec((rows, cols), lambda i, at: (0, at[i])),
            ),
            name="widen",
        )(jnp.stack(col_at).astype(jnp.int32), *arrays)
    full = jnp.zeros((rows, width), F32)
    for array, column in zip(arrays, col_at):
        full = lax.dynamic_update_slice(full, array.astype(F32), (0, column * cols))
    return full


def dot_nt(a, b):
    return lax.dot_general(a, b, (((1,), (1,)), ((), ())), preferred_element_type=F32)


def dot_tn(a, b):
    return lax.dot_general(a, b, (((0,), (0,)), ((), ())), preferred_element_type=F32)


def dot_nn(a, b):
    return lax.dot_general(a, b, (((1,), (0,)), ((), ())), preferred_element_type=F32)


def inverse_rms(v):
    return lax.rsqrt(jnp.mean(v * v, axis=-1, keepdims=True) + EPS)


def turn(u):
    return pltpu.roll(u, HEAD_WIDTH // 2, 1)


def norm_rope(v, gain, cosine, sine):
    u = v * inverse_rms(v) * gain
    return u * cosine + turn(u) * sine


def norm_rope_back(grad, v, gain, cosine, sine):
    r = inverse_rms(v)
    du = grad * cosine + turn(grad * sine)
    scaled = gain * du
    dv = r * scaled - v * (r * r * r) * jnp.mean(scaled * v, axis=-1, keepdims=True)
    return dv, du * v * r


def masked_exp(q, k, key_place, q_place, q_start):
    scores = dot_nt(q, k)
    allowed = (key_place <= q_place) & (key_place >= q_start)
    return jnp.where(allowed, jnp.exp2(scores * EXP2_SCALE), 0.0)


def load_queries(q_ref, gain_ref, cos_ref, sin_ref, held_ref, block):
    gain = gain_ref[...]
    for slot in range(2):
        rows = slice(slot * block, (slot + 1) * block)
        for head in range(2):
            v = q_ref[rows, head * HEAD_WIDTH : (head + 1) * HEAD_WIDTH]
            rotated = norm_rope(v, gain, cos_ref[rows, :], sin_ref[rows, :])
            held_ref[slot, head * block : (head + 1) * block, :] = rotated.astype(BF16)


def attend_kernel(
    sel_ref, q_ref, k_ref, v_ref, cos_ref, sin_ref, qg_ref, kg_ref, kp_ref, qp_ref, qs_ref,
    out_ref, held, acc, total,
):
    block = q_ref.shape[0] // 2
    pairs = k_ref.shape[0] // block
    load_queries(q_ref, qg_ref, cos_ref, sin_ref, held, block)
    for p in range(pairs):
        rows = slice(p * block, (p + 1) * block)
        slot = p if p < 2 else sel_ref[p - 2]
        k = norm_rope(k_ref[rows, :], kg_ref[...], cos_ref[rows, :], sin_ref[rows, :]).astype(BF16)
        e = masked_exp(held[slot], k, kp_ref[:, rows], qp_ref[slot], qs_ref[slot])
        added = dot_nn(e.astype(BF16), v_ref[rows, :])
        summed = jnp.sum(e, axis=-1, keepdims=True)
        if p < 2:
            acc[slot] = added
            total[slot] = summed
        else:
            acc[slot] += added
            total[slot] += summed
    for slot in range(2):
        value = (acc[slot] / total[slot]).astype(out_ref.dtype)
        for head in range(2):
            out_ref[
                slot * block : (slot + 1) * block, head * HEAD_WIDTH : (head + 1) * HEAD_WIDTH
            ] = value[head * block : (head + 1) * block, :]


def attend_back_kernel(
    sel_ref, q_ref, k_ref, v_ref, cos_ref, sin_ref, qg_ref, kg_ref, kp_ref, qp_ref, qs_ref,
    att_ref, gatt_ref, dq_ref, dk_ref, dv_ref, dqg_ref, dkg_ref,
    held, keys, grads, dots, total, raised, dq_acc,
):
    block = q_ref.shape[0] // 2
    pairs = k_ref.shape[0] // block
    load_queries(q_ref, qg_ref, cos_ref, sin_ref, held, block)
    for slot in range(2):
        rows = slice(slot * block, (slot + 1) * block)
        for head in range(2):
            columns = slice(head * HEAD_WIDTH, (head + 1) * HEAD_WIDTH)
            there = slice(head * block, (head + 1) * block)
            g = gatt_ref[rows, columns]
            grads[slot, there, :] = g
            dots[slot, there, :] = jnp.sum(
                g.astype(F32) * att_ref[rows, columns].astype(F32), axis=-1, keepdims=True
            )
    for p in range(pairs):
        rows = slice(p * block, (p + 1) * block)
        slot = p if p < 2 else sel_ref[p - 2]
        k = norm_rope(k_ref[rows, :], kg_ref[...], cos_ref[rows, :], sin_ref[rows, :]).astype(BF16)
        keys[rows, :] = k
        e = masked_exp(held[slot], k, kp_ref[:, rows], qp_ref[slot], qs_ref[slot])
        raised[p] = e
        summed = jnp.sum(e, axis=-1, keepdims=True)
        if p < 2:
            total[slot] = summed
        else:
            total[slot] += summed
    total[...] = 1.0 / total[...]

    @pl.when(pl.program_id(0) == 0)
    def _():
        dqg_ref[...] = jnp.zeros_like(dqg_ref)
        dkg_ref[...] = jnp.zeros_like(dkg_ref)

    for p in range(pairs):
        rows = slice(p * block, (p + 1) * block)
        slot = p if p < 2 else sel_ref[p - 2]
        g = grads[slot]
        shares = raised[p] * total[slot]
        dshares = dot_nt(g, v_ref[rows, :])
        dscores = (shares * (dshares - dots[slot])).astype(BF16)
        dv_ref[rows, :] = dot_tn(shares.astype(BF16), g).astype(dv_ref.dtype)
        added = dot_nn(dscores, keys[rows, :])
        if p < 2:
            dq_acc[slot] = added
        else:
            dq_acc[slot] += added
        dk = dot_tn(dscores, held[slot]) * SCALE
        dv, dgain = norm_rope_back(
            dk, k_ref[rows, :], kg_ref[...], cos_ref[rows, :], sin_ref[rows, :]
        )
        dk_ref[rows, :] = dv.astype(dk_ref.dtype)
        dkg_ref[...] += jnp.sum(dgain, axis=0, keepdims=True)
    for slot in range(2):
        rows = slice(slot * block, (slot + 1) * block)
        for head in range(2):
            columns = slice(head * HEAD_WIDTH, (head + 1) * HEAD_WIDTH)
            dv, dgain = norm_rope_back(
                dq_acc[slot, head * block : (head + 1) * block, :] * SCALE,
                q_ref[rows, columns],
                qg_ref[...],
                cos_ref[rows, :],
                sin_ref[rows, :],
            )
            dq_ref[rows, columns] = dv.astype(dq_ref.dtype)
            dqg_ref[...] += jnp.sum(dgain, axis=0, keepdims=True)


def attention_specs(count, total):
    pair = HEADS // KV_HEADS * HEAD_WIDTH
    fixed2 = lambda h, sel: (0, 0)
    fixed3 = lambda h, sel: (0, 0, 0)
    by_head = lambda h, sel: (0, h)
    q_spec = pl.BlockSpec((count, pair), by_head)
    k_spec = pl.BlockSpec((total, HEAD_WIDTH), by_head)
    inputs = [
        q_spec,
        k_spec,
        k_spec,
        pl.BlockSpec((total, HEAD_WIDTH), fixed2),
        pl.BlockSpec((total, HEAD_WIDTH), fixed2),
        pl.BlockSpec((1, HEAD_WIDTH), fixed2),
        pl.BlockSpec((1, HEAD_WIDTH), fixed2),
        pl.BlockSpec((1, total), fixed2),
        pl.BlockSpec((2, count, 1), fixed3),
        pl.BlockSpec((2, count, 1), fixed3),
    ]
    return q_spec, k_spec, pl.BlockSpec((1, HEAD_WIDTH), fixed2), inputs


def attend(sel, count, total, operands):
    q_spec, _, _, inputs = attention_specs(count, total)
    return pl.pallas_call(
        attend_kernel,
        out_shape=jax.ShapeDtypeStruct((count, HEADS * HEAD_WIDTH), BF16),
        grid_spec=pltpu.PrefetchScalarGridSpec(
            num_scalar_prefetch=1,
            grid=(KV_HEADS,),
            in_specs=inputs,
            out_specs=q_spec,
            scratch_shapes=[
                pltpu.VMEM((2, count, HEAD_WIDTH), BF16),
                pltpu.VMEM((2, count, HEAD_WIDTH), F32),
                pltpu.VMEM((2, count, 1), F32),
            ],
        ),
        compiler_params=pltpu.CompilerParams(vmem_limit_bytes=VMEM_LIMIT),
        name="attend",
    )(sel, *operands)


def attend_back(sel, count, total, operands):
    q_spec, k_spec, gain_spec, inputs = attention_specs(count, total)
    block = count // 2
    width = KV_HEADS * HEAD_WIDTH
    return pl.pallas_call(
        attend_back_kernel,
        out_shape=(
            jax.ShapeDtypeStruct((count, HEADS * HEAD_WIDTH), BF16),
            jax.ShapeDtypeStruct((total, width), BF16),
            jax.ShapeDtypeStruct((total, width), BF16),
            jax.ShapeDtypeStruct((1, HEAD_WIDTH), F32),
            jax.ShapeDtypeStruct((1, HEAD_WIDTH), F32),
        ),
        grid_spec=pltpu.PrefetchScalarGridSpec(
            num_scalar_prefetch=1,
            grid=(KV_HEADS,),
            in_specs=inputs + [q_spec, q_spec],
            out_specs=[q_spec, k_spec, k_spec, gain_spec, gain_spec],
            scratch_shapes=[
                pltpu.VMEM((2, count, HEAD_WIDTH), BF16),
                pltpu.VMEM((total, HEAD_WIDTH), BF16),
                pltpu.VMEM((2, count, HEAD_WIDTH), BF16),
                pltpu.VMEM((2, count, 1), F32),
                pltpu.VMEM((2, count, 1), F32),
                pltpu.VMEM((total // block, count, block), F32),
                pltpu.VMEM((2, count, HEAD_WIDTH), F32),
            ],
        ),
        compiler_params=pltpu.CompilerParams(vmem_limit_bytes=VMEM_LIMIT),
        name="attend_back",
    )(sel, *operands)


def rms_back(grad, v, gain):
    r = inverse_rms(v)
    scaled = grad * gain
    dv = r * scaled - v * (r * r * r) * jnp.mean(scaled * v, axis=-1, keepdims=True)
    return dv, jnp.sum(grad * v * r, axis=0)


def matmul(a, b):
    return jnp.dot(a, b, preferred_element_type=F32)


def body(
    tokens,
    attn_gain,
    w_query,
    w_key,
    w_value,
    q_gain,
    k_gain,
    w_out,
    mlp_gain,
    w_gate,
    w_up,
    w_down,
    segments,
    spans,
    out_grad,
):
    shards = lax.axis_size("shard")
    z = lax.axis_index("shard")
    count = tokens.shape[0]
    block = count // 2
    total = block * (shards + 1)
    span_row = spans[0]
    segment_row = segments[0]

    def span_of(index):
        return lax.dynamic_index_in_dim(span_row, index % shards, keepdims=False)

    span = span_of(z)
    slots = []
    remote = []
    sel = []
    numbers = [span, 2 * shards - 1 - span]
    for k in range(1, shards):
        slot = jnp.where(span < span_of(z + k), 0, 1)
        slots.append(slot)
        remote.append(z_shift(lax.dynamic_slice_in_dim(tokens, slot * block, block, axis=0), k))
        other = span_of(z - k + shards)
        sel.append(jnp.where(other < span, 0, 1))
        numbers.append(jnp.where(other < span, other, 2 * shards - 1 - other))
    sel = jnp.stack(sel).astype(jnp.int32)

    sizes = [attn_gain.shape[0], mlp_gain.shape[0], q_gain.shape[0], k_gain.shape[0]]
    own_gains = jnp.concatenate([attn_gain, mlp_gain, q_gain, k_gain])
    gains = jnp.stack([own_gains] + [z_shift(own_gains, k) for k in range(1, shards)])
    order = (z - jnp.arange(shards)) % shards
    pick = order[:, None] == jnp.arange(shards)[None, :]
    gains = jnp.sum(jnp.where(pick[:, :, None], gains.astype(F32)[None], 0.0), axis=1)
    parts = []
    start = 0
    for size in sizes:
        parts.append(gains[:, start : start + size].reshape(1, shards * size))
        start += size
    attn_g, mlp_g, q_g, k_g = parts

    full_query = gather_weight(w_query, False)
    full_key = gather_weight(w_key, True)
    full_value = gather_weight(w_value, True)
    full_out = gather_weight(w_out, True)
    full_gate = gather_weight(w_gate, False)
    full_up = gather_weight(w_up, True)
    full_down = gather_weight(w_down, False)

    place = jnp.concatenate([n * block + jnp.arange(block, dtype=jnp.int32) for n in numbers])
    seg = jnp.concatenate([lax.dynamic_slice_in_dim(segment_row, n * block, block) for n in numbers])
    doc_start = jnp.sum((segment_row[None, :] < seg[:, None]).astype(jnp.int32), axis=1)
    steps = jnp.arange(HEAD_WIDTH // 2, dtype=F32) * (2.0 / HEAD_WIDTH)
    inverse = jnp.power(F32(THETA), -steps)
    angles = (place - doc_start).astype(F32)[:, None] * inverse[None, :]
    cosine, sine = jnp.cos(angles), jnp.sin(angles)
    cosine = jnp.concatenate([cosine, cosine], axis=1)
    sine = jnp.concatenate([-sine, sine], axis=1)

    def by_slot(v):
        v = v[:count].reshape(2, 1, block, 1)
        return jnp.concatenate([v, v], axis=1).reshape(2, count, 1)

    rows = jnp.concatenate([tokens] + remote, axis=0).astype(F32)
    normed = (rows * inverse_rms(rows) * attn_g).astype(BF16)
    queries = matmul(normed[:count], full_query)
    keys_pre = matmul(normed, full_key)
    values = matmul(normed, full_value).astype(BF16)
    operands = (
        queries, keys_pre, values, cosine, sine, q_g, k_g,
        place[None, :], by_slot(place), by_slot(doc_start),
    )
    attended = attend(sel, count, total, operands)
    residual = tokens.astype(F32) + matmul(attended, full_out)
    mixed = (residual * inverse_rms(residual) * mlp_g).astype(BF16)
    gate = matmul(mixed, full_gate)
    upward = matmul(mixed, full_up)
    sig = jax.nn.sigmoid(gate)
    hidden = (gate * sig * upward).astype(BF16)
    result = (residual + matmul(hidden, full_down)).astype(BF16)

    grad_w_down = reduce_weight(hidden, out_grad, False)
    grad_hidden = dot_nt(out_grad, full_down)
    grad_gate = (grad_hidden * upward * sig * (1.0 + gate * (1.0 - sig))).astype(BF16)
    grad_upward = (grad_hidden * gate * sig).astype(BF16)
    grad_w_gate = reduce_weight(mixed, grad_gate, False)
    grad_w_up = reduce_weight(mixed, grad_upward, True)
    grad_mixed = dot_nt(grad_gate, full_gate) + dot_nt(grad_upward, full_up)
    grad_residual, grad_mlp_gain = rms_back(grad_mixed, residual, mlp_g)
    grad_residual = grad_residual + out_grad.astype(F32)
    grad_branch = grad_residual.astype(BF16)
    grad_attended = dot_nt(grad_branch, full_out).astype(BF16)
    grad_w_out = reduce_weight(attended, grad_branch, True)

    dq, dk, dv, grad_q_gain, grad_k_gain = attend_back(
        sel, count, total, operands + (attended, grad_attended)
    )
    grad_normed_kv = dot_nt(dk, full_key) + dot_nt(dv, full_value)
    grad_normed_own = grad_normed_kv[:count] + dot_nt(dq, full_query)
    back = []
    for k in range(1, shards):
        term = grad_normed_kv[count + (k - 1) * block : count + k * block].astype(BF16)
        back.append(z_shift(term, shards - k).astype(F32))
    grad_w_query = reduce_weight(normed[:count], dq, False)
    grad_w_key = reduce_weight(normed, dk, True)
    grad_w_value = reduce_weight(normed, dv, True)

    partial = jnp.concatenate([grad_normed_own, grad_normed_kv[count:]], axis=0)
    grad_attn_gain = jnp.sum(partial * rows * inverse_rms(rows), axis=0)
    for slot, term in zip(slots, back):
        first = jnp.where(slot == 0, term, 0.0)
        grad_normed_own = grad_normed_own + jnp.concatenate([first, term - first], axis=0)
    grad_tokens = grad_residual + rms_back(grad_normed_own, tokens.astype(F32), attn_g)[0]

    packed = jnp.concatenate(
        [grad_attn_gain, grad_mlp_gain, grad_q_gain[0], grad_k_gain[0]]
    ).reshape(-1, HEAD_WIDTH)
    for bit in range(lax.axis_size("dp").bit_length() - 1):
        packed = packed + dp_swap(packed, bit)
    packed = sum([z_shift(packed, k) for k in range(1, shards)], packed).reshape(-1)
    gain_grads = []
    start = 0
    for size in sizes:
        gain_grads.append(lax.dynamic_slice_in_dim(packed, start + z * size, size))
        start += size * shards

    return (
        result,
        grad_tokens,
        gain_grads[0],
        grad_w_query,
        grad_w_key,
        grad_w_value,
        gain_grads[2],
        gain_grads[3],
        grad_w_out,
        gain_grads[1],
        grad_w_gate,
        grad_w_up,
        grad_w_down,
    )


def solution(mesh):
    rows = P("shard", None)
    both = P(("dp", "shard"), None)
    placed = (
        both, P("shard"), rows, rows, rows, P("shard"), P("shard"), rows, P("shard"), rows, rows, rows,
        P("dp", None), P("dp", None), both,
    )
    return jax.shard_map(
        body,
        mesh=mesh,
        in_specs=placed,
        out_specs=(
            both, both, P("shard"), rows, rows, rows, P("shard"), P("shard"), rows, P("shard"),
            rows, rows, rows,
        ),
        check_vma=False,
    )
```

time: 1940 us -> 848 us (0.44)
  waiting for transfers between devices: 1310 us -> 359 us
  matrix products: 352 us -> 114 us
  Pallas kernels: 0 us -> 145 us
  starting transfers between devices: 1.32 us -> 135 us
  local copies, waits for them, and re-layouts: 103 us -> 30.4 us
  blocking collectives: 54.2 us -> 0 us
  other arithmetic: 88 us -> 39.6 us
    reduce_scatter x8 -> x0, waiting for transfers between devices: 665 us -> none  [the longest x1 114 us: body(): lax.psum_scatter(grad_wgate.astype(jnp.bfloat16), 'shard', scatter_dimens...]
    all_gather x8 -> x0, waiting for transfers between devices: 562 us -> none  [the longest x1 134 us: body(): lax.all_gather(key_values, 'shard', axis=0, tiled=True)]
    ppermute x0 -> x176, waiting for transfers between devices: none -> 359 us  [the longest x54 212 us: z_shift(): lax.ppermute(x, 'shard', [(i, (i + step) % count) for i in range(count)])]
    dot_general x42 -> x28, matrix products: 345 us -> 114 us  [the longest x14 42 us: product(): lax.dot_general(left, columns, (((0,), (0,)), ((), ())), preferred_elemen...]
    pallas_call x0 -> x16, Pallas kernels: none -> 145 us  [the longest x1 65.4 us: attend_back(): pl.pallas_call(attend_back_kernel, out_shape=(jax.ShapeDtypeStruct((count...]
    ppermute x0 -> x176, starting transfers between devices: none -> 135 us  [the longest x122 68.3 us: dp_swap(): return lax.ppermute(x, 'dp', [(i, i ^ 1 << bit) for i in range(count)])]
    psum x1 -> x0, waiting for transfers between devices: 77.6 us -> none  [body(): lax.psum(attn_own[1].astype(jnp.bfloat16), 'dp').astype(jnp.float32)]
    reduce_sum x6 -> x4, other arithmetic: 31.9 us -> 6.53 us  [the longest x1 2.55 us: body(): grad_attn_gain = jnp.sum(partial * rows * inverse_rms(rows), axis=0)]
  transfers between devices with their start and end apart: 17 -> 176, of which waited for: 16 -> 55; matrix products, arithmetic and copies ran while one was open for 12% -> 14% of each run, Pallas kernels for 0% -> 9%
where the time goes in v1:
time: 848 us; the launch traced here: 840 us
  waiting for transfers between devices  359 us (42%)
  Pallas kernels  145 us (17%)
  starting transfers between devices  135 us (16%)
  matrix products  114 us (13%)
  other arithmetic  39.6 us (5%)
  local copies, waits for them, and re-layouts  30.4 us (4%)
  between operations  17.1 us (2%)
    ppermute x54, waiting for transfers between devices, z_shift(): lax.ppermute(x, 'shard', [(i, (i + step) % count) for i in range(count)])  212 us
    ppermute x122, waiting for transfers between devices, dp_swap(): return lax.ppermute(x, 'dp', [(i, i ^ 1 << bit) for i in range(count)])  147 us
    ppermute x122, starting transfers between devices, dp_swap(): return lax.ppermute(x, 'dp', [(i, i ^ 1 << bit) for i in range(count)])  68.3 us
    ppermute x54, starting transfers between devices, z_shift(): lax.ppermute(x, 'shard', [(i, (i + step) % count) for i in range(count)])  66.9 us
    pallas_call x1, Pallas kernels, attend_back(): pl.pallas_call(attend_back_kernel, out_shape=(jax.ShapeDtypeStruct((count...  65.4 us
    dot_general x14, matrix products, product(): lax.dot_general(left, columns, (((0,), (0,)), ((), ())), preferred_elemen...  42 us
    dot_general x7, matrix products, matmul(): return jnp.dot(a, b, preferred_element_type=F32)  38 us
    pallas_call x7, Pallas kernels, reduce_weight(): pl.pallas_call(widen_kernel, out_shape=jax.ShapeDtypeStruct((rows, width)...  35.5 us
  transfers between devices with their start and end apart: 176, of which 55 were waited for; matrix products, arithmetic and copies ran while one was open for 14% of the time, Pallas kernels for 9%

profile of v1, /device:TPU:0, one launch (start us, length us, event | category | flops | bytes accessed | tf_op | source)
XLA Modules:
  0.0 840.3 jit_solution(5166125794114801)
XLA Ops:
  64.9 10.9 %collective-permute-done.28 = bf16[256,128]{1,0:T(8,128)(2,1)S(1)} collective-permute-done((bf16[256,128]{1,0:T(8,128)(2,1)S(1)}, bf16[256,128]{1,0:T(8,128)(2,1)S(1)}, u32[]{:S(2)}, u32[]{:S(2)}) %collective-permute-start.28) | collective-permute-done | bytes 65568 | tf_op jit(solution)/shard_map/ppermute | solution.py:30
  96.2 36.1 %collective-permute-done.38 = bf16[512,128]{1,0:T(8,128)(2,1)S(1)} collective-permute-done((bf16[512,128]{1,0:T(8,128)(2,1)S(1)}, bf16[512,128]{1,0:T(8,128)(2,1)S(1)}, u32[]{:S(2)}, u32[]{:S(2)}) %collective-permute-start.38) | collective-permute-done | bytes 131104 | tf_op jit(solution)/shard_map/ppermute | solution.py:30
  132.3 10.3 %collective-permute-start.47 = (bf16[256,384]{1,0:T(8,128)(2,1)}, bf16[256,384]{1,0:T(8,128)(2,1)}, u32[]{:S(2)}, u32[]{:S(2)}) collective-permute-start(bf16[256,384]{1,0:T(8,128)(2,1)} %copy-done.95), channel_id=1, source_target_pairs={{0,1},{1,2},{2,3},{3,0},{4,5},{5,6},{6,7},{7,4},{8,9},{9,10},{10,1... | collective-permute-start | bytes 589832 | tf_op jit(solution)/shard_map/ppermute | solution.py:30
  161.1 8.2 collective-permute-done.31.refs_3_
  218.1 7.0 collective-permute-done.69.refs_1_
  229.6 30.2 %attend.1.att_ref = bf16[512,2048]{1,0:T(8,128)(2,1)S(1)} custom-call(s32[3]{0:T(128)S(1)} %pad_add_fusion.1.sel_ref, f32[512,2048]{1,0:T(8,128)S(1)} %fusion.45.q_ref, f32[1280,1024]{1,0:T(8,128)} %fusion.81.k_ref, bf16[1280,1024]{1,0:T(8,128)(2,1)S(1)} %convolution_convert_fusion.3.v_ref, f32[1280,128]{1,0:T(8,128)S(1)} %get-tuple-element.77.cos_ref, ...), custom_call_target="tpu_custom_call" | custom-call | tf_op jit(solution)/shard_map/attend/pallas_call | solution.py:356
  278.7 12.1 %collective-permute-done.59.refs_1_ = bf16[3,256,384]{2,1,0:T(8,128)(2,1)S(1)} collective-permute-done((bf16[3,256,384]{2,1,0:T(8,128)(2,1)}, bf16[3,256,384]{2,1,0:T(8,128)(2,1)S(1)}, u32[]{:S(2)}, u32[]{:S(2)}) %collective-permute-start.59) | collective-permute-done | bytes 589856 | tf_op jit(solution)/shard_map/ppermute | solution.py:25
  292.3 10.3 %collective-permute-done.51.refs_3_ = bf16[3,256,384]{2,1,0:T(8,128)(2,1)S(1)} collective-permute-done((bf16[3,256,384]{2,1,0:T(8,128)(2,1)}, bf16[3,256,384]{2,1,0:T(8,128)(2,1)S(1)}, u32[]{:S(2)}, u32[]{:S(2)}) %collective-permute-start.51) | collective-permute-done | bytes 589856 | tf_op jit(solution)/shard_map/ppermute | solution.py:25
  314.4 7.6 fusion.82
  326.7 11.1 %fusion.2 = (bf16[512,3072]{1,0:T(8,128)(2,1)}, bf16[512,3072]{1,0:T(8,128)(2,1)}, bf16[512,3072]{1,0:T(8,128)(2,1)}) fusion(f32[3072,512]{0,1:T(8,128)} %fusion.83, f32[512,3072]{1,0:T(8,128)} %fusion.82, bf16[512,1024]{1,0:T(8,128)(2,1)S(1)} %copy-done.59, bf16[1024,3072]{1,0:T(8,128)(2,1)S(1)} %place.12), kind=kOutput, calls=%fused_computation.8 | convolution fusion | flops 3246391296 | bytes 29360128 | tf_op jit(solution)/shard_map/dot_general | solution.py:416
  337.8 6.9 add_convert_fusion.12
  359.1 65.4 %attend_back.1 = (bf16[512,2048]{1,0:T(8,128)(2,1)S(1)}, bf16[1280,1024]{1,0:T(8,128)(2,1)S(1)}, bf16[1280,1024]{1,0:T(8,128)(2,1)S(1)}, f32[1,128]{1,0:T(1,128)S(1)}, f32[1,128]{1,0:T(1,128)S(1)}) custom-call(s32[3]{0:T(128)S(1)} %pad_add_fusion.1.sel_ref, f32[512,2048]{1,0:T(8,128)} %copy-done, f32[1280,1024]{1,0:T(8,128)} %fusion.81.k_ref, ...), custom_call_target="tpu_custom_call" | custom-call | tf_op jit(solution)/shard_map/attend_back/pallas_call | solution.py:379
  464.1 18.8 %collective-permute-done.77 = bf16[256,1024]{1,0:T(8,128)(2,1)S(1)} collective-permute-done((bf16[256,1024]{1,0:T(8,128)(2,1)S(1)}, bf16[256,1024]{1,0:T(8,128)(2,1)S(1)}, u32[]{:S(2)}, u32[]{:S(2)}) %collective-permute-start.77) | collective-permute-done | bytes 524320 | tf_op jit(solution)/shard_map/ppermute | solution.py:30
  506.1 9.8 %collective-permute-done.99 = bf16[1024,256]{1,0:T(8,128)(2,1)S(1)} collective-permute-done((bf16[1024,256]{1,0:T(8,128)(2,1)S(1)}, bf16[1024,256]{1,0:T(8,128)(2,1)S(1)}, u32[]{:S(2)}, u32[]{:S(2)}) %collective-permute-start.99) | collective-permute-done | bytes 524320 | tf_op jit(solution)/shard_map/ppermute | solution.py:25
  516.2 10.0 %collective-permute-done.112 = bf16[1024,256]{1,0:T(8,128)(2,1)S(1)} collective-permute-done((bf16[1024,256]{1,0:T(8,128)(2,1)S(1)}, bf16[1024,256]{1,0:T(8,128)(2,1)S(1)}, u32[]{:S(2)}, u32[]{:S(2)}) %collective-permute-start.112) | collective-permute-done | bytes 524320 | tf_op jit(solution)/shard_map/ppermute | solution.py:25
  526.9 6.5 collective-permute-done.100
  539.7 9.7 %collective-permute-start.101 = (bf16[256,128]{1,0:T(8,128)(2,1)S(1)}, bf16[256,128]{1,0:T(8,128)(2,1)S(1)}, u32[]{:S(2)}, u32[]{:S(2)}) collective-permute-start(bf16[256,128]{1,0:T(8,128)(2,1)S(1)} %constant_dynamic-slice_fusion.15), channel_id=1, source_target_pairs={{0,1},{1,2},{2,3},{3,0},{4,5},{5,6},{6,7},{7,4},{8,9},{9,10},{10,1... | collective-permute-start | bytes 196616 | tf_op jit(solution)/shard_map/ppermute | solution.py:30
  554.5 6.7 collective-permute-done.114
  599.0 11.5 %collective-permute-done.125 = bf16[2048,256]{1,0:T(8,128)(2,1)S(1)} collective-permute-done((bf16[2048,256]{1,0:T(8,128)(2,1)S(1)}, bf16[2048,256]{1,0:T(8,128)(2,1)S(1)}, u32[]{:S(2)}, u32[]{:S(2)}) %collective-permute-start.125) | collective-permute-done | bytes 1048608 | tf_op jit(solution)/shard_map/ppermute | solution.py:25
  627.4 6.6 collective-permute-done.88
  634.1 6.8 collective-permute-done.127
  640.9 7.9 collective-permute-done.89
  648.8 7.4 collective-permute-done.128
  656.3 6.7 collective-permute-done.90
  665.7 26.1 %collective-permute-done.164 = bf16[3072,256]{1,0:T(8,128)(2,1)S(1)} collective-permute-done((bf16[3072,256]{1,0:T(8,128)(2,1)S(1)}, bf16[3072,256]{1,0:T(8,128)(2,1)S(1)}, u32[]{:S(2)}, u32[]{:S(2)}) %collective-permute-start.164) | collective-permute-done | bytes 1572896 | tf_op jit(solution)/shard_map/ppermute | solution.py:25
  694.6 9.3 %collective-permute-done.152 = bf16[1024,384]{1,0:T(8,128)(2,1)S(1)} collective-permute-done((bf16[1024,384]{1,0:T(8,128)(2,1)S(1)}, bf16[1024,384]{1,0:T(8,128)(2,1)S(1)}, u32[]{:S(2)}, u32[]{:S(2)}) %collective-permute-start.152) | collective-permute-done | bytes 786464 | tf_op jit(solution)/shard_map/ppermute | solution.py:25
  706.0 9.0 %collective-permute-done.140 = bf16[256,384]{1,0:T(8,128)(2,1)S(1)} collective-permute-done((bf16[256,384]{1,0:T(8,128)(2,1)S(1)}, bf16[256,384]{1,0:T(8,128)(2,1)S(1)}, u32[]{:S(2)}, u32[]{:S(2)}) %collective-permute-start.140) | collective-permute-done | bytes 196640 | tf_op jit(solution)/shard_map/ppermute | solution.py:30
  723.7 6.8 collective-permute-done.166
  731.7 8.2 collective-permute-done.141
  740.8 8.0 collective-permute-done.154
  757.3 7.9 collective-permute-done.142
  766.1 8.2 collective-permute-done.155
  (789 shorter events, 415.3 us)
Async XLA Ops:
  1.6 57.4 %collective-permute-start.6 = (bf16[256,256]{1,0:T(8,128)(2,1)S(1)}, bf16[256,256]{1,0:T(8,128)(2,1)}, u32[]{:S(2)}, u32[]{:S(2)}) collective-permute-start(bf16[256,256]{1,0:T(8,128)(2,1)S(1)} %constant_dynamic-slice_fusion.32), channel_id=1, source_target_pairs={{0,1},{1,2},{2,3},{3,0},{4,5},{5,6},{6,7},{7,4},{8,9},{9,10},{10,1... | collective-permute-start | bytes 393224 | tf_op jit(solution)/shard_map/ppermute | solution.py:30
  5.4 43.3 %collective-permute-start.5 = (bf16[576]{0:T(1024)(128)(2,1)S(1)}, bf16[576]{0:T(1024)(128)(2,1)S(1)}, u32[]{:S(2)}, u32[]{:S(2)}) collective-permute-start(bf16[576]{0:T(1024)(128)(2,1)S(1)} %pad_maximum_fusion.10), channel_id=1, source_target_pairs={{0,3},{1,0},{2,1},{3,2},{4,7},{5,4},{6,5},{7,6},{8,11},{9,8},{10,9... | collective-permute-start | bytes 3464 | tf_op jit(solution)/shard_map/ppermute | solution.py:30
  11.6 52.9 %collective-permute-start.36 = (bf16[512,128]{1,0:T(8,128)(2,1)S(1)}, bf16[512,128]{1,0:T(8,128)(2,1)}, u32[]{:S(2)}, u32[]{:S(2)}) collective-permute-start(bf16[512,128]{1,0:T(8,128)(2,1)S(1)} %constant_dynamic-slice_fusion.24), channel_id=1, source_target_pairs={{0,1},{1,2},{2,3},{3,0},{4,5},{5,6},{6,7},{7,4},{8,9},{9,10},{10,1... | collective-permute-start | bytes 393224 | tf_op jit(solution)/shard_map/ppermute | solution.py:30
  87.5 63.9 %collective-permute-start.2 = (bf16[256,1024]{1,0:T(8,128)(2,1)}, bf16[256,1024]{1,0:T(8,128)(2,1)}, u32[]{:S(2)}, u32[]{:S(2)}) collective-permute-start(bf16[256,1024]{1,0:T(8,128)(2,1)} %get-tuple-element.39), channel_id=1, source_target_pairs={{0,3},{1,0},{2,1},{3,2},{4,7},{5,4},{6,5},{7,6},{8,11},{9,8},{10,9... | collective-permute-start | bytes 1572872 | tf_op jit(solution)/shard_map/ppermute | solution.py:30
  90.3 63.6 %collective-permute-start.1 = (bf16[256,1024]{1,0:T(8,128)(2,1)}, bf16[256,1024]{1,0:T(8,128)(2,1)}, u32[]{:S(2)}, u32[]{:S(2)}) collective-permute-start(bf16[256,1024]{1,0:T(8,128)(2,1)} %get-tuple-element.38), channel_id=1, source_target_pairs={{0,2},{1,3},{2,0},{3,1},{4,6},{5,7},{6,4},{7,5},{8,10},{9,11},{10,... | collective-permute-start | bytes 1572872 | tf_op jit(solution)/shard_map/ppermute | solution.py:30
  90.9 64.6 %collective-permute-start = (bf16[256,1024]{1,0:T(8,128)(2,1)}, bf16[256,1024]{1,0:T(8,128)(2,1)}, u32[]{:S(2)}, u32[]{:S(2)}) collective-permute-start(bf16[256,1024]{1,0:T(8,128)(2,1)} %get-tuple-element.37), channel_id=1, source_target_pairs={{0,1},{1,2},{2,3},{3,0},{4,5},{5,6},{6,7},{7,4},{8,9},{9,10},{10,1... | collective-permute-start | bytes 1572872 | tf_op jit(solution)/shard_map/ppermute | solution.py:30
  92.9 49.6 %collective-permute-start.67 = (bf16[768,128]{1,0:T(8,128)(2,1)}, bf16[768,128]{1,0:T(8,128)(2,1)S(1)}, u32[]{:S(2)}, u32[]{:S(2)}) collective-permute-start(bf16[768,128]{1,0:T(8,128)(2,1)} %copy-done.93), channel_id=1, source_target_pairs={{0,1},{1,2},{2,3},{3,0},{4,5},{5,6},{6,7},{7,4},{8,9},{9,10},{10,1... | collective-permute-start | bytes 589832 | tf_op jit(solution)/shard_map/ppermute | solution.py:30
  96.0 36.2 %collective-permute-start.38 = (bf16[512,128]{1,0:T(8,128)(2,1)S(1)}, bf16[512,128]{1,0:T(8,128)(2,1)S(1)}, u32[]{:S(2)}, u32[]{:S(2)}) collective-permute-start(bf16[512,128]{1,0:T(8,128)(2,1)S(1)} %collective-permute-done.37), channel_id=1, source_target_pairs={{0,1},{1,2},{2,3},{3,0},{4,5},{5,6},{6,7},{7,4},{8,9},{9,10},{10,1... | collective-permute-start | bytes 393224 | tf_op jit(solution)/shard_map/ppermute | solution.py:30
  217.0 44.7 %collective-permute-start.72 = (bf16[3,768,128]{2,1,0:T(8,128)(2,1)S(1)}, bf16[3,768,128]{2,1,0:T(8,128)(2,1)}, u32[]{:S(2)}, u32[]{:S(2)}) collective-permute-start(bf16[3,768,128]{2,1,0:T(8,128)(2,1)S(1)} %pad_maximum_fusion.5.refs_0_), channel_id=1, source_target_pairs={{0,4},{4,0},{8,12},{12,8},{16,20},{20,16},{24,28},{28,24},{1,5},{5... | collective-permute-start | bytes 1769480 | tf_op jit(solution)/shard_map/ppermute | solution.py:25
  217.5 45.1 %collective-permute-start.49 = (bf16[3,256,384]{2,1,0:T(8,128)(2,1)}, bf16[3,256,384]{2,1,0:T(8,128)(2,1)}, u32[]{:S(2)}, u32[]{:S(2)}) collective-permute-start(bf16[3,256,384]{2,1,0:T(8,128)(2,1)} %pad_maximum_fusion.3.refs_0_), channel_id=1, source_target_pairs={{0,8},{4,12},{8,0},{12,4},{16,24},{20,28},{24,16},{28,20},{1,9},{5... | collective-permute-start | bytes 1769480 | tf_op jit(solution)/shard_map/ppermute | solution.py:25
  225.0 37.6 %collective-permute-start.71 = (bf16[3,768,128]{2,1,0:T(8,128)(2,1)}, bf16[3,768,128]{2,1,0:T(8,128)(2,1)}, u32[]{:S(2)}, u32[]{:S(2)}) collective-permute-start(bf16[3,768,128]{2,1,0:T(8,128)(2,1)} %collective-permute-done.69.refs_1_), channel_id=1, source_target_pairs={{0,16},{4,20},{8,24},{12,28},{16,0},{20,4},{24,8},{28,12},{1,17},{... | collective-permute-start | bytes 1769480 | tf_op jit(solution)/shard_map/ppermute | solution.py:25
  226.6 37.4 %collective-permute-start.73 = (bf16[3,768,128]{2,1,0:T(8,128)(2,1)}, bf16[3,768,128]{2,1,0:T(8,128)(2,1)}, u32[]{:S(2)}, u32[]{:S(2)}) collective-permute-start(bf16[3,768,128]{2,1,0:T(8,128)(2,1)} %collective-permute-done.69.refs_1_), channel_id=1, source_target_pairs={{0,4},{4,0},{8,12},{12,8},{16,20},{20,16},{24,28},{28,24},{1,5},{5... | collective-permute-start | bytes 1769480 | tf_op jit(solution)/shard_map/ppermute | solution.py:25
  226.6 38.2 %collective-permute-start.74 = (bf16[3,768,128]{2,1,0:T(8,128)(2,1)}, bf16[3,768,128]{2,1,0:T(8,128)(2,1)}, u32[]{:S(2)}, u32[]{:S(2)}) collective-permute-start(bf16[3,768,128]{2,1,0:T(8,128)(2,1)} %collective-permute-done.70.refs_2_), channel_id=1, source_target_pairs={{0,4},{4,0},{8,12},{12,8},{16,20},{20,16},{24,28},{28,24},{1,5},{5... | collective-permute-start | bytes 1769480 | tf_op jit(solution)/shard_map/ppermute | solution.py:25
  263.9 38.7 %collective-permute-start.51 = (bf16[3,256,384]{2,1,0:T(8,128)(2,1)}, bf16[3,256,384]{2,1,0:T(8,128)(2,1)S(1)}, u32[]{:S(2)}, u32[]{:S(2)}) collective-permute-start(bf16[3,256,384]{2,1,0:T(8,128)(2,1)} %collective-permute-done.49.refs_1_), channel_id=1, source_target_pairs={{0,16},{4,20},{8,24},{12,28},{16,0},{20,4},{24,8},{28,12},{1,17},{... | collective-permute-start | bytes 1769480 | tf_op jit(solution)/shard_map/ppermute | solution.py:25
  268.9 39.2 %collective-permute-start.60 = (bf16[3,256,384]{2,1,0:T(8,128)(2,1)}, bf16[3,256,384]{2,1,0:T(8,128)(2,1)}, u32[]{:S(2)}, u32[]{:S(2)}) collective-permute-start(bf16[3,256,384]{2,1,0:T(8,128)(2,1)} %pad_maximum_fusion.4.refs_0_), channel_id=1, source_target_pairs={{0,8},{4,12},{8,0},{12,4},{16,24},{20,28},{24,16},{28,20},{1,9},{5... | collective-permute-start | bytes 1769480 | tf_op jit(solution)/shard_map/ppermute | solution.py:25
  444.7 38.2 %collective-permute-start.77 = (bf16[256,1024]{1,0:T(8,128)(2,1)S(1)}, bf16[256,1024]{1,0:T(8,128)(2,1)S(1)}, u32[]{:S(2)}, u32[]{:S(2)}) collective-permute-start(bf16[256,1024]{1,0:T(8,128)(2,1)S(1)} %get-tuple-element.36), channel_id=1, source_target_pairs={{0,2},{1,3},{2,0},{3,1},{4,6},{5,7},{6,4},{7,5},{8,10},{9,11},{10,... | collective-permute-start | bytes 1572872 | tf_op jit(solution)/shard_map/ppermute | solution.py:30
  446.8 37.7 %collective-permute-start.76 = (bf16[256,1024]{1,0:T(8,128)(2,1)S(1)}, bf16[256,1024]{1,0:T(8,128)(2,1)S(1)}, u32[]{:S(2)}, u32[]{:S(2)}) collective-permute-start(bf16[256,1024]{1,0:T(8,128)(2,1)S(1)} %get-tuple-element.34), channel_id=1, source_target_pairs={{0,3},{1,0},{2,1},{3,2},{4,7},{5,4},{6,5},{7,6},{8,11},{9,8},{10,9... | collective-permute-start | bytes 1572872 | tf_op jit(solution)/shard_map/ppermute | solution.py:30
  452.8 121.2 %collective-permute-start.85 = (bf16[1024,1024]{1,0:T(8,128)(2,1)}, bf16[1024,1024]{1,0:T(8,128)(2,1)}, u32[]{:S(2)}, u32[]{:S(2)}) collective-permute-start(bf16[1024,1024]{1,0:T(8,128)(2,1)} %convolution_convert_fusion.6), channel_id=1, source_target_pairs={{0,4},{4,0},{8,12},{12,8},{16,20},{20,16},{24,28},{28,24},{1,5},{5... | collective-permute-start | bytes 6291464 | tf_op jit(solution)/shard_map/ppermute | solution.py:25
  452.8 43.9 %collective-permute-start.98 = (bf16[1024,512]{1,0:T(8,128)(2,1)}, bf16[1024,512]{1,0:T(8,128)(2,1)}, u32[]{:S(2)}, u32[]{:S(2)}) collective-permute-start(bf16[1024,512]{1,0:T(8,128)(2,1)} %convolution_convert_fusion.8), channel_id=1, source_target_pairs={{0,4},{4,0},{8,12},{12,8},{16,20},{20,16},{24,28},{28,24},{1,5},{5... | collective-permute-start | bytes 3145736 | tf_op jit(solution)/shard_map/ppermute | solution.py:25
  462.9 38.2 %collective-permute-start.111 = (bf16[1024,512]{1,0:T(8,128)(2,1)}, bf16[1024,512]{1,0:T(8,128)(2,1)}, u32[]{:S(2)}, u32[]{:S(2)}) collective-permute-start(bf16[1024,512]{1,0:T(8,128)(2,1)} %convolution_convert_fusion.7), channel_id=1, source_target_pairs={{0,4},{4,0},{8,12},{12,8},{16,20},{20,16},{24,28},{28,24},{1,5},{5... | collective-permute-start | bytes 3145736 | tf_op jit(solution)/shard_map/ppermute | solution.py:25
  482.9 94.3 %collective-permute-start.124 = (bf16[2048,512]{1,0:T(8,128)(2,1)}, bf16[2048,512]{1,0:T(8,128)(2,1)}, u32[]{:S(2)}, u32[]{:S(2)}) collective-permute-start(bf16[2048,512]{1,0:T(8,128)(2,1)} %convolution_convert_fusion.5), channel_id=1, source_target_pairs={{0,4},{4,0},{8,12},{12,8},{16,20},{20,16},{24,28},{28,24},{1,5},{5... | collective-permute-start | bytes 6291464 | tf_op jit(solution)/shard_map/ppermute | solution.py:25
  496.3 116.0 %collective-permute-start.137 = (bf16[1024,1536]{1,0:T(8,128)(2,1)S(1)}, bf16[1024,1536]{1,0:T(8,128)(2,1)S(1)}, u32[]{:S(2)}, u32[]{:S(2)}) collective-permute-start(bf16[1024,1536]{1,0:T(8,128)(2,1)S(1)} %copy-done.133), channel_id=1, source_target_pairs={{0,4},{4,0},{8,12},{12,8},{16,20},{20,16},{24,28},{28,24},{1,5},{5... | collective-permute-start | bytes 9437192 | tf_op jit(solution)/shard_map/ppermute | solution.py:25
  516.0 101.0 %collective-permute-start.150 = (bf16[1024,1536]{1,0:T(8,128)(2,1)S(1)}, bf16[1024,1536]{1,0:T(8,128)(2,1)}, u32[]{:S(2)}, u32[]{:S(2)}) collective-permute-start(bf16[1024,1536]{1,0:T(8,128)(2,1)S(1)} %copy-done.132), channel_id=1, source_target_pairs={{0,4},{4,0},{8,12},{12,8},{16,20},{20,16},{24,28},{28,24},{1,5},{5... | collective-permute-start | bytes 9437192 | tf_op jit(solution)/shard_map/ppermute | solution.py:25
  581.2 41.6 %collective-permute-start.163 = (bf16[3072,512]{1,0:T(8,128)(2,1)S(1)}, bf16[3072,512]{1,0:T(8,128)(2,1)S(1)}, u32[]{:S(2)}, u32[]{:S(2)}) collective-permute-start(bf16[3072,512]{1,0:T(8,128)(2,1)S(1)} %copy-done.131), channel_id=1, source_target_pairs={{0,4},{4,0},{8,12},{12,8},{16,20},{20,16},{24,28},{28,24},{1,5},{5... | collective-permute-start | bytes 9437192 | tf_op jit(solution)/shard_map/ppermute | solution.py:25
  594.8 120.3 %collective-permute-start.84 = (f32[18,128]{1,0:T(8,128)S(1)}, f32[18,128]{1,0:T(8,128)S(1)}, u32[]{:S(2)}, u32[]{:S(2)}) collective-permute-start(f32[18,128]{1,0:T(8,128)S(1)} %add.1038), channel_id=1, source_target_pairs={{0,3},{1,0},{2,1},{3,2},{4,7},{5,4},{6,5},{7,6},{8,11},{9,8},{10,9... | collective-permute-start | bytes 27656 | tf_op jit(solution)/shard_map/ppermute | solution.py:30
  617.0 46.1 %collective-permute-start.138 = (bf16[1024,768]{1,0:T(8,128)(2,1)S(1)}, bf16[1024,768]{1,0:T(8,128)(2,1)S(1)}, u32[]{:S(2)}, u32[]{:S(2)}) collective-permute-start(bf16[1024,768]{1,0:T(8,128)(2,1)S(1)} %constant_dynamic-slice_fusion.8), channel_id=1, source_target_pairs={{0,8},{4,12},{8,0},{12,4},{16,24},{20,28},{24,16},{28,20},{1,9},{5... | collective-permute-start | bytes 4718600 | tf_op jit(solution)/shard_map/ppermute | solution.py:25
  622.8 41.0 %collective-permute-start.151 = (bf16[1024,768]{1,0:T(8,128)(2,1)S(1)}, bf16[1024,768]{1,0:T(8,128)(2,1)S(1)}, u32[]{:S(2)}, u32[]{:S(2)}) collective-permute-start(bf16[1024,768]{1,0:T(8,128)(2,1)S(1)} %constant_dynamic-slice_fusion.5), channel_id=1, source_target_pairs={{0,16},{4,20},{8,24},{12,28},{16,0},{20,4},{24,8},{28,12},{1,17},{... | collective-permute-start | bytes 4718600 | tf_op jit(solution)/shard_map/ppermute | solution.py:25
  626.0 65.9 %collective-permute-start.164 = (bf16[3072,256]{1,0:T(8,128)(2,1)S(1)}, bf16[3072,256]{1,0:T(8,128)(2,1)S(1)}, u32[]{:S(2)}, u32[]{:S(2)}) collective-permute-start(bf16[3072,256]{1,0:T(8,128)(2,1)S(1)} %constant_dynamic-slice_fusion.2), channel_id=1, source_target_pairs={{0,8},{4,12},{8,0},{12,4},{16,24},{20,28},{24,16},{28,20},{1,9},{5... | collective-permute-start | bytes 4718600 | tf_op jit(solution)/shard_map/ppermute | solution.py:25
  663.0 52.7 %collective-permute-start.83 = (f32[18,128]{1,0:T(8,128)S(1)}, f32[18,128]{1,0:T(8,128)S(1)}, u32[]{:S(2)}, u32[]{:S(2)}) collective-permute-start(f32[18,128]{1,0:T(8,128)S(1)} %add.1038), channel_id=1, source_target_pairs={{0,2},{1,3},{2,0},{3,1},{4,6},{5,7},{6,4},{7,5},{8,10},{9,11},{10,... | collective-permute-start | bytes 27656 | tf_op jit(solution)/shard_map/ppermute | solution.py:30
  795.6 37.3 %collective-permute-start.172 = (bf16[768,128]{1,0:T(8,128)(2,1)S(1)}, bf16[768,128]{1,0:T(8,128)(2,1)S(1)}, u32[]{:S(2)}, u32[]{:S(2)}) collective-permute-start(bf16[768,128]{1,0:T(8,128)(2,1)S(1)} %add_convert_fusion.22.refs_0_), channel_id=1, source_target_pairs={{0,4},{4,0},{8,12},{12,8},{16,20},{20,16},{24,28},{28,24},{1,5},{5... | collective-permute-start | bytes 589832 | tf_op jit(solution)/shard_map/ppermute | solution.py:25
  795.6 37.3 %collective-permute-start.173 = (bf16[768,128]{1,0:T(8,128)(2,1)}, bf16[768,128]{1,0:T(8,128)(2,1)S(1)}, u32[]{:S(2)}, u32[]{:S(2)}) collective-permute-start(bf16[768,128]{1,0:T(8,128)(2,1)} %collective-permute-done.169.refs_1_), channel_id=1, source_target_pairs={{0,4},{4,0},{8,12},{12,8},{16,20},{20,16},{24,28},{28,24},{1,5},{5... | collective-permute-start | bytes 589832 | tf_op jit(solution)/shard_map/ppermute | solution.py:25
  796.1 36.8 %collective-permute-start.174 = (bf16[768,128]{1,0:T(8,128)(2,1)}, bf16[768,128]{1,0:T(8,128)(2,1)S(1)}, u32[]{:S(2)}, u32[]{:S(2)}) collective-permute-start(bf16[768,128]{1,0:T(8,128)(2,1)} %collective-permute-done.170.refs_2_), channel_id=1, source_target_pairs={{0,4},{4,0},{8,12},{12,8},{16,20},{20,16},{24,28},{28,24},{1,5},{5... | collective-permute-start | bytes 589832 | tf_op jit(solution)/shard_map/ppermute | solution.py:25
  (286 other events, 4432.7 us)

commit v2 on v1

--- a/solution.py
+++ b/solution.py
@@ -17,7 +17,7 @@
 BF16 = jnp.bfloat16
 SCALE = HEAD_WIDTH ** (-0.5)
 EXP2_SCALE = SCALE * math.log2(math.e)
-VMEM_LIMIT = 40 * 1024 * 1024
+VMEM_LIMIT = 48 * 1024 * 1024
 
 
 def dp_swap(x, bit):
@@ -181,6 +181,271 @@
     return full
 
 
+def after(done, values):
+    return lax.optimization_barrier((done, values))[1]
+
+
+def stream_masks(order):
+    masks = [0]
+    for bit in order:
+        masks = masks + [m ^ (1 << bit) for m in masks]
+    return masks
+
+
+def pieces_of(order, core_last=True):
+    d = lax.axis_index("dp")
+    masks = stream_masks(order)
+    masks = masks + [m ^ 1 for m in masks] if core_last else masks
+    return masks, [column_piece(d ^ m, order) for m in masks]
+
+
+def place_units_kernel(shards, unit, width, units, offset, counts, at_ref, own_ref, *refs):
+    out_ref, sems = refs[-2], refs[-1]
+    rows = units * unit
+    zero = pl.multiple_of(at_ref[0] * rows, rows)
+    copies = [pltpu.make_async_copy(own_ref, out_ref.at[pl.ds(zero, rows), :], sems.at[0])]
+    piece = 0
+    for i, count in enumerate(counts):
+        for e in range(count):
+            column = pl.multiple_of(at_ref[shards + piece] * width, width)
+            for t in range(1, shards):
+                for u in range(units):
+                    row = pl.multiple_of(at_ref[t] * rows + u * unit, unit)
+                    source = refs[i].at[
+                        e, t - 1, :, offset + u * width : offset + (u + 1) * width
+                    ]
+                    copies.append(
+                        pltpu.make_async_copy(
+                            source,
+                            out_ref.at[pl.ds(row, unit), pl.ds(column, width)],
+                            sems.at[len(copies)],
+                        )
+                    )
+            piece += 1
+    for copy in copies:
+        copy.start()
+    for copy in copies:
+        copy.wait()
+
+
+def place_units(own, arrays, unit, offset, flip):
+    shards = lax.axis_size("shard")
+    z = lax.axis_index("shard")
+    rows, total = own.shape
+    width = total // lax.axis_size("dp")
+    units = rows // unit
+    _, columns = pieces_of(plane_order(flip))
+    at = jnp.stack([(z - t) % shards for t in range(shards)] + columns).astype(jnp.int32)
+    counts = [a.shape[0] for a in arrays]
+    return pl.pallas_call(
+        functools.partial(place_units_kernel, shards, unit, width, units, offset, counts),
+        out_shape=jax.ShapeDtypeStruct((shards * rows, total), own.dtype),
+        grid_spec=pltpu.PrefetchScalarGridSpec(
+            num_scalar_prefetch=1,
+            grid=(1,),
+            in_specs=[pl.BlockSpec(memory_space=pl.ANY)] * (1 + len(arrays)),
+            out_specs=pl.BlockSpec((shards * rows, total), lambda i, at: (0, 0)),
+            scratch_shapes=[pltpu.SemaphoreType.DMA((1 + sum(counts) * (shards - 1) * units,))],
+        ),
+        compiler_params=pltpu.CompilerParams(vmem_limit_bytes=VMEM_LIMIT),
+        name="place",
+    )(at, own, *arrays)
+
+
+def own_piece(own, unit, flip):
+    order = plane_order(flip)
+    rows, total = own.shape
+    width = total // lax.axis_size("dp")
+    piece = lax.dynamic_slice_in_dim(
+        own, column_piece(lax.axis_index("dp"), order) * width, width, axis=1
+    )
+    return jnp.concatenate(jnp.split(piece, rows // unit, axis=0), axis=1)
+
+
+def grow(streams, step):
+    bits = [plane_order(bool(s))[step] for s in range(len(streams))]
+    return [dp_swap(x, bit) for x, bit in zip(streams, bits)]
+
+
+def join(held, arrived):
+    return [jnp.concatenate([a, b], axis=0) for a, b in zip(held, arrived)]
+
+
+def grads_kernel(units, items, counts, at_ref, *refs):
+    lefts, rights, arrived, outs, turned = [], [], [], [], []
+    start = 0
+    for group, count in zip((lefts, rights, arrived, outs, turned), counts):
+        group.extend(refs[start : start + count])
+        start += count
+
+    @pl.when(pl.program_id(0) == 0)
+    def _():
+        for u, (left, starts, size) in enumerate(units):
+            for a, first in enumerate(starts):
+                turned[u][a * size : (a + 1) * size, :] = lefts[left][:, first : first + size].T
+
+    for stream, unit, right, offset, width in items:
+        rows = rights[right].shape[0]
+        pair = jnp.concatenate([rights[right][...], rights[right + 1][...]], axis=1)
+        value = dot_nn(turned[unit][:, :rows], pair)
+        columns = slice(offset, offset + width)
+        for i in range(2):
+            part = value[:, i * width : (i + 1) * width]
+            if arrived:
+                part = part + arrived[stream][i, :, columns].astype(F32)
+            outs[stream][i, :, columns] = part.astype(BF16)
+
+
+def grads(streams, unit, own, arrived=()):
+    shards = lax.axis_size("shard")
+    d = lax.axis_index("dp")
+    lefts, units, rights, right_specs, items, widths, at = [], [], [], [], [], [], []
+    unit_index = {}
+    pieces = lax.axis_size("dp") // 2
+    for s, stream in enumerate(streams):
+        order = plane_order(bool(s))
+        at += [column_piece(d ^ m ^ (0 if own else 1), order) for m in stream_masks(order)]
+        offset = 0
+        for left, right in stream:
+            width = right.shape[1] // (2 * pieces)
+            for i in range(2):
+                rights.append(right)
+                right_specs.append(
+                    pl.BlockSpec(
+                        (right.shape[0], width),
+                        lambda e, at, s=s, i=i: (0, at[s * pieces + 2 * e + i]),
+                    )
+                )
+            rows = left.shape[1] // shards
+            for u in range(rows // unit):
+                if (id(left), u) not in unit_index:
+                    known = [i for i, x in enumerate(lefts) if x is left]
+                    if not known:
+                        lefts.append(left)
+                    index = known[0] if known else len(lefts) - 1
+                    unit_index[id(left), u] = len(units)
+                    units.append((index, [k * rows + u * unit for k in range(shards)], unit))
+                items.append((s, unit_index[id(left), u], len(rights) - 2, offset, width))
+                offset += width
+        widths.append(offset)
+    out_specs = [pl.BlockSpec((2, shards * unit, w), lambda e, at: (e, 0, 0)) for w in widths]
+    counts = (len(lefts), len(rights), len(arrived), len(widths), len(units))
+    flops = sum(2 * rights[i[2]].shape[0] * shards * unit * i[4] for i in items) * pieces
+    return pl.pallas_call(
+        functools.partial(grads_kernel, units, items, counts),
+        out_shape=[jax.ShapeDtypeStruct((pieces, shards * unit, w), BF16) for w in widths],
+        grid_spec=pltpu.PrefetchScalarGridSpec(
+            num_scalar_prefetch=1,
+            grid=(pieces // 2,),
+            in_specs=[pl.BlockSpec(x.shape, lambda e, at: (0, 0)) for x in lefts]
+            + right_specs
+            + out_specs[: len(arrived)],
+            out_specs=out_specs,
+            scratch_shapes=[
+                pltpu.VMEM((shards * unit, lefts[u[0]].shape[0]), BF16) for u in units
+            ],
+        ),
+        compiler_params=pltpu.CompilerParams(vmem_limit_bytes=VMEM_LIMIT),
+        cost_estimate=pl.CostEstimate(
+            flops=flops, bytes_accessed=8 * pieces * shards * unit * sum(widths), transcendentals=0
+        ),
+        name="grads",
+    )(jnp.stack(at).astype(jnp.int32), *lefts, *rights, *arrived)
+
+
+def fold_sent(streams):
+    return [x[x.shape[0] // 2 :] for x in streams]
+
+
+def fold(streams, arrived):
+    return [
+        (x[: x.shape[0] // 2].astype(F32) + a.astype(F32)).astype(BF16)
+        for x, a in zip(streams, arrived)
+    ]
+
+
+def fold_swap(sent, step):
+    bits = [plane_order(bool(s))[::-1][step] for s in range(len(sent))]
+    return [dp_swap(x, bit) for x, bit in zip(sent, bits)]
+
+
+def z_parts(streams, unit):
+    shards = lax.axis_size("shard")
+    z = lax.axis_index("shard")
+    whole = jnp.concatenate([x[0] for x in streams], axis=1) if len(streams) > 1 else streams[0][0]
+
+    def part(k):
+        return lax.dynamic_slice_in_dim(whole, ((z + k) % shards) * unit, unit, axis=0)
+
+    return part(0), [part(k) for k in range(1, shards)]
+
+
+def z_sum(mine, arrived, streams):
+    total = mine.astype(F32)
+    for a in arrived:
+        total = total + a.astype(F32)
+    total = total.astype(BF16)
+    parts, start = [], 0
+    for x in streams:
+        parts.append(total[None, :, start : start + x.shape[2]])
+        start += x.shape[2]
+    return parts
+
+
+def widen_units_kernel(unit, parts, pieces, at_ref, *refs):
+    step = pl.program_id(0)
+    outs = refs[-len(parts) :]
+
+    def move(far):
+        for out_ref, (stream, offset, units, width) in zip(outs, parts):
+            ref = refs[2 * stream + far]
+            for u in range(units):
+                out_ref[u * unit : (u + 1) * unit, :] = ref[
+                    0, :, offset + u * width : offset + (u + 1) * width
+                ].astype(F32)
+
+    @pl.when(step < pieces)
+    def _():
+        move(0)
+
+    @pl.when(step >= pieces)
+    def _():
+        move(1)
+
+
+def widen_units(bundle, unit, weights):
+    count_dp = lax.axis_size("dp")
+    columns, specs, operands, parts, out_specs, shapes = [], [], [], [], [], []
+    offsets = [0] * len(bundle)
+    for s, (near, far) in enumerate(bundle):
+        pieces = near.shape[0]
+        columns += pieces_of(plane_order(bool(s)))[1]
+        taken = (1,) + near.shape[1:]
+        specs += [
+            pl.BlockSpec(taken, lambda i, at: (jnp.minimum(i, pieces - 1), 0, 0)),
+            pl.BlockSpec(taken, lambda i, at: (jnp.maximum(i - pieces, 0), 0, 0)),
+        ]
+        operands += [near, far]
+    for w, s in weights:
+        rows, total = w.shape
+        width = total // count_dp
+        parts.append((s, offsets[s], rows // unit, width))
+        offsets[s] += rows // unit * width
+        shapes.append(jax.ShapeDtypeStruct((rows, total), F32))
+        out_specs.append(
+            pl.BlockSpec((rows, width), lambda i, at, s=s: (0, at[s * count_dp + i]))
+        )
+    return pl.pallas_call(
+        functools.partial(widen_units_kernel, unit, parts, pieces),
+        out_shape=shapes,
+        grid_spec=pltpu.PrefetchScalarGridSpec(
+            num_scalar_prefetch=1, grid=(count_dp,), in_specs=specs, out_specs=out_specs
+        ),
+        compiler_params=pltpu.CompilerParams(vmem_limit_bytes=VMEM_LIMIT),
+        name="widen",
+    )(jnp.stack(columns).astype(jnp.int32), *operands)
+
+
 def dot_nt(a, b):
     return lax.dot_general(a, b, (((1,), (1,)), ((), ())), preferred_element_type=F32)
 
@@ -351,6 +616,15 @@
     return q_spec, k_spec, pl.BlockSpec((1, HEAD_WIDTH), fixed2), inputs
 
 
+def attention_cost(count, total, products):
+    scores = HEADS * count // 2 * total
+    return pl.CostEstimate(
+        flops=products * 2 * HEAD_WIDTH * scores,
+        bytes_accessed=16 * HEAD_WIDTH * HEADS * total,
+        transcendentals=scores,
+    )
+
+
 def attend(sel, count, total, operands):
     q_spec, _, _, inputs = attention_specs(count, total)
     return pl.pallas_call(
@@ -368,6 +642,7 @@
             ],
         ),
         compiler_params=pltpu.CompilerParams(vmem_limit_bytes=VMEM_LIMIT),
+        cost_estimate=attention_cost(count, total, 2),
         name="attend",
     )(sel, *operands)
 
@@ -401,6 +676,7 @@
             ],
         ),
         compiler_params=pltpu.CompilerParams(vmem_limit_bytes=VMEM_LIMIT),
+        cost_estimate=attention_cost(count, total, 5),
         name="attend_back",
     )(sel, *operands)
 
@@ -446,13 +722,13 @@
 
     span = span_of(z)
     slots = []
-    remote = []
+    remote_own = []
     sel = []
     numbers = [span, 2 * shards - 1 - span]
     for k in range(1, shards):
         slot = jnp.where(span < span_of(z + k), 0, 1)
         slots.append(slot)
-        remote.append(z_shift(lax.dynamic_slice_in_dim(tokens, slot * block, block, axis=0), k))
+        remote_own.append(lax.dynamic_slice_in_dim(tokens, slot * block, block, axis=0))
         other = span_of(z - k + shards)
         sel.append(jnp.where(other < span, 0, 1))
         numbers.append(jnp.where(other < span, other, 2 * shards - 1 - other))
@@ -460,7 +736,66 @@
 
     sizes = [attn_gain.shape[0], mlp_gain.shape[0], q_gain.shape[0], k_gain.shape[0]]
     own_gains = jnp.concatenate([attn_gain, mlp_gain, q_gain, k_gain])
-    gains = jnp.stack([own_gains] + [z_shift(own_gains, k) for k in range(1, shards)])
+    unit = w_query.shape[0]
+    count_dp = lax.axis_size("dp")
+    bundled = all(
+        w.shape[1] % (128 * count_dp) == 0 and w.shape[0] % unit == 0
+        for w in (w_query, w_key, w_value, w_out, w_gate, w_up, w_down)
+    ) and count_dp == 8
+    if bundled:
+
+        def own_pieces(streams):
+            own = [
+                jnp.concatenate([own_piece(w, unit, bool(s)) for w in stream], axis=1)
+                for s, stream in enumerate(streams)
+            ]
+            return jnp.concatenate(own, axis=1), own[0].shape[1]
+
+        def fetch(both):
+            return [z_shift(both, k) for k in range(1, shards)]
+
+        def streams_of(got, split):
+            return [
+                jnp.stack([g[:unit, :split] for g in got])[None],
+                jnp.stack([g[:unit, split:] for g in got])[None],
+            ]
+
+        def widely(held):
+            for step in range(1, len(plane_order(False))):
+                held = join(held, grow(held, step - 1))
+            return held, grow(held, len(plane_order(False)) - 1)
+
+        def cores(held, arrived):
+            return [[h, a, dp_swap(h, 0), dp_swap(a, 0)] for h, a in zip(held, arrived)]
+
+        both, split_attn = own_pieces([[w_query], [w_key, w_value]])
+        room = 16 * both.shape[1]
+        packed = jnp.pad(own_gains, (0, room - own_gains.shape[0])).reshape(16, both.shape[1])
+        first = fetch(jnp.concatenate([both, packed], axis=0))
+        gains = jnp.stack(
+            [own_gains] + [g[unit:].reshape(-1)[: own_gains.shape[0]] for g in first]
+        )
+        remote = [z_shift(x, k + 1) for k, x in enumerate(after(first, remote_own))]
+        held, arrived = widely(streams_of(first, split_attn))
+        held, arrived = after(remote, (held, arrived))
+        near_q, near_kv = cores(held, arrived)
+        both, split_out = own_pieces([[w_gate], [w_out]])
+        second = fetch(after((near_q, near_kv), both))
+        piece = w_key.shape[1] // count_dp
+        full_query = place_units(w_query, near_q, unit, 0, False)
+        full_key = place_units(w_key, near_kv, unit, 0, True)
+        full_value = place_units(w_value, near_kv, unit, piece, True)
+    else:
+        gains = jnp.stack([own_gains] + [z_shift(own_gains, k) for k in range(1, shards)])
+        remote = [z_shift(x, k + 1) for k, x in enumerate(remote_own)]
+        full_query = gather_weight(w_query, False)
+        full_key = gather_weight(w_key, True)
+        full_value = gather_weight(w_value, True)
+        full_out = gather_weight(w_out, True)
+        full_gate = gather_weight(w_gate, False)
+        full_up = gather_weight(w_up, True)
+        full_down = gather_weight(w_down, False)
+
     order = (z - jnp.arange(shards)) % shards
     pick = order[:, None] == jnp.arange(shards)[None, :]
     gains = jnp.sum(jnp.where(pick[:, :, None], gains.astype(F32)[None], 0.0), axis=1)
@@ -471,14 +806,6 @@
         start += size
     attn_g, mlp_g, q_g, k_g = parts
 
-    full_query = gather_weight(w_query, False)
-    full_key = gather_weight(w_key, True)
-    full_value = gather_weight(w_value, True)
-    full_out = gather_weight(w_out, True)
-    full_gate = gather_weight(w_gate, False)
-    full_up = gather_weight(w_up, True)
-    full_down = gather_weight(w_down, False)
-
     place = jnp.concatenate([n * block + jnp.arange(block, dtype=jnp.int32) for n in numbers])
     seg = jnp.concatenate([lax.dynamic_slice_in_dim(segment_row, n * block, block) for n in numbers])
     doc_start = jnp.sum((segment_row[None, :] < seg[:, None]).astype(jnp.int32), axis=1)
@@ -502,54 +829,170 @@
         queries, keys_pre, values, cosine, sine, q_g, k_g,
         place[None, :], by_slot(place), by_slot(doc_start),
     )
+    if bundled:
+        second, operands = lax.optimization_barrier((second, operands))
+        both, split_down = own_pieces([[w_up], [w_down]])
+        third = fetch(after(second, both))
+        held = streams_of(second, split_out)
+        held = join(held, grow(held, 0)) if len(plane_order(False)) > 1 else held
     attended = attend(sel, count, total, operands)
+    if bundled:
+        held, third, attended = lax.optimization_barrier((held, third, attended))
+        later = streams_of(third, split_down)
+        later_arrived = grow(later, 0)
+        arrived = grow(held, 1)
+        later, later_arrived, held, arrived = lax.optimization_barrier(
+            (later, later_arrived, held, arrived)
+        )
+        near_gate, near_out = cores(held, arrived)
+        later = join(later, later_arrived)
+        later, near_gate, near_out = lax.optimization_barrier((later, near_gate, near_out))
+        later_arrived = grow(later, 1)
+        full_out = place_units(w_out, near_out, unit, 0, True)
+        full_gate = place_units(w_gate, near_gate, unit, 0, False)
     residual = tokens.astype(F32) + matmul(attended, full_out)
     mixed = (residual * inverse_rms(residual) * mlp_g).astype(BF16)
     gate = matmul(mixed, full_gate)
+    if bundled:
+        later_arrived, gate = lax.optimization_barrier((later_arrived, gate))
+        near_up, near_down = cores(later, later_arrived)
+        full_up = place_units(w_up, near_up, unit, 0, False)
+        full_down = place_units(w_down, near_down, unit, 0, True)
     upward = matmul(mixed, full_up)
     sig = jax.nn.sigmoid(gate)
     hidden = (gate * sig * upward).astype(BF16)
     result = (residual + matmul(hidden, full_down)).astype(BF16)
 
-    grad_w_down = reduce_weight(hidden, out_grad, False)
-    grad_hidden = dot_nt(out_grad, full_down)
+    def swap_cores(streams):
+        return [dp_swap(x, 0) for x in streams]
+
+    def z_send(streams, chained=False):
+        mine, sent = z_parts(streams, unit)
+        got = []
+        for k, x in enumerate(sent):
+            got.append(z_shift(after(got[-1], x) if chained and got else x, k + 1))
+        return mine, got
+
+    barrier = lax.optimization_barrier
+
+    grad_rows = out_grad
+    if bundled:
+        down_pairs = [[(hidden, out_grad)]]
+        theirs = grads(down_pairs, unit, False)
+        theirs, grad_rows = barrier((theirs, out_grad))
+        down_core = swap_cores(theirs)
+    else:
+        grad_w_down = reduce_weight(hidden, out_grad, False)
+    grad_hidden = dot_nt(grad_rows, full_down)
     grad_gate = (grad_hidden * upward * sig * (1.0 + gate * (1.0 - sig))).astype(BF16)
     grad_upward = (grad_hidden * gate * sig).astype(BF16)
-    grad_w_gate = reduce_weight(mixed, grad_gate, False)
-    grad_w_up = reduce_weight(mixed, grad_upward, True)
+    if bundled:
+        down_core, grad_gate, grad_upward = barrier((down_core, grad_gate, grad_upward))
+        down_sum = grads(down_pairs, unit, True, down_core)
+        down_sum, grad_gate, grad_upward = barrier((down_sum, grad_gate, grad_upward))
+        down_first = fold_swap(fold_sent(down_sum), 0)
     grad_mixed = dot_nt(grad_gate, full_gate) + dot_nt(grad_upward, full_up)
     grad_residual, grad_mlp_gain = rms_back(grad_mixed, residual, mlp_g)
     grad_residual = grad_residual + out_grad.astype(F32)
     grad_branch = grad_residual.astype(BF16)
-    grad_attended = dot_nt(grad_branch, full_out).astype(BF16)
-    grad_w_out = reduce_weight(attended, grad_branch, True)
+    if bundled:
+        mlp_pairs = [[(mixed, grad_gate)], [(mixed, grad_upward), (attended, grad_branch)]]
+        theirs = grads(mlp_pairs, unit, False)
+        theirs, down_first, branch = barrier((theirs, down_first, grad_branch))
+        mlp_core = swap_cores(theirs)
+        down_sum = fold(down_sum, down_first)
+        down_second = fold_swap(fold_sent(down_sum), 1)
+        grad_attended = dot_nt(branch, full_out).astype(BF16)
+        mlp_core, down_second, grad_attended = barrier((mlp_core, down_second, grad_attended))
+        down_sum = fold(down_sum, down_second)
+        down_mine, down_z = z_send(down_sum)
+        mlp_sum = grads(mlp_pairs, unit, True, mlp_core)
+        mlp_sum, grad_attended = barrier((mlp_sum, grad_attended))
+        mlp_first = fold_swap(fold_sent(mlp_sum), 0)
+    else:
+        grad_attended = dot_nt(grad_branch, full_out).astype(BF16)
+        grad_w_gate = reduce_weight(mixed, grad_gate, False)
+        grad_w_up = reduce_weight(mixed, grad_upward, True)
+        grad_w_out = reduce_weight(attended, grad_branch, True)
 
     dq, dk, dv, grad_q_gain, grad_k_gain = attend_back(
         sel, count, total, operands + (attended, grad_attended)
     )
+    if bundled:
+        mlp_first, down_z, dq, dk, dv = barrier((mlp_first, down_z, dq, dk, dv))
+        mlp_sum = fold(mlp_sum, mlp_first)
+        mlp_second = fold_swap(fold_sent(mlp_sum), 1)
+        attn_pairs = [[(normed, dq)], [(normed, dk), (normed, dv)]]
+        theirs = grads(attn_pairs, unit, False)
     grad_normed_kv = dot_nt(dk, full_key) + dot_nt(dv, full_value)
+    terms = [
+        grad_normed_kv[count + (k - 1) * block : count + k * block].astype(BF16)
+        for k in range(1, shards)
+    ]
+    if bundled:
+        mlp_second, theirs = barrier((mlp_second, theirs))
+        down_sum = z_sum(down_mine, down_z, down_sum)
+        attn_core = swap_cores(theirs)
+        mlp_sum = fold(mlp_sum, mlp_second)
+    back = []
+    for k, term in enumerate(terms):
+        back.append(z_shift(after(back[-1], term) if back else term, shards - k - 1))
     grad_normed_own = grad_normed_kv[:count] + dot_nt(dq, full_query)
-    back = []
-    for k in range(1, shards):
-        term = grad_normed_kv[count + (k - 1) * block : count + k * block].astype(BF16)
-        back.append(z_shift(term, shards - k).astype(F32))
-    grad_w_query = reduce_weight(normed[:count], dq, False)
-    grad_w_key = reduce_weight(normed, dk, True)
-    grad_w_value = reduce_weight(normed, dv, True)
-
     partial = jnp.concatenate([grad_normed_own, grad_normed_kv[count:]], axis=0)
     grad_attn_gain = jnp.sum(partial * rows * inverse_rms(rows), axis=0)
+    gain_sum = jnp.concatenate(
+        [grad_attn_gain, grad_mlp_gain, grad_q_gain[0], grad_k_gain[0]]
+    ).reshape(-1, HEAD_WIDTH)
+    if bundled:
+        mlp_mine, mlp_z = z_send(mlp_sum, True)
+        attn_core, grad_normed_own = barrier((attn_core, grad_normed_own))
+        attn_sum = grads(attn_pairs, unit, True, attn_core)
+        attn_first = fold_swap(fold_sent(attn_sum), 0)
+        gain_other = dp_swap(gain_sum, 0)
+        attn_first, back, gain_other = barrier((attn_first, back, gain_other))
+        gain_sum = gain_sum + gain_other
+        attn_sum = fold(attn_sum, attn_first)
+        attn_second = fold_swap(fold_sent(attn_sum), 1)
+        gain_other = dp_swap(gain_sum, 1)
+        attn_second, mlp_z, gain_other = barrier((attn_second, mlp_z, gain_other))
+        gain_sum = gain_sum + gain_other
+        attn_sum = fold(attn_sum, attn_second)
+        attn_mine, attn_z = z_send(attn_sum)
+        gain_sum = gain_sum + dp_swap(gain_sum, 2)
+        mlp_sum = z_sum(mlp_mine, mlp_z, mlp_sum)
+
+        def whole(streams):
+            for step in range(len(plane_order(False))):
+                streams = join(streams, grow(streams, step))
+            return [(x, dp_swap(x, 0)) for x in streams]
+
+        mlp_sum = [jnp.concatenate([down_sum[0], mlp_sum[0]], axis=2), mlp_sum[1]]
+        grad_w_down, grad_w_gate, grad_w_up, grad_w_out = widen_units(
+            whole(mlp_sum), unit, [(w_down, 0), (w_gate, 0), (w_up, 1), (w_out, 1)]
+        )
+        attn_z, gain_sum = after(
+            (grad_w_down, grad_w_gate, grad_w_up, grad_w_out, gain_sum), (attn_z, gain_sum)
+        )
+        gain_sum = sum([z_shift(gain_sum, k) for k in range(1, shards)], gain_sum)
+        attn_sum = z_sum(attn_mine, attn_z, attn_sum)
+        grad_w_query, grad_w_key, grad_w_value = widen_units(
+            whole(attn_sum), unit, [(w_query, 0), (w_key, 1), (w_value, 1)]
+        )
+    else:
+        for bit in range(count_dp.bit_length() - 1):
+            gain_sum = gain_sum + dp_swap(gain_sum, bit)
+        gain_sum = sum([z_shift(gain_sum, k) for k in range(1, shards)], gain_sum)
+        grad_w_query = reduce_weight(normed[:count], dq, False)
+        grad_w_key = reduce_weight(normed, dk, True)
+        grad_w_value = reduce_weight(normed, dv, True)
+
     for slot, term in zip(slots, back):
+        term = term.astype(F32)
         first = jnp.where(slot == 0, term, 0.0)
         grad_normed_own = grad_normed_own + jnp.concatenate([first, term - first], axis=0)
     grad_tokens = grad_residual + rms_back(grad_normed_own, tokens.astype(F32), attn_g)[0]
 
-    packed = jnp.concatenate(
-        [grad_attn_gain, grad_mlp_gain, grad_q_gain[0], grad_k_gain[0]]
-    ).reshape(-1, HEAD_WIDTH)
-    for bit in range(lax.axis_size("dp").bit_length() - 1):
-        packed = packed + dp_swap(packed, bit)
-    packed = sum([z_shift(packed, k) for k in range(1, shards)], packed).reshape(-1)
+    packed = gain_sum.reshape(-1)
     gain_grads = []
     start = 0
     for size in sizes:

time: 848 us -> 696 us (0.82)
  waiting for transfers between devices: 359 us -> 214 us
  starting transfers between devices: 135 us -> 94.3 us
  Pallas kernels: 145 us -> 182 us
  matrix products: 114 us -> 86.6 us
  other arithmetic: 39.6 us -> 53.3 us
  local copies, waits for them, and re-layouts: 30.4 us -> 40.4 us
    ppermute x54 -> x27, waiting for transfers between devices: 212 us -> 98.8 us  [z_shift(): lax.ppermute(x, 'shard', [(i, (i + step) % count) for i in range(count)])]
    dot_general x14 -> x0, matrix products: 42 us -> none  [product(): lax.dot_general(left, columns, (((0,), (0,)), ((), ())), preferred_elemen...]
    pallas_call x14 -> x15, Pallas kernels: 49.5 us -> 89.8 us  [the longest x6 52.4 us: grads(): pl.pallas_call(functools.partial(grads_kernel, units, items, counts), out...]
    ppermute x122 -> x54, waiting for transfers between devices: 147 us -> 115 us  [dp_swap(): return lax.ppermute(x, 'dp', [(i, i ^ 1 << bit) for i in range(count)])]
    ppermute x122 -> x54, starting transfers between devices: 68.3 us -> 40 us  [dp_swap(): return lax.ppermute(x, 'dp', [(i, i ^ 1 << bit) for i in range(count)])]
    ppermute x54 -> x27, starting transfers between devices: 66.9 us -> 54.3 us  [z_shift(): lax.ppermute(x, 'shard', [(i, (i + step) % count) for i in range(count)])]
    concatenate x0 -> x20, other arithmetic: none -> 11.6 us  [the longest x14 7.01 us: join(): return [jnp.concatenate([a, b], axis=0) for a, b in zip(held, arrived)]]
    dot_general x7, matrix products: 38 us -> 46.9 us  [matmul(): return jnp.dot(a, b, preferred_element_type=F32)]
  transfers between devices with their start and end apart: 176 -> 81, of which waited for: 55 -> 27; matrix products, arithmetic and copies ran while one was open for 14% -> 20% of each run, Pallas kernels for 9% -> 21%
where the time goes in v2:
time: 696 us; the launch traced here: 687 us
  waiting for transfers between devices  214 us (31%)
  Pallas kernels  182 us (26%)
  starting transfers between devices  94.3 us (14%)
  matrix products  86.6 us (12%)
  other arithmetic  53.3 us (8%)
  local copies, waits for them, and re-layouts  40.4 us (6%)
  between operations  15.9 us (2%)
    ppermute x54, waiting for transfers between devices, dp_swap(): return lax.ppermute(x, 'dp', [(i, i ^ 1 << bit) for i in range(count)])  115 us
    ppermute x27, waiting for transfers between devices, z_shift(): lax.ppermute(x, 'shard', [(i, (i + step) % count) for i in range(count)])  98.8 us
    pallas_call x1, Pallas kernels, attend_back(): pl.pallas_call(attend_back_kernel, out_shape=(jax.ShapeDtypeStruct((count...  63.8 us
    ppermute x27, starting transfers between devices, z_shift(): lax.ppermute(x, 'shard', [(i, (i + step) % count) for i in range(count)])  54.3 us
    pallas_call x6, Pallas kernels, grads(): pl.pallas_call(functools.partial(grads_kernel, units, items, counts), out...  52.4 us
    dot_general x7, matrix products, matmul(): return jnp.dot(a, b, preferred_element_type=F32)  46.9 us
    ppermute x54, starting transfers between devices, dp_swap(): return lax.ppermute(x, 'dp', [(i, i ^ 1 << bit) for i in range(count)])  40 us
    dot_general x7, matrix products, dot_nt(): lax.dot_general(a, b, (((1,), (1,)), ((), ())), preferred_element_type=F32)  39.6 us
  transfers between devices with their start and end apart: 81, of which 27 were waited for; matrix products, arithmetic and copies ran while one was open for 20% of the time, Pallas kernels for 21%

profile of v2, /device:TPU:0, one launch (start us, length us, event | category | flops | bytes accessed | tf_op | source)
XLA Modules:
  0.0 686.6 jit_solution(3464287620371478190)
XLA Ops:
  55.7 6.5 collective-permute-done.3
  62.2 20.0 %collective-permute-done.4 = bf16[256,1024]{1,0:T(8,128)(2,1)} collective-permute-done((bf16[256,1024]{1,0:T(8,128)(2,1)}, bf16[256,1024]{1,0:T(8,128)(2,1)}, u32[]{:S(2)}, u32[]{:S(2)}) %collective-permute-start.4) | collective-permute-done | bytes 524320 | tf_op jit(solution)/shard_map/ppermute | solution.py:30
  90.9 11.2 %collective-permute-start.14 = (bf16[256,640]{1,0:T(8,128)(2,1)S(1)}, bf16[256,640]{1,0:T(8,128)(2,1)S(1)}, u32[]{:S(2)}, u32[]{:S(2)}) collective-permute-start(bf16[256,640]{1,0:T(8,128)(2,1)S(1)} %copy-done.57), channel_id=1, source_target_pairs={{0,1},{1,2},{2,3},{3,0},{4,5},{5,6},{6,7},{7,4},{8,9},{9,10},{10,1... | collective-permute-start | bytes 983048 | tf_op jit(solution)/shard_map/ppermute | solution.py:30
  122.9 6.6 fusion.14.q_ref
  137.5 28.2 %attend.1.refs_1_.att_ref = bf16[512,2048]{1,0:T(8,128)(2,1)S(1)} custom-call(s32[3]{0:T(128)S(1)} %pad_add_fusion.1.sel_ref, f32[512,2048]{1,0:T(8,128)} %fusion.14.q_ref, f32[1280,1024]{1,0:T(8,128)} %fusion.41.k_ref, bf16[1280,1024]{1,0:T(8,128)(2,1)} %convolution_convert_fusion.v_ref, f32[1280,128]{1,0:T(8,128)S(1)} %get-tuple-element.151.cos_ref, ...), custom_call_target="tpu_custom_call" | custom-call | flops 2684354560 | bytes 41943040 | tf_op jit(solution)/shard_map/attend/pallas_call | solution.py:630
  176.5 32.4 %collective-permute-done.23 = bf16[1,3,256,384]{3,2,1,0:T(8,128)(2,1)S(1)} collective-permute-done((bf16[1,3,256,384]{3,2,1,0:T(8,128)(2,1)S(1)}, bf16[1,3,256,384]{3,2,1,0:T(8,128)(2,1)S(1)}, u32[]{:S(2)}, u32[]{:S(2)}) %collective-permute-start.23) | collective-permute-done | bytes 589856 | tf_op jit(solution)/shard_map/ppermute | solution.py:25
  232.8 8.2 %fusion.42 = f32[512,3072]{1,0:T(8,128)} fusion(bf16[512,1024]{1,0:T(8,128)(2,1)S(1)} %multiply_convert_fusion.3.refs_0_, bf16[1024,3072]{1,0:T(8,128)(2,1)} %place.11), kind=kOutput, calls=%fused_computation.213 | convolution fusion | flops 3221225472 | bytes 13631488 | tf_op jit(solution)/shard_map/dot_general | solution.py:692
  254.0 10.1 %multiply_convert_fusion.2 = (bf16[512,3072]{1,0:T(8,128)(2,1)}, f32[512,3072]{1,0:T(8,128)}) fusion(f32[512,3072]{1,0:T(8,128)} %fusion.42, bf16[512,1024]{1,0:T(8,128)(2,1)S(1)} %multiply_convert_fusion.3.refs_0_, bf16[1024,3072]{1,0:T(8,128)(2,1)} %place.12), kind=kOutput, calls=%fused_computation.6 | convolution fusion | flops 3230662656 | bytes 23068672 | tf_op jit(solution)/shard_map/dot_general | solution.py:692
  264.1 6.8 grads.6
  271.7 6.9 %collective-permute-done.34.refs_2_ = bf16[2,3,256,384]{3,2,1,0:T(8,128)(2,1)} collective-permute-done((bf16[2,3,256,384]{3,2,1,0:T(8,128)(2,1)}, bf16[2,3,256,384]{3,2,1,0:T(8,128)(2,1)}, u32[]{:S(2)}, u32[]{:S(2)}) %collective-permute-start.34) | collective-permute-done | bytes 1179680 | tf_op jit(solution)/shard_map/ppermute | solution.py:25
  280.3 6.5 place.13
  286.8 10.2 %multiply_convert_fusion = (bf16[512,3072]{1,0:T(8,128)(2,1)S(1)}, bf16[512,3072]{1,0:T(8,128)(2,1)S(1)}) fusion(f32[512,3072]{1,0:T(8,128)} %fusion.42, f32[512,3072]{1,0:T(8,128)} %get-tuple-element.335, bf16[512,1024]{1,0:T(8,128)(2,1)S(1)} %copy-done.2, bf16[3072,1024]{1,0:T(8,128)(2,1)} %place.13), kind=kOutput, calls=%fused_computation.4 | convolution fusion | flops 3241672704 | bytes 26214400 | tf_op jit(solution)/shard_map/dot_general | solution.py:450
  297.0 8.1 %grads.7 = bf16[4,1024,384]{2,1,0:T(8,128)(2,1)S(1)} custom-call(s32[4]{0:T(128)S(1)} %pad_add_fusion.2.at_ref, bf16[512,3072]{1,0:T(8,128)(2,1)} %get-tuple-element.334.refs_0_, bf16[512,1024]{1,0:T(8,128)(2,1)S(1)} %copy-done.2, bf16[512,1024]{1,0:T(8,128)(2,1)S(1)} %copy-done.2, bf16[4,1024,384]{2,1,0:T(8,128)(2,1)} %collective-permute-done.36.refs_3_), custom_call_target="tpu_custom_call" | custom-call | flops 1610612736 | bytes 12582912 | tf_op jit(solution)/shard_map/grads/pallas_call | solution.py:334
  305.2 6.3 fusion.43
  319.5 9.2 %grads.8 = (bf16[4,1024,384]{2,1,0:T(8,128)(2,1)}, bf16[4,1024,640]{2,1,0:T(8,128)(2,1)}) custom-call(s32[8]{0:T(128)S(1)} %stack.196.at_ref, bf16[512,1024]{1,0:T(8,128)(2,1)S(1)} %multiply_convert_fusion.3.refs_0_, bf16[512,2048]{1,0:T(8,128)(2,1)S(1)} %copy-done.4, bf16[512,3072]{1,0:T(8,128)(2,1)} %copy-done.23, bf16[512,3072]{1,0:T(8,128)(2,1)} %copy-done.23, ...), custom_call_target="tpu_custom_call" | custom-call | flops 4294967296 | bytes 33554432 | tf_op jit(solution)/shard_map/grads/pallas_call | solution.py:334
  328.7 20.9 %collective-permute-done.37 = bf16[2,1024,384]{2,1,0:T(8,128)(2,1)} collective-permute-done((bf16[2,1024,384]{2,1,0:T(8,128)(2,1)}, bf16[2,1024,384]{2,1,0:T(8,128)(2,1)}, u32[]{:S(2)}, u32[]{:S(2)}) %collective-permute-start.37) | collective-permute-done | bytes 1572896 | tf_op jit(solution)/shard_map/ppermute | solution.py:25
  354.6 6.1 convolution_convert_fusion.1.gatt_ref
  360.7 11.9 %collective-permute-done.40 = bf16[1,1024,384]{2,1,0:T(8,128)(2,1)} collective-permute-done((bf16[1,1024,384]{2,1,0:T(8,128)(2,1)S(1)}, bf16[1,1024,384]{2,1,0:T(8,128)(2,1)}, u32[]{:S(2)}, u32[]{:S(2)}) %collective-permute-start.40) | collective-permute-done | bytes 786464 | tf_op jit(solution)/shard_map/ppermute | solution.py:25
  372.6 11.0 %grads.9 = (bf16[4,1024,384]{2,1,0:T(8,128)(2,1)}, bf16[4,1024,640]{2,1,0:T(8,128)(2,1)}) custom-call(s32[8]{0:T(128)S(1)} %stack.192.at_ref, bf16[512,1024]{1,0:T(8,128)(2,1)S(1)} %multiply_convert_fusion.3.refs_0_, bf16[512,2048]{1,0:T(8,128)(2,1)S(1)} %copy-done.5, bf16[512,3072]{1,0:T(8,128)(2,1)} %copy-done.23, bf16[512,3072]{1,0:T(8,128)(2,1)} %copy-done.23, ...), custom_call_target="tpu_custom_call" | custom-call | flops 4294967296 | bytes 33554432 | tf_op jit(solution)/shard_map/grads/pallas_call | solution.py:334
  398.5 63.8 %attend_back.1 = (bf16[512,2048]{1,0:T(8,128)(2,1)S(1)}, bf16[1280,1024]{1,0:T(8,128)(2,1)}, bf16[1280,1024]{1,0:T(8,128)(2,1)}, f32[1,128]{1,0:T(1,128)S(1)}, f32[1,128]{1,0:T(1,128)S(1)}) custom-call(s32[3]{0:T(128)S(1)} %pad_add_fusion.1.sel_ref, f32[512,2048]{1,0:T(8,128)} %fusion.14.q_ref, f32[1280,1024]{1,0:T(8,128)} %fusion.41.k_ref, ...), custom_call_target="tpu_custom_call" | custom-call | flops 6710886400 | bytes 41943040 | tf_op jit(solution)/shard_map/attend_back/pallas_call | solution.py:654
  470.9 8.4 %grads.10 = (bf16[4,1024,256]{2,1,0:T(8,128)(2,1)S(1)}, bf16[4,1024,256]{2,1,0:T(8,128)(2,1)S(1)}) custom-call(s32[8]{0:T(128)S(1)} %stack.196.at_ref, bf16[1280,1024]{1,0:T(8,128)(2,1)} %copy-done.30, bf16[512,2048]{1,0:T(8,128)(2,1)} %copy-done, bf16[512,2048]{1,0:T(8,128)(2,1)} %copy-done, bf16[1280,1024]{1,0:T(8,128)(2,1)} %get-tuple-element.214.refs_3_.refs_4_, ...), custom_call_target="tpu_custom_call" | custom-call | flops 3758096384 | bytes 16777216 | tf_op jit(solution)/shard_map/grads/pallas_call | solution.py:334
  487.7 7.0 %collective-permute-done.47 = bf16[1,1024,640]{2,1,0:T(8,128)(2,1)} collective-permute-done((bf16[1,1024,640]{2,1,0:T(8,128)(2,1)S(1)}, bf16[1,1024,640]{2,1,0:T(8,128)(2,1)}, u32[]{:S(2)}, u32[]{:S(2)}) %collective-permute-start.47) | collective-permute-done | bytes 1310752 | tf_op jit(solution)/shard_map/ppermute | solution.py:25
  495.3 6.1 fusion.40
  507.0 9.4 %collective-permute-done.52 = bf16[256,1024]{1,0:T(8,128)(2,1)S(1)} collective-permute-done((bf16[256,1024]{1,0:T(8,128)(2,1)S(1)}, bf16[256,1024]{1,0:T(8,128)(2,1)S(1)}, u32[]{:S(2)}, u32[]{:S(2)}) %collective-permute-start.52) | collective-permute-done | bytes 524320 | tf_op jit(solution)/shard_map/ppermute | solution.py:30
  526.2 9.0 %grads.11 = (bf16[4,1024,256]{2,1,0:T(8,128)(2,1)S(1)}, bf16[4,1024,256]{2,1,0:T(8,128)(2,1)S(1)}) custom-call(s32[8]{0:T(128)S(1)} %stack.192.at_ref, bf16[1280,1024]{1,0:T(8,128)(2,1)} %copy-done.30, bf16[512,2048]{1,0:T(8,128)(2,1)} %copy-done, bf16[512,2048]{1,0:T(8,128)(2,1)} %copy-done, bf16[1280,1024]{1,0:T(8,128)(2,1)} %get-tuple-element.214.refs_3_.refs_4_, ...), custom_call_target="tpu_custom_call" | custom-call | flops 3758096384 | bytes 16777216 | tf_op jit(solution)/shard_map/grads/pallas_call | solution.py:334
  539.9 13.1 %collective-permute-done.53 = bf16[256,1024]{1,0:T(8,128)(2,1)} collective-permute-done((bf16[256,1024]{1,0:T(8,128)(2,1)}, bf16[256,1024]{1,0:T(8,128)(2,1)}, u32[]{:S(2)}, u32[]{:S(2)}) %collective-permute-start.53) | collective-permute-done | bytes 524320 | tf_op jit(solution)/shard_map/ppermute | solution.py:30
  555.9 33.5 %collective-permute-done.59 = bf16[256,1024]{1,0:T(8,128)(2,1)S(1)} collective-permute-done((bf16[256,1024]{1,0:T(8,128)(2,1)S(1)}, bf16[256,1024]{1,0:T(8,128)(2,1)S(1)}, u32[]{:S(2)}, u32[]{:S(2)}) %collective-permute-start.59) | collective-permute-done | bytes 524320 | tf_op jit(solution)/shard_map/ppermute | solution.py:30
  611.4 5.9 collective-permute-done.65
  624.1 8.7 %add_convert_fusion.6 = bf16[512,1024]{1,0:T(8,128)(2,1)} fusion(f32[512,1024]{1,0:T(8,128)} %copy-done.34, bf16[512,3072]{1,0:T(8,128)(2,1)} %get-tuple-element.334.refs_0_, bf16[3072,1024]{1,0:T(8,128)(2,1)} %place.13), kind=kOutput, calls=%fused_computation.48 | convolution fusion | flops 3222274048 | bytes 12582912 | tf_op jit(solution)/shard_map/dot_general | solution.py:692
  645.8 5.8 widen.2
  652.0 10.5 %collective-permute-done.69 = bf16[256,512]{1,0:T(8,128)(2,1)S(1)} collective-permute-done((bf16[256,512]{1,0:T(8,128)(2,1)S(1)}, bf16[256,512]{1,0:T(8,128)(2,1)S(1)}, u32[]{:S(2)}, u32[]{:S(2)}) %collective-permute-start.69) | collective-permute-done | bytes 262176 | tf_op jit(solution)/shard_map/ppermute | solution.py:30
  669.9 6.2 collective-permute-start.72
  (460 shorter events, 256.5 us)
Async XLA Ops:
  4.0 34.9 %collective-permute-start = (bf16[272,512]{1,0:T(8,128)(2,1)}, bf16[272,512]{1,0:T(8,128)(2,1)}, u32[]{:S(2)}, u32[]{:S(2)}) collective-permute-start(bf16[272,512]{1,0:T(8,128)(2,1)} %pad_maximum_fusion.18), channel_id=1, source_target_pairs={{0,1},{1,2},{2,3},{3,0},{4,5},{5,6},{6,7},{7,4},{8,9},{9,10},{10,1... | collective-permute-start | bytes 835592 | tf_op jit(solution)/shard_map/ppermute | solution.py:30
  7.1 32.8 %collective-permute-start.1 = (bf16[272,512]{1,0:T(8,128)(2,1)}, bf16[272,512]{1,0:T(8,128)(2,1)}, u32[]{:S(2)}, u32[]{:S(2)}) collective-permute-start(bf16[272,512]{1,0:T(8,128)(2,1)} %pad_maximum_fusion.18), channel_id=1, source_target_pairs={{0,2},{1,3},{2,0},{3,1},{4,6},{5,7},{6,4},{7,5},{8,10},{9,11},{10,... | collective-permute-start | bytes 835592 | tf_op jit(solution)/shard_map/ppermute | solution.py:30
  9.6 31.2 %collective-permute-start.2 = (bf16[272,512]{1,0:T(8,128)(2,1)}, bf16[272,512]{1,0:T(8,128)(2,1)}, u32[]{:S(2)}, u32[]{:S(2)}) collective-permute-start(bf16[272,512]{1,0:T(8,128)(2,1)} %pad_maximum_fusion.18), channel_id=1, source_target_pairs={{0,3},{1,0},{2,1},{3,2},{4,7},{5,4},{6,5},{7,6},{8,11},{9,8},{10,9... | collective-permute-start | bytes 835592 | tf_op jit(solution)/shard_map/ppermute | solution.py:30
  45.8 36.4 %collective-permute-start.4 = (bf16[256,1024]{1,0:T(8,128)(2,1)}, bf16[256,1024]{1,0:T(8,128)(2,1)}, u32[]{:S(2)}, u32[]{:S(2)}) collective-permute-start(bf16[256,1024]{1,0:T(8,128)(2,1)} %get-tuple-element.137), channel_id=1, source_target_pairs={{0,2},{1,3},{2,0},{3,1},{4,6},{5,7},{6,4},{7,5},{8,10},{9,11},{10,... | collective-permute-start | bytes 1572872 | tf_op jit(solution)/shard_map/ppermute | solution.py:30
  46.1 36.0 %collective-permute-start.5 = (bf16[256,1024]{1,0:T(8,128)(2,1)}, bf16[256,1024]{1,0:T(8,128)(2,1)}, u32[]{:S(2)}, u32[]{:S(2)}) collective-permute-start(bf16[256,1024]{1,0:T(8,128)(2,1)} %get-tuple-element.138), channel_id=1, source_target_pairs={{0,3},{1,0},{2,1},{3,2},{4,7},{5,4},{6,5},{7,6},{8,11},{9,8},{10,9... | collective-permute-start | bytes 1572872 | tf_op jit(solution)/shard_map/ppermute | solution.py:30
  52.1 32.1 %collective-permute-start.9 = (bf16[2,3,256,256]{3,2,1,0:T(8,128)(2,1)S(1)}, bf16[2,3,256,256]{3,2,1,0:T(8,128)(2,1)S(1)}, u32[]{:S(2)}, u32[]{:S(2)}) collective-permute-start(bf16[2,3,256,256]{3,2,1,0:T(8,128)(2,1)S(1)} %pad_maximum_fusion.7.refs_0_), channel_id=1, source_target_pairs={{0,8},{4,12},{8,0},{12,4},{16,24},{20,28},{24,16},{28,20},{1,9},{5... | collective-permute-start | bytes 2359304 | tf_op jit(solution)/shard_map/ppermute | solution.py:25
  53.9 30.3 %collective-permute-start.8 = (bf16[2,3,256,256]{3,2,1,0:T(8,128)(2,1)S(1)}, bf16[2,3,256,256]{3,2,1,0:T(8,128)(2,1)}, u32[]{:S(2)}, u32[]{:S(2)}) collective-permute-start(bf16[2,3,256,256]{3,2,1,0:T(8,128)(2,1)S(1)} %pad_maximum_fusion.6.refs_0_), channel_id=1, source_target_pairs={{0,16},{4,20},{8,24},{12,28},{16,0},{20,4},{24,8},{28,12},{1,17},{... | collective-permute-start | bytes 2359304 | tf_op jit(solution)/shard_map/ppermute | solution.py:25
  90.9 38.6 %collective-permute-start.14 = (bf16[256,640]{1,0:T(8,128)(2,1)S(1)}, bf16[256,640]{1,0:T(8,128)(2,1)S(1)}, u32[]{:S(2)}, u32[]{:S(2)}) collective-permute-start(bf16[256,640]{1,0:T(8,128)(2,1)S(1)} %copy-done.57), channel_id=1, source_target_pairs={{0,1},{1,2},{2,3},{3,0},{4,5},{5,6},{6,7},{7,4},{8,9},{9,10},{10,1... | collective-permute-start | bytes 983048 | tf_op jit(solution)/shard_map/ppermute | solution.py:30
  130.5 35.2 %collective-permute-start.18 = (bf16[1,3,256,256]{3,2,1,0:T(8,128)(2,1)}, bf16[1,3,256,256]{3,2,1,0:T(8,128)(2,1)}, u32[]{:S(2)}, u32[]{:S(2)}) collective-permute-start(bf16[1,3,256,256]{3,2,1,0:T(8,128)(2,1)} %maximum_bitcast_fusion.5), channel_id=1, source_target_pairs={{0,16},{4,20},{8,24},{12,28},{16,0},{20,4},{24,8},{28,12},{1,17},{... | collective-permute-start | bytes 1179656 | tf_op jit(solution)/shard_map/ppermute | solution.py:25
  131.1 36.4 %collective-permute-start.17 = (bf16[1,3,256,384]{3,2,1,0:T(8,128)(2,1)S(1)}, bf16[1,3,256,384]{3,2,1,0:T(8,128)(2,1)}, u32[]{:S(2)}, u32[]{:S(2)}) collective-permute-start(bf16[1,3,256,384]{3,2,1,0:T(8,128)(2,1)S(1)} %maximum_bitcast_fusion), channel_id=1, source_target_pairs={{0,8},{4,12},{8,0},{12,4},{16,24},{20,28},{24,16},{28,20},{1,9},{5... | collective-permute-start | bytes 1769480 | tf_op jit(solution)/shard_map/ppermute | solution.py:25
  132.5 36.2 %collective-permute-start.19 = (bf16[256,768]{1,0:T(8,128)(2,1)}, bf16[256,768]{1,0:T(8,128)(2,1)}, u32[]{:S(2)}, u32[]{:S(2)}) collective-permute-start(bf16[256,768]{1,0:T(8,128)(2,1)} %pad_maximum_fusion.15), channel_id=1, source_target_pairs={{0,1},{1,2},{2,3},{3,0},{4,5},{5,6},{6,7},{7,4},{8,9},{9,10},{10,1... | collective-permute-start | bytes 1179656 | tf_op jit(solution)/shard_map/ppermute | solution.py:30
  134.1 34.7 %collective-permute-start.20 = (bf16[256,768]{1,0:T(8,128)(2,1)}, bf16[256,768]{1,0:T(8,128)(2,1)}, u32[]{:S(2)}, u32[]{:S(2)}) collective-permute-start(bf16[256,768]{1,0:T(8,128)(2,1)} %pad_maximum_fusion.15), channel_id=1, source_target_pairs={{0,2},{1,3},{2,0},{3,1},{4,6},{5,7},{6,4},{7,5},{8,10},{9,11},{10,... | collective-permute-start | bytes 1179656 | tf_op jit(solution)/shard_map/ppermute | solution.py:30
  137.0 31.7 %collective-permute-start.21 = (bf16[256,768]{1,0:T(8,128)(2,1)}, bf16[256,768]{1,0:T(8,128)(2,1)}, u32[]{:S(2)}, u32[]{:S(2)}) collective-permute-start(bf16[256,768]{1,0:T(8,128)(2,1)} %pad_maximum_fusion.15), channel_id=1, source_target_pairs={{0,3},{1,0},{2,1},{3,2},{4,7},{5,4},{6,5},{7,6},{8,11},{9,8},{10,9... | collective-permute-start | bytes 1179656 | tf_op jit(solution)/shard_map/ppermute | solution.py:30
  169.8 39.0 %collective-permute-start.24 = (bf16[2,3,256,384]{3,2,1,0:T(8,128)(2,1)S(1)}, bf16[2,3,256,384]{3,2,1,0:T(8,128)(2,1)S(1)}, u32[]{:S(2)}, u32[]{:S(2)}) collective-permute-start(bf16[2,3,256,384]{3,2,1,0:T(8,128)(2,1)S(1)} %pad_maximum_fusion.3.refs_0_), channel_id=1, source_target_pairs={{0,16},{4,20},{8,24},{12,28},{16,0},{20,4},{24,8},{28,12},{1,17},{... | collective-permute-start | bytes 3538952 | tf_op jit(solution)/shard_map/ppermute | solution.py:25
  172.5 36.4 %collective-permute-start.25 = (bf16[2,3,256,256]{3,2,1,0:T(8,128)(2,1)S(1)}, bf16[2,3,256,256]{3,2,1,0:T(8,128)(2,1)S(1)}, u32[]{:S(2)}, u32[]{:S(2)}) collective-permute-start(bf16[2,3,256,256]{3,2,1,0:T(8,128)(2,1)S(1)} %pad_maximum_fusion.8.refs_0_), channel_id=1, source_target_pairs={{0,8},{4,12},{8,0},{12,4},{16,24},{20,28},{24,16},{28,20},{1,9},{5... | collective-permute-start | bytes 2359304 | tf_op jit(solution)/shard_map/ppermute | solution.py:25
  175.2 33.6 %collective-permute-start.23 = (bf16[1,3,256,384]{3,2,1,0:T(8,128)(2,1)S(1)}, bf16[1,3,256,384]{3,2,1,0:T(8,128)(2,1)S(1)}, u32[]{:S(2)}, u32[]{:S(2)}) collective-permute-start(bf16[1,3,256,384]{3,2,1,0:T(8,128)(2,1)S(1)} %maximum_bitcast_fusion.2), channel_id=1, source_target_pairs={{0,16},{4,20},{8,24},{12,28},{16,0},{20,4},{24,8},{28,12},{1,17},{... | collective-permute-start | bytes 1769480 | tf_op jit(solution)/shard_map/ppermute | solution.py:25
  175.9 33.0 %collective-permute-start.22 = (bf16[1,3,256,384]{3,2,1,0:T(8,128)(2,1)S(1)}, bf16[1,3,256,384]{3,2,1,0:T(8,128)(2,1)S(1)}, u32[]{:S(2)}, u32[]{:S(2)}) collective-permute-start(bf16[1,3,256,384]{3,2,1,0:T(8,128)(2,1)S(1)} %maximum_bitcast_fusion.1), channel_id=1, source_target_pairs={{0,8},{4,12},{8,0},{12,4},{16,24},{20,28},{24,16},{28,20},{1,9},{5... | collective-permute-start | bytes 1769480 | tf_op jit(solution)/shard_map/ppermute | solution.py:25
  312.8 36.7 %collective-permute-start.37 = (bf16[2,1024,384]{2,1,0:T(8,128)(2,1)}, bf16[2,1024,384]{2,1,0:T(8,128)(2,1)}, u32[]{:S(2)}, u32[]{:S(2)}) collective-permute-start(bf16[2,1024,384]{2,1,0:T(8,128)(2,1)} %slice.224), channel_id=1, source_target_pairs={{0,16},{4,20},{8,24},{12,28},{16,0},{20,4},{24,8},{28,12},{1,17},{... | collective-permute-start | bytes 4718600 | tf_op jit(solution)/shard_map/ppermute | solution.py:25
  387.2 75.2 %collective-permute-start.42 = (bf16[2,1024,640]{2,1,0:T(8,128)(2,1)}, bf16[2,1024,640]{2,1,0:T(8,128)(2,1)}, u32[]{:S(2)}, u32[]{:S(2)}) collective-permute-start(bf16[2,1024,640]{2,1,0:T(8,128)(2,1)} %slice.229), channel_id=1, source_target_pairs={{0,8},{4,12},{8,0},{12,4},{16,24},{20,28},{24,16},{28,20},{1,9},{5... | collective-permute-start | bytes 7864328 | tf_op jit(solution)/shard_map/ppermute | solution.py:25
  390.1 72.3 %collective-permute-start.41 = (bf16[2,1024,384]{2,1,0:T(8,128)(2,1)}, bf16[2,1024,384]{2,1,0:T(8,128)(2,1)}, u32[]{:S(2)}, u32[]{:S(2)}) collective-permute-start(bf16[2,1024,384]{2,1,0:T(8,128)(2,1)} %slice.228), channel_id=1, source_target_pairs={{0,16},{4,20},{8,24},{12,28},{16,0},{20,4},{24,8},{28,12},{1,17},{... | collective-permute-start | bytes 4718600 | tf_op jit(solution)/shard_map/ppermute | solution.py:25
  392.3 70.0 %collective-permute-start.43 = (bf16[256,384]{1,0:T(8,128)(2,1)S(1)}, bf16[256,384]{1,0:T(8,128)(2,1)S(1)}, u32[]{:S(2)}, u32[]{:S(2)}) collective-permute-start(bf16[256,384]{1,0:T(8,128)(2,1)S(1)} %get-tuple-element.287), channel_id=1, source_target_pairs={{0,1},{1,2},{2,3},{3,0},{4,5},{5,6},{6,7},{7,4},{8,9},{9,10},{10,1... | collective-permute-start | bytes 589832 | tf_op jit(solution)/shard_map/ppermute | solution.py:30
  396.1 66.3 %collective-permute-start.44 = (bf16[256,384]{1,0:T(8,128)(2,1)S(1)}, bf16[256,384]{1,0:T(8,128)(2,1)S(1)}, u32[]{:S(2)}, u32[]{:S(2)}) collective-permute-start(bf16[256,384]{1,0:T(8,128)(2,1)S(1)} %get-tuple-element.286), channel_id=1, source_target_pairs={{0,2},{1,3},{2,0},{3,1},{4,6},{5,7},{6,4},{7,5},{8,10},{9,11},{10,... | collective-permute-start | bytes 589832 | tf_op jit(solution)/shard_map/ppermute | solution.py:30
  396.1 66.3 %collective-permute-start.45 = (bf16[256,384]{1,0:T(8,128)(2,1)S(1)}, bf16[256,384]{1,0:T(8,128)(2,1)S(1)}, u32[]{:S(2)}, u32[]{:S(2)}) collective-permute-start(bf16[256,384]{1,0:T(8,128)(2,1)S(1)} %get-tuple-element.285), channel_id=1, source_target_pairs={{0,3},{1,0},{2,1},{3,2},{4,7},{5,4},{6,5},{7,6},{8,11},{9,8},{10,9... | collective-permute-start | bytes 589832 | tf_op jit(solution)/shard_map/ppermute | solution.py:30
  494.7 30.1 %collective-permute-start.48 = (bf16[4,1024,256]{2,1,0:T(8,128)(2,1)S(1)}, bf16[4,1024,256]{2,1,0:T(8,128)(2,1)S(1)}, u32[]{:S(2)}, u32[]{:S(2)}) collective-permute-start(bf16[4,1024,256]{2,1,0:T(8,128)(2,1)S(1)} %get-tuple-element.218), channel_id=1, source_target_pairs={{0,4},{4,0},{8,12},{12,8},{16,20},{20,16},{24,28},{28,24},{1,5},{5... | collective-permute-start | bytes 6291464 | tf_op jit(solution)/shard_map/ppermute | solution.py:25
  494.7 31.5 %collective-permute-start.49 = (bf16[4,1024,256]{2,1,0:T(8,128)(2,1)S(1)}, bf16[4,1024,256]{2,1,0:T(8,128)(2,1)}, u32[]{:S(2)}, u32[]{:S(2)}) collective-permute-start(bf16[4,1024,256]{2,1,0:T(8,128)(2,1)S(1)} %get-tuple-element.219), channel_id=1, source_target_pairs={{0,4},{4,0},{8,12},{12,8},{16,20},{20,16},{24,28},{28,24},{1,5},{5... | collective-permute-start | bytes 6291464 | tf_op jit(solution)/shard_map/ppermute | solution.py:25
  516.3 36.7 %collective-permute-start.53 = (bf16[256,1024]{1,0:T(8,128)(2,1)}, bf16[256,1024]{1,0:T(8,128)(2,1)}, u32[]{:S(2)}, u32[]{:S(2)}) collective-permute-start(bf16[256,1024]{1,0:T(8,128)(2,1)} %get-tuple-element.225), channel_id=1, source_target_pairs={{0,2},{1,3},{2,0},{3,1},{4,6},{5,7},{6,4},{7,5},{8,10},{9,11},{10,... | collective-permute-start | bytes 1572872 | tf_op jit(solution)/shard_map/ppermute | solution.py:30
  521.6 31.4 %collective-permute-start.58 = (bf16[256,1024]{1,0:T(8,128)(2,1)}, bf16[256,1024]{1,0:T(8,128)(2,1)S(1)}, u32[]{:S(2)}, u32[]{:S(2)}) collective-permute-start(bf16[256,1024]{1,0:T(8,128)(2,1)} %get-tuple-element.272), channel_id=1, source_target_pairs={{0,1},{1,2},{2,3},{3,0},{4,5},{5,6},{6,7},{7,4},{8,9},{9,10},{10,1... | collective-permute-start | bytes 1572872 | tf_op jit(solution)/shard_map/ppermute | solution.py:30
  535.3 54.4 %collective-permute-start.50 = (bf16[2,1024,256]{2,1,0:T(8,128)(2,1)S(1)}, bf16[2,1024,256]{2,1,0:T(8,128)(2,1)S(1)}, u32[]{:S(2)}, u32[]{:S(2)}) collective-permute-start(bf16[2,1024,256]{2,1,0:T(8,128)(2,1)S(1)} %slice.235), channel_id=1, source_target_pairs={{0,16},{4,20},{8,24},{12,28},{16,0},{20,4},{24,8},{28,12},{1,17},{... | collective-permute-start | bytes 3145736 | tf_op jit(solution)/shard_map/ppermute | solution.py:25
  537.0 52.7 %collective-permute-start.51 = (bf16[2,1024,256]{2,1,0:T(8,128)(2,1)S(1)}, bf16[2,1024,256]{2,1,0:T(8,128)(2,1)S(1)}, u32[]{:S(2)}, u32[]{:S(2)}) collective-permute-start(bf16[2,1024,256]{2,1,0:T(8,128)(2,1)S(1)} %slice.236), channel_id=1, source_target_pairs={{0,8},{4,12},{8,0},{12,4},{16,24},{20,28},{24,16},{28,20},{1,9},{5... | collective-permute-start | bytes 3145736 | tf_op jit(solution)/shard_map/ppermute | solution.py:25
  553.0 36.6 %collective-permute-start.54 = (bf16[256,1024]{1,0:T(8,128)(2,1)S(1)}, bf16[256,1024]{1,0:T(8,128)(2,1)S(1)}, u32[]{:S(2)}, u32[]{:S(2)}) collective-permute-start(bf16[256,1024]{1,0:T(8,128)(2,1)S(1)} %copy-done.55), channel_id=1, source_target_pairs={{0,1},{1,2},{2,3},{3,0},{4,5},{5,6},{6,7},{7,4},{8,9},{9,10},{10,1... | collective-permute-start | bytes 1572872 | tf_op jit(solution)/shard_map/ppermute | solution.py:30
  553.1 36.4 %collective-permute-start.59 = (bf16[256,1024]{1,0:T(8,128)(2,1)S(1)}, bf16[256,1024]{1,0:T(8,128)(2,1)S(1)}, u32[]{:S(2)}, u32[]{:S(2)}) collective-permute-start(bf16[256,1024]{1,0:T(8,128)(2,1)S(1)} %copy-done.56), channel_id=1, source_target_pairs={{0,2},{1,3},{2,0},{3,1},{4,6},{5,7},{6,4},{7,5},{8,10},{9,11},{10,... | collective-permute-start | bytes 1572872 | tf_op jit(solution)/shard_map/ppermute | solution.py:30
  555.8 33.8 %collective-permute-start.55 = (f32[18,128]{1,0:T(8,128)S(1)}, f32[18,128]{1,0:T(8,128)S(1)}, u32[]{:S(2)}, u32[]{:S(2)}) collective-permute-start(f32[18,128]{1,0:T(8,128)S(1)} %maximum_bitcast_fusion.6), channel_id=1, source_target_pairs={{0,4},{4,0},{8,12},{12,8},{16,20},{20,16},{24,28},{28,24},{1,5},{5... | collective-permute-start | bytes 27656 | tf_op jit(solution)/shard_map/ppermute | solution.py:25
  (120 other events, 1651.0 us)

commit v3 on v2

--- a/solution.py
+++ b/solution.py
@@ -898,16 +898,14 @@
     if bundled:
         mlp_pairs = [[(mixed, grad_gate)], [(mixed, grad_upward), (attended, grad_branch)]]
         theirs = grads(mlp_pairs, unit, False)
-        theirs, down_first, branch = barrier((theirs, down_first, grad_branch))
+        theirs, branch = barrier((theirs, grad_branch))
         mlp_core = swap_cores(theirs)
+        grad_attended = dot_nt(branch, full_out).astype(BF16)
+        mlp_core, grad_attended = barrier((mlp_core, grad_attended))
+        mlp_sum = grads(mlp_pairs, unit, True, mlp_core)
+        mlp_sum, down_first, grad_attended = barrier((mlp_sum, down_first, grad_attended))
         down_sum = fold(down_sum, down_first)
         down_second = fold_swap(fold_sent(down_sum), 1)
-        grad_attended = dot_nt(branch, full_out).astype(BF16)
-        mlp_core, down_second, grad_attended = barrier((mlp_core, down_second, grad_attended))
-        down_sum = fold(down_sum, down_second)
-        down_mine, down_z = z_send(down_sum)
-        mlp_sum = grads(mlp_pairs, unit, True, mlp_core)
-        mlp_sum, grad_attended = barrier((mlp_sum, grad_attended))
         mlp_first = fold_swap(fold_sent(mlp_sum), 0)
     else:
         grad_attended = dot_nt(grad_branch, full_out).astype(BF16)
@@ -919,7 +917,9 @@
         sel, count, total, operands + (attended, grad_attended)
     )
     if bundled:
-        mlp_first, down_z, dq, dk, dv = barrier((mlp_first, down_z, dq, dk, dv))
+        mlp_first, down_second, dq, dk, dv = barrier((mlp_first, down_second, dq, dk, dv))
+        down_sum = fold(down_sum, down_second)
+        down_mine, down_z = z_send(down_sum, True)
         mlp_sum = fold(mlp_sum, mlp_first)
         mlp_second = fold_swap(fold_sent(mlp_sum), 1)
         attn_pairs = [[(normed, dq)], [(normed, dk), (normed, dv)]]
@@ -931,7 +931,6 @@
     ]
     if bundled:
         mlp_second, theirs = barrier((mlp_second, theirs))
-        down_sum = z_sum(down_mine, down_z, down_sum)
         attn_core = swap_cores(theirs)
         mlp_sum = fold(mlp_sum, mlp_second)
     back = []
@@ -949,7 +948,8 @@
         attn_sum = grads(attn_pairs, unit, True, attn_core)
         attn_first = fold_swap(fold_sent(attn_sum), 0)
         gain_other = dp_swap(gain_sum, 0)
-        attn_first, back, gain_other = barrier((attn_first, back, gain_other))
+        attn_first, back, gain_other, down_z = barrier((attn_first, back, gain_other, down_z))
+        down_sum = z_sum(down_mine, down_z, down_sum)
         gain_sum = gain_sum + gain_other
         attn_sum = fold(attn_sum, attn_first)
         attn_second = fold_swap(fold_sent(attn_sum), 1)
@@ -967,11 +967,9 @@
             return [(x, dp_swap(x, 0)) for x in streams]
 
         mlp_sum = [jnp.concatenate([down_sum[0], mlp_sum[0]], axis=2), mlp_sum[1]]
+        mlp_whole, attn_z = barrier((whole(mlp_sum), attn_z))
         grad_w_down, grad_w_gate, grad_w_up, grad_w_out = widen_units(
-            whole(mlp_sum), unit, [(w_down, 0), (w_gate, 0), (w_up, 1), (w_out, 1)]
-        )
-        attn_z, gain_sum = after(
-            (grad_w_down, grad_w_gate, grad_w_up, grad_w_out, gain_sum), (attn_z, gain_sum)
+            mlp_whole, unit, [(w_down, 0), (w_gate, 0), (w_up, 1), (w_out, 1)]
         )
         gain_sum = sum([z_shift(gain_sum, k) for k in range(1, shards)], gain_sum)
         attn_sum = z_sum(attn_mine, attn_z, attn_sum)

time: 696 us -> 710 us (1.020)
  starting transfers between devices: 94.3 us -> 104 us
    ppermute x27, starting transfers between devices: 54.3 us -> 64.3 us  [z_shift(): lax.ppermute(x, 'shard', [(i, (i + step) % count) for i in range(count)])]
    ppermute x27, waiting for transfers between devices: 98.8 us -> 108 us  [z_shift(): lax.ppermute(x, 'shard', [(i, (i + step) % count) for i in range(count)])]
  transfers between devices with their start and end apart: 81 -> 81, of which waited for: 27 -> 31; matrix products, arithmetic and copies ran while one was open for 20% -> 19% of each run, Pallas kernels for 21% -> 21%
where the time goes in v3:
time: 710 us; the launch traced here: 701 us
  waiting for transfers between devices  217 us (31%)
  Pallas kernels  181 us (25%)
  starting transfers between devices  104 us (15%)
  matrix products  87.8 us (12%)
  other arithmetic  53.3 us (8%)
  local copies, waits for them, and re-layouts  41.5 us (6%)
  between operations  16 us (2%)
    ppermute x54, waiting for transfers between devices, dp_swap(): return lax.ppermute(x, 'dp', [(i, i ^ 1 << bit) for i in range(count)])  109 us
    ppermute x27, waiting for transfers between devices, z_shift(): lax.ppermute(x, 'shard', [(i, (i + step) % count) for i in range(count)])  108 us
    ppermute x27, starting transfers between devices, z_shift(): lax.ppermute(x, 'shard', [(i, (i + step) % count) for i in range(count)])  64.3 us
    pallas_call x1, Pallas kernels, attend_back(): pl.pallas_call(attend_back_kernel, out_shape=(jax.ShapeDtypeStruct((count...  63.8 us
    pallas_call x6, Pallas kernels, grads(): pl.pallas_call(functools.partial(grads_kernel, units, items, counts), out...  51.8 us
    dot_general x7, matrix products, matmul(): return jnp.dot(a, b, preferred_element_type=F32)  47 us
    dot_general x7, matrix products, dot_nt(): lax.dot_general(a, b, (((1,), (1,)), ((), ())), preferred_element_type=F32)  40.8 us
    ppermute x54, starting transfers between devices, dp_swap(): return lax.ppermute(x, 'dp', [(i, i ^ 1 << bit) for i in range(count)])  39.9 us
  transfers between devices with their start and end apart: 81, of which 31 were waited for; matrix products, arithmetic and copies ran while one was open for 19% of the time, Pallas kernels for 21%

profile of v3, /device:TPU:0, one launch (start us, length us, event | category | flops | bytes accessed | tf_op | source)
XLA Modules:
  0.0 700.6 jit_solution(16858687064933880578)
XLA Ops:
  55.7 6.5 collective-permute-done.3
  62.2 20.0 %collective-permute-done.4 = bf16[256,1024]{1,0:T(8,128)(2,1)} collective-permute-done((bf16[256,1024]{1,0:T(8,128)(2,1)}, bf16[256,1024]{1,0:T(8,128)(2,1)}, u32[]{:S(2)}, u32[]{:S(2)}) %collective-permute-start.4) | collective-permute-done | bytes 524320 | tf_op jit(solution)/shard_map/ppermute | solution.py:30
  90.9 11.2 %collective-permute-start.14 = (bf16[256,640]{1,0:T(8,128)(2,1)S(1)}, bf16[256,640]{1,0:T(8,128)(2,1)S(1)}, u32[]{:S(2)}, u32[]{:S(2)}) collective-permute-start(bf16[256,640]{1,0:T(8,128)(2,1)S(1)} %copy-done.60), channel_id=1, source_target_pairs={{0,1},{1,2},{2,3},{3,0},{4,5},{5,6},{6,7},{7,4},{8,9},{9,10},{10,1... | collective-permute-start | bytes 983048 | tf_op jit(solution)/shard_map/ppermute | solution.py:30
  123.2 6.6 fusion.14.q_ref
  137.5 27.9 %attend.1.refs_1_.att_ref = bf16[512,2048]{1,0:T(8,128)(2,1)S(1)} custom-call(s32[3]{0:T(128)S(1)} %pad_add_fusion.1.sel_ref, f32[512,2048]{1,0:T(8,128)} %fusion.14.q_ref, f32[1280,1024]{1,0:T(8,128)} %fusion.41.k_ref, bf16[1280,1024]{1,0:T(8,128)(2,1)} %convolution_convert_fusion.v_ref, f32[1280,128]{1,0:T(8,128)S(1)} %get-tuple-element.156.cos_ref, ...), custom_call_target="tpu_custom_call" | custom-call | flops 2684354560 | bytes 41943040 | tf_op jit(solution)/shard_map/attend/pallas_call | solution.py:630
  176.2 32.4 %collective-permute-done.23 = bf16[1,3,256,384]{3,2,1,0:T(8,128)(2,1)S(1)} collective-permute-done((bf16[1,3,256,384]{3,2,1,0:T(8,128)(2,1)S(1)}, bf16[1,3,256,384]{3,2,1,0:T(8,128)(2,1)S(1)}, u32[]{:S(2)}, u32[]{:S(2)}) %collective-permute-start.23) | collective-permute-done | bytes 589856 | tf_op jit(solution)/shard_map/ppermute | solution.py:25
  232.6 8.2 %fusion.42 = f32[512,3072]{1,0:T(8,128)} fusion(bf16[512,1024]{1,0:T(8,128)(2,1)S(1)} %multiply_convert_fusion.3.refs_0_, bf16[1024,3072]{1,0:T(8,128)(2,1)} %place.11), kind=kOutput, calls=%fused_computation.213 | convolution fusion | flops 3221225472 | bytes 13631488 | tf_op jit(solution)/shard_map/dot_general | solution.py:692
  253.8 10.1 %multiply_convert_fusion.2 = (bf16[512,3072]{1,0:T(8,128)(2,1)}, f32[512,3072]{1,0:T(8,128)}) fusion(f32[512,3072]{1,0:T(8,128)} %fusion.42, bf16[512,1024]{1,0:T(8,128)(2,1)S(1)} %multiply_convert_fusion.3.refs_0_, bf16[1024,3072]{1,0:T(8,128)(2,1)} %place.12), kind=kOutput, calls=%fused_computation.6 | convolution fusion | flops 3230662656 | bytes 23068672 | tf_op jit(solution)/shard_map/dot_general | solution.py:692
  263.9 6.8 grads.6
  271.5 6.9 collective-permute-done.34.refs_2_
  280.1 6.5 place.13
  286.6 10.2 %multiply_convert_fusion = (bf16[512,3072]{1,0:T(8,128)(2,1)S(1)}, bf16[512,3072]{1,0:T(8,128)(2,1)S(1)}) fusion(f32[512,3072]{1,0:T(8,128)} %fusion.42, f32[512,3072]{1,0:T(8,128)} %get-tuple-element.345, bf16[512,1024]{1,0:T(8,128)(2,1)S(1)} %copy-done.2, bf16[3072,1024]{1,0:T(8,128)(2,1)} %place.13), kind=kOutput, calls=%fused_computation.4 | convolution fusion | flops 3241672704 | bytes 26214400 | tf_op jit(solution)/shard_map/dot_general | solution.py:450
  296.9 8.1 %grads.7 = bf16[4,1024,384]{2,1,0:T(8,128)(2,1)S(1)} custom-call(s32[4]{0:T(128)S(1)} %pad_add_fusion.2.at_ref, bf16[512,3072]{1,0:T(8,128)(2,1)} %get-tuple-element.344.refs_0_, bf16[512,1024]{1,0:T(8,128)(2,1)S(1)} %copy-done.2, bf16[512,1024]{1,0:T(8,128)(2,1)S(1)} %copy-done.2, bf16[4,1024,384]{2,1,0:T(8,128)(2,1)} %collective-permute-done.36.refs_3_), custom_call_target="tpu_custom_call" | custom-call | flops 1610612736 | bytes 12582912 | tf_op jit(solution)/shard_map/grads/pallas_call | solution.py:334
  305.0 7.5 %fusion.43 = f32[512,1024]{1,0:T(8,128)S(1)} fusion(bf16[512,3072]{1,0:T(8,128)(2,1)S(1)} %get-tuple-element.196.refs_4_.refs_5_, bf16[1024,3072]{1,0:T(8,128)(2,1)} %place.12), kind=kOutput, calls=%fused_computation.214 | convolution fusion | flops 3221225472 | bytes 11534336 | tf_op jit(solution)/shard_map/dot_general | solution.py:450
  318.4 9.2 %grads.8 = (bf16[4,1024,384]{2,1,0:T(8,128)(2,1)}, bf16[4,1024,640]{2,1,0:T(8,128)(2,1)}) custom-call(s32[8]{0:T(128)S(1)} %stack.196.at_ref, bf16[512,1024]{1,0:T(8,128)(2,1)S(1)} %multiply_convert_fusion.3.refs_0_, bf16[512,2048]{1,0:T(8,128)(2,1)S(1)} %copy-done.4, bf16[512,3072]{1,0:T(8,128)(2,1)} %copy-done.25, bf16[512,3072]{1,0:T(8,128)(2,1)} %copy-done.25, ...), custom_call_target="tpu_custom_call" | custom-call | flops 4294967296 | bytes 33554432 | tf_op jit(solution)/shard_map/grads/pallas_call | solution.py:334
  330.0 6.1 convolution_convert_fusion.1.gatt_ref
  341.1 10.7 %grads.9 = (bf16[4,1024,384]{2,1,0:T(8,128)(2,1)}, bf16[4,1024,640]{2,1,0:T(8,128)(2,1)}) custom-call(s32[8]{0:T(128)S(1)} %stack.192.at_ref, bf16[512,1024]{1,0:T(8,128)(2,1)S(1)} %multiply_convert_fusion.3.refs_0_, bf16[512,2048]{1,0:T(8,128)(2,1)S(1)} %copy-done.5, bf16[512,3072]{1,0:T(8,128)(2,1)} %copy-done.25, bf16[512,3072]{1,0:T(8,128)(2,1)} %copy-done.25, ...), custom_call_target="tpu_custom_call" | custom-call | flops 4294967296 | bytes 33554432 | tf_op jit(solution)/shard_map/grads/pallas_call | solution.py:334
  351.8 14.4 %collective-permute-done.39 = bf16[2,1024,384]{2,1,0:T(8,128)(2,1)} collective-permute-done((bf16[2,1024,384]{2,1,0:T(8,128)(2,1)}, bf16[2,1024,384]{2,1,0:T(8,128)(2,1)}, u32[]{:S(2)}, u32[]{:S(2)}) %collective-permute-start.39) | collective-permute-done | bytes 1572896 | tf_op jit(solution)/shard_map/ppermute | solution.py:25
  377.7 63.8 %attend_back.1 = (bf16[512,2048]{1,0:T(8,128)(2,1)S(1)}, bf16[1280,1024]{1,0:T(8,128)(2,1)}, bf16[1280,1024]{1,0:T(8,128)(2,1)}, f32[1,128]{1,0:T(1,128)S(1)}, f32[1,128]{1,0:T(1,128)S(1)}) custom-call(s32[3]{0:T(128)S(1)} %pad_add_fusion.1.sel_ref, f32[512,2048]{1,0:T(8,128)} %fusion.14.q_ref, f32[1280,1024]{1,0:T(8,128)} %fusion.41.k_ref, ...), custom_call_target="tpu_custom_call" | custom-call | flops 6710886400 | bytes 41943040 | tf_op jit(solution)/shard_map/attend_back/pallas_call | solution.py:654
  453.6 8.1 %grads.10 = (bf16[4,1024,256]{2,1,0:T(8,128)(2,1)S(1)}, bf16[4,1024,256]{2,1,0:T(8,128)(2,1)S(1)}) custom-call(s32[8]{0:T(128)S(1)} %stack.196.at_ref, bf16[1280,1024]{1,0:T(8,128)(2,1)} %copy-done.32, bf16[512,2048]{1,0:T(8,128)(2,1)} %copy-done, bf16[512,2048]{1,0:T(8,128)(2,1)} %copy-done, bf16[1280,1024]{1,0:T(8,128)(2,1)} %get-tuple-element.218.refs_3_.refs_4_, ...), custom_call_target="tpu_custom_call" | custom-call | flops 3758096384 | bytes 16777216 | tf_op jit(solution)/shard_map/grads/pallas_call | solution.py:334
  469.8 8.0 %collective-permute-done.44 = bf16[1,1024,640]{2,1,0:T(8,128)(2,1)} collective-permute-done((bf16[1,1024,640]{2,1,0:T(8,128)(2,1)S(1)}, bf16[1,1024,640]{2,1,0:T(8,128)(2,1)}, u32[]{:S(2)}, u32[]{:S(2)}) %collective-permute-start.44) | collective-permute-done | bytes 1310752 | tf_op jit(solution)/shard_map/ppermute | solution.py:25
  478.3 6.0 fusion.40
  491.8 9.6 %collective-permute-done.49 = bf16[256,1024]{1,0:T(8,128)(2,1)S(1)} collective-permute-done((bf16[256,1024]{1,0:T(8,128)(2,1)S(1)}, bf16[256,1024]{1,0:T(8,128)(2,1)S(1)}, u32[]{:S(2)}, u32[]{:S(2)}) %collective-permute-start.49) | collective-permute-done | bytes 524320 | tf_op jit(solution)/shard_map/ppermute | solution.py:30
  509.9 9.0 %grads.11 = (bf16[4,1024,256]{2,1,0:T(8,128)(2,1)S(1)}, bf16[4,1024,256]{2,1,0:T(8,128)(2,1)S(1)}) custom-call(s32[8]{0:T(128)S(1)} %stack.192.at_ref, bf16[1280,1024]{1,0:T(8,128)(2,1)} %copy-done.32, bf16[512,2048]{1,0:T(8,128)(2,1)} %copy-done, bf16[512,2048]{1,0:T(8,128)(2,1)} %copy-done, bf16[1280,1024]{1,0:T(8,128)(2,1)} %get-tuple-element.218.refs_3_.refs_4_, ...), custom_call_target="tpu_custom_call" | custom-call | flops 3758096384 | bytes 16777216 | tf_op jit(solution)/shard_map/grads/pallas_call | solution.py:334
  522.0 10.2 %collective-permute-done.53 = bf16[256,384]{1,0:T(8,128)(2,1)S(1)} collective-permute-done((bf16[256,384]{1,0:T(8,128)(2,1)S(1)}, bf16[256,384]{1,0:T(8,128)(2,1)S(1)}, u32[]{:S(2)}, u32[]{:S(2)}) %collective-permute-start.53) | collective-permute-done | bytes 196640 | tf_op jit(solution)/shard_map/ppermute | solution.py:30
  532.3 10.8 %collective-permute-start.54 = (bf16[256,384]{1,0:T(8,128)(2,1)S(1)}, bf16[256,384]{1,0:T(8,128)(2,1)S(1)}, u32[]{:S(2)}, u32[]{:S(2)}) collective-permute-start(bf16[256,384]{1,0:T(8,128)(2,1)S(1)} %get-tuple-element.234), channel_id=1, source_target_pairs={{0,2},{1,3},{2,0},{3,1},{4,6},{5,7},{6,4},{7,5},{8,10},{9,11},{10,... | collective-permute-start | bytes 589832 | tf_op jit(solution)/shard_map/ppermute | solution.py:30
  545.3 7.0 %collective-permute-done.54 = bf16[256,384]{1,0:T(8,128)(2,1)S(1)} collective-permute-done((bf16[256,384]{1,0:T(8,128)(2,1)S(1)}, bf16[256,384]{1,0:T(8,128)(2,1)S(1)}, u32[]{:S(2)}, u32[]{:S(2)}) %collective-permute-start.54) | collective-permute-done | bytes 196640 | tf_op jit(solution)/shard_map/ppermute | solution.py:30
  556.6 34.2 %collective-permute-done.59 = bf16[256,1024]{1,0:T(8,128)(2,1)S(1)} collective-permute-done((bf16[256,1024]{1,0:T(8,128)(2,1)S(1)}, bf16[256,1024]{1,0:T(8,128)(2,1)S(1)}, u32[]{:S(2)}, u32[]{:S(2)}) %collective-permute-start.59) | collective-permute-done | bytes 524320 | tf_op jit(solution)/shard_map/ppermute | solution.py:30
  608.1 6.7 collective-permute-done.61
  630.7 8.7 %add_convert_fusion.6 = bf16[512,1024]{1,0:T(8,128)(2,1)} fusion(f32[512,1024]{1,0:T(8,128)} %copy-done.36, bf16[512,3072]{1,0:T(8,128)(2,1)} %get-tuple-element.344.refs_0_, bf16[3072,1024]{1,0:T(8,128)(2,1)} %place.13), kind=kOutput, calls=%fused_computation.48 | convolution fusion | flops 3222274048 | bytes 12582912 | tf_op jit(solution)/shard_map/dot_general | solution.py:692
  653.9 6.2 collective-permute-done.72
  660.1 10.3 %collective-permute-done.73 = bf16[256,512]{1,0:T(8,128)(2,1)S(1)} collective-permute-done((bf16[256,512]{1,0:T(8,128)(2,1)S(1)}, bf16[256,512]{1,0:T(8,128)(2,1)S(1)}, u32[]{:S(2)}, u32[]{:S(2)}) %collective-permute-start.73) | collective-permute-done | bytes 262176 | tf_op jit(solution)/shard_map/ppermute | solution.py:30
  (459 shorter events, 276.8 us)
Async XLA Ops:
  4.0 34.9 %collective-permute-start = (bf16[272,512]{1,0:T(8,128)(2,1)}, bf16[272,512]{1,0:T(8,128)(2,1)}, u32[]{:S(2)}, u32[]{:S(2)}) collective-permute-start(bf16[272,512]{1,0:T(8,128)(2,1)} %pad_maximum_fusion.18), channel_id=1, source_target_pairs={{0,1},{1,2},{2,3},{3,0},{4,5},{5,6},{6,7},{7,4},{8,9},{9,10},{10,1... | collective-permute-start | bytes 835592 | tf_op jit(solution)/shard_map/ppermute | solution.py:30
  7.1 32.8 %collective-permute-start.1 = (bf16[272,512]{1,0:T(8,128)(2,1)}, bf16[272,512]{1,0:T(8,128)(2,1)}, u32[]{:S(2)}, u32[]{:S(2)}) collective-permute-start(bf16[272,512]{1,0:T(8,128)(2,1)} %pad_maximum_fusion.18), channel_id=1, source_target_pairs={{0,2},{1,3},{2,0},{3,1},{4,6},{5,7},{6,4},{7,5},{8,10},{9,11},{10,... | collective-permute-start | bytes 835592 | tf_op jit(solution)/shard_map/ppermute | solution.py:30
  9.6 31.2 %collective-permute-start.2 = (bf16[272,512]{1,0:T(8,128)(2,1)}, bf16[272,512]{1,0:T(8,128)(2,1)}, u32[]{:S(2)}, u32[]{:S(2)}) collective-permute-start(bf16[272,512]{1,0:T(8,128)(2,1)} %pad_maximum_fusion.18), channel_id=1, source_target_pairs={{0,3},{1,0},{2,1},{3,2},{4,7},{5,4},{6,5},{7,6},{8,11},{9,8},{10,9... | collective-permute-start | bytes 835592 | tf_op jit(solution)/shard_map/ppermute | solution.py:30
  45.8 36.4 %collective-permute-start.4 = (bf16[256,1024]{1,0:T(8,128)(2,1)}, bf16[256,1024]{1,0:T(8,128)(2,1)}, u32[]{:S(2)}, u32[]{:S(2)}) collective-permute-start(bf16[256,1024]{1,0:T(8,128)(2,1)} %get-tuple-element.142), channel_id=1, source_target_pairs={{0,2},{1,3},{2,0},{3,1},{4,6},{5,7},{6,4},{7,5},{8,10},{9,11},{10,... | collective-permute-start | bytes 1572872 | tf_op jit(solution)/shard_map/ppermute | solution.py:30
  46.1 36.0 %collective-permute-start.5 = (bf16[256,1024]{1,0:T(8,128)(2,1)}, bf16[256,1024]{1,0:T(8,128)(2,1)}, u32[]{:S(2)}, u32[]{:S(2)}) collective-permute-start(bf16[256,1024]{1,0:T(8,128)(2,1)} %get-tuple-element.143), channel_id=1, source_target_pairs={{0,3},{1,0},{2,1},{3,2},{4,7},{5,4},{6,5},{7,6},{8,11},{9,8},{10,9... | collective-permute-start | bytes 1572872 | tf_op jit(solution)/shard_map/ppermute | solution.py:30
  52.1 32.1 %collective-permute-start.9 = (bf16[2,3,256,256]{3,2,1,0:T(8,128)(2,1)S(1)}, bf16[2,3,256,256]{3,2,1,0:T(8,128)(2,1)S(1)}, u32[]{:S(2)}, u32[]{:S(2)}) collective-permute-start(bf16[2,3,256,256]{3,2,1,0:T(8,128)(2,1)S(1)} %pad_maximum_fusion.7.refs_0_), channel_id=1, source_target_pairs={{0,8},{4,12},{8,0},{12,4},{16,24},{20,28},{24,16},{28,20},{1,9},{5... | collective-permute-start | bytes 2359304 | tf_op jit(solution)/shard_map/ppermute | solution.py:25
  53.9 30.3 %collective-permute-start.8 = (bf16[2,3,256,256]{3,2,1,0:T(8,128)(2,1)S(1)}, bf16[2,3,256,256]{3,2,1,0:T(8,128)(2,1)}, u32[]{:S(2)}, u32[]{:S(2)}) collective-permute-start(bf16[2,3,256,256]{3,2,1,0:T(8,128)(2,1)S(1)} %pad_maximum_fusion.6.refs_0_), channel_id=1, source_target_pairs={{0,16},{4,20},{8,24},{12,28},{16,0},{20,4},{24,8},{28,12},{1,17},{... | collective-permute-start | bytes 2359304 | tf_op jit(solution)/shard_map/ppermute | solution.py:25
  90.9 38.9 %collective-permute-start.14 = (bf16[256,640]{1,0:T(8,128)(2,1)S(1)}, bf16[256,640]{1,0:T(8,128)(2,1)S(1)}, u32[]{:S(2)}, u32[]{:S(2)}) collective-permute-start(bf16[256,640]{1,0:T(8,128)(2,1)S(1)} %copy-done.60), channel_id=1, source_target_pairs={{0,1},{1,2},{2,3},{3,0},{4,5},{5,6},{6,7},{7,4},{8,9},{9,10},{10,1... | collective-permute-start | bytes 983048 | tf_op jit(solution)/shard_map/ppermute | solution.py:30
  130.7 34.8 %collective-permute-start.18 = (bf16[1,3,256,256]{3,2,1,0:T(8,128)(2,1)}, bf16[1,3,256,256]{3,2,1,0:T(8,128)(2,1)}, u32[]{:S(2)}, u32[]{:S(2)}) collective-permute-start(bf16[1,3,256,256]{3,2,1,0:T(8,128)(2,1)} %maximum_bitcast_fusion.5), channel_id=1, source_target_pairs={{0,16},{4,20},{8,24},{12,28},{16,0},{20,4},{24,8},{28,12},{1,17},{... | collective-permute-start | bytes 1179656 | tf_op jit(solution)/shard_map/ppermute | solution.py:25
  131.3 36.0 %collective-permute-start.17 = (bf16[1,3,256,384]{3,2,1,0:T(8,128)(2,1)S(1)}, bf16[1,3,256,384]{3,2,1,0:T(8,128)(2,1)}, u32[]{:S(2)}, u32[]{:S(2)}) collective-permute-start(bf16[1,3,256,384]{3,2,1,0:T(8,128)(2,1)S(1)} %maximum_bitcast_fusion), channel_id=1, source_target_pairs={{0,8},{4,12},{8,0},{12,4},{16,24},{20,28},{24,16},{28,20},{1,9},{5... | collective-permute-start | bytes 1769480 | tf_op jit(solution)/shard_map/ppermute | solution.py:25
  132.8 35.7 %collective-permute-start.19 = (bf16[256,768]{1,0:T(8,128)(2,1)}, bf16[256,768]{1,0:T(8,128)(2,1)}, u32[]{:S(2)}, u32[]{:S(2)}) collective-permute-start(bf16[256,768]{1,0:T(8,128)(2,1)} %pad_maximum_fusion.15), channel_id=1, source_target_pairs={{0,1},{1,2},{2,3},{3,0},{4,5},{5,6},{6,7},{7,4},{8,9},{9,10},{10,1... | collective-permute-start | bytes 1179656 | tf_op jit(solution)/shard_map/ppermute | solution.py:30
  134.1 34.4 %collective-permute-start.20 = (bf16[256,768]{1,0:T(8,128)(2,1)}, bf16[256,768]{1,0:T(8,128)(2,1)}, u32[]{:S(2)}, u32[]{:S(2)}) collective-permute-start(bf16[256,768]{1,0:T(8,128)(2,1)} %pad_maximum_fusion.15), channel_id=1, source_target_pairs={{0,2},{1,3},{2,0},{3,1},{4,6},{5,7},{6,4},{7,5},{8,10},{9,11},{10,... | collective-permute-start | bytes 1179656 | tf_op jit(solution)/shard_map/ppermute | solution.py:30
  137.0 31.5 %collective-permute-start.21 = (bf16[256,768]{1,0:T(8,128)(2,1)}, bf16[256,768]{1,0:T(8,128)(2,1)}, u32[]{:S(2)}, u32[]{:S(2)}) collective-permute-start(bf16[256,768]{1,0:T(8,128)(2,1)} %pad_maximum_fusion.15), channel_id=1, source_target_pairs={{0,3},{1,0},{2,1},{3,2},{4,7},{5,4},{6,5},{7,6},{8,11},{9,8},{10,9... | collective-permute-start | bytes 1179656 | tf_op jit(solution)/shard_map/ppermute | solution.py:30
  169.6 39.0 %collective-permute-start.24 = (bf16[2,3,256,384]{3,2,1,0:T(8,128)(2,1)S(1)}, bf16[2,3,256,384]{3,2,1,0:T(8,128)(2,1)S(1)}, u32[]{:S(2)}, u32[]{:S(2)}) collective-permute-start(bf16[2,3,256,384]{3,2,1,0:T(8,128)(2,1)S(1)} %pad_maximum_fusion.3.refs_0_), channel_id=1, source_target_pairs={{0,16},{4,20},{8,24},{12,28},{16,0},{20,4},{24,8},{28,12},{1,17},{... | collective-permute-start | bytes 3538952 | tf_op jit(solution)/shard_map/ppermute | solution.py:25
  172.3 36.4 %collective-permute-start.25 = (bf16[2,3,256,256]{3,2,1,0:T(8,128)(2,1)S(1)}, bf16[2,3,256,256]{3,2,1,0:T(8,128)(2,1)S(1)}, u32[]{:S(2)}, u32[]{:S(2)}) collective-permute-start(bf16[2,3,256,256]{3,2,1,0:T(8,128)(2,1)S(1)} %pad_maximum_fusion.8.refs_0_), channel_id=1, source_target_pairs={{0,8},{4,12},{8,0},{12,4},{16,24},{20,28},{24,16},{28,20},{1,9},{5... | collective-permute-start | bytes 2359304 | tf_op jit(solution)/shard_map/ppermute | solution.py:25
  175.0 33.6 %collective-permute-start.23 = (bf16[1,3,256,384]{3,2,1,0:T(8,128)(2,1)S(1)}, bf16[1,3,256,384]{3,2,1,0:T(8,128)(2,1)S(1)}, u32[]{:S(2)}, u32[]{:S(2)}) collective-permute-start(bf16[1,3,256,384]{3,2,1,0:T(8,128)(2,1)S(1)} %maximum_bitcast_fusion.2), channel_id=1, source_target_pairs={{0,16},{4,20},{8,24},{12,28},{16,0},{20,4},{24,8},{28,12},{1,17},{... | collective-permute-start | bytes 1769480 | tf_op jit(solution)/shard_map/ppermute | solution.py:25
  175.6 33.0 %collective-permute-start.22 = (bf16[1,3,256,384]{3,2,1,0:T(8,128)(2,1)S(1)}, bf16[1,3,256,384]{3,2,1,0:T(8,128)(2,1)S(1)}, u32[]{:S(2)}, u32[]{:S(2)}) collective-permute-start(bf16[1,3,256,384]{3,2,1,0:T(8,128)(2,1)S(1)} %maximum_bitcast_fusion.1), channel_id=1, source_target_pairs={{0,8},{4,12},{8,0},{12,4},{16,24},{20,28},{24,16},{28,20},{1,9},{5... | collective-permute-start | bytes 1769480 | tf_op jit(solution)/shard_map/ppermute | solution.py:25
  217.0 28.7 %collective-permute-start.32 = (bf16[2,3,256,384]{3,2,1,0:T(8,128)(2,1)S(1)}, bf16[2,3,256,384]{3,2,1,0:T(8,128)(2,1)}, u32[]{:S(2)}, u32[]{:S(2)}) collective-permute-start(bf16[2,3,256,384]{3,2,1,0:T(8,128)(2,1)S(1)} %pad_maximum_fusion.4.refs_0_), channel_id=1, source_target_pairs={{0,4},{4,0},{8,12},{12,8},{16,20},{20,16},{24,28},{28,24},{1,5},{5... | collective-permute-start | bytes 3538952 | tf_op jit(solution)/shard_map/ppermute | solution.py:25
  329.4 36.8 %collective-permute-start.39 = (bf16[2,1024,384]{2,1,0:T(8,128)(2,1)}, bf16[2,1024,384]{2,1,0:T(8,128)(2,1)}, u32[]{:S(2)}, u32[]{:S(2)}) collective-permute-start(bf16[2,1024,384]{2,1,0:T(8,128)(2,1)} %slice.224), channel_id=1, source_target_pairs={{0,16},{4,20},{8,24},{12,28},{16,0},{20,4},{24,8},{28,12},{1,17},{... | collective-permute-start | bytes 4718600 | tf_op jit(solution)/shard_map/ppermute | solution.py:25
  369.8 75.3 %collective-permute-start.41 = (bf16[2,1024,640]{2,1,0:T(8,128)(2,1)}, bf16[2,1024,640]{2,1,0:T(8,128)(2,1)}, u32[]{:S(2)}, u32[]{:S(2)}) collective-permute-start(bf16[2,1024,640]{2,1,0:T(8,128)(2,1)} %slice.227), channel_id=1, source_target_pairs={{0,8},{4,12},{8,0},{12,4},{16,24},{20,28},{24,16},{28,20},{1,9},{5... | collective-permute-start | bytes 7864328 | tf_op jit(solution)/shard_map/ppermute | solution.py:25
  372.6 72.4 %collective-permute-start.40 = (bf16[2,1024,384]{2,1,0:T(8,128)(2,1)}, bf16[2,1024,384]{2,1,0:T(8,128)(2,1)}, u32[]{:S(2)}, u32[]{:S(2)}) collective-permute-start(bf16[2,1024,384]{2,1,0:T(8,128)(2,1)} %slice.226), channel_id=1, source_target_pairs={{0,16},{4,20},{8,24},{12,28},{16,0},{20,4},{24,8},{28,12},{1,17},{... | collective-permute-start | bytes 4718600 | tf_op jit(solution)/shard_map/ppermute | solution.py:25
  377.2 67.8 %collective-permute-start.42 = (bf16[1,1024,384]{2,1,0:T(8,128)(2,1)}, bf16[1,1024,384]{2,1,0:T(8,128)(2,1)}, u32[]{:S(2)}, u32[]{:S(2)}) collective-permute-start(bf16[1,1024,384]{2,1,0:T(8,128)(2,1)} %slice.271), channel_id=1, source_target_pairs={{0,8},{4,12},{8,0},{12,4},{16,24},{20,28},{24,16},{28,20},{1,9},{5... | collective-permute-start | bytes 2359304 | tf_op jit(solution)/shard_map/ppermute | solution.py:25
  448.5 29.2 %collective-permute-start.44 = (bf16[1,1024,640]{2,1,0:T(8,128)(2,1)S(1)}, bf16[1,1024,640]{2,1,0:T(8,128)(2,1)}, u32[]{:S(2)}, u32[]{:S(2)}) collective-permute-start(bf16[1,1024,640]{2,1,0:T(8,128)(2,1)S(1)} %slice.273), channel_id=1, source_target_pairs={{0,16},{4,20},{8,24},{12,28},{16,0},{20,4},{24,8},{28,12},{1,17},{... | collective-permute-start | bytes 3932168 | tf_op jit(solution)/shard_map/ppermute | solution.py:25
  477.7 30.9 %collective-permute-start.45 = (bf16[4,1024,256]{2,1,0:T(8,128)(2,1)S(1)}, bf16[4,1024,256]{2,1,0:T(8,128)(2,1)S(1)}, u32[]{:S(2)}, u32[]{:S(2)}) collective-permute-start(bf16[4,1024,256]{2,1,0:T(8,128)(2,1)S(1)} %get-tuple-element.222), channel_id=1, source_target_pairs={{0,4},{4,0},{8,12},{12,8},{16,20},{20,16},{24,28},{28,24},{1,5},{5... | collective-permute-start | bytes 6291464 | tf_op jit(solution)/shard_map/ppermute | solution.py:25
  477.7 32.2 %collective-permute-start.46 = (bf16[4,1024,256]{2,1,0:T(8,128)(2,1)S(1)}, bf16[4,1024,256]{2,1,0:T(8,128)(2,1)}, u32[]{:S(2)}, u32[]{:S(2)}) collective-permute-start(bf16[4,1024,256]{2,1,0:T(8,128)(2,1)S(1)} %get-tuple-element.223), channel_id=1, source_target_pairs={{0,4},{4,0},{8,12},{12,8},{16,20},{20,16},{24,28},{28,24},{1,5},{5... | collective-permute-start | bytes 6291464 | tf_op jit(solution)/shard_map/ppermute | solution.py:25
  501.4 51.4 %collective-permute-start.50 = (bf16[256,1024]{1,0:T(8,128)(2,1)}, bf16[256,1024]{1,0:T(8,128)(2,1)}, u32[]{:S(2)}, u32[]{:S(2)}) collective-permute-start(bf16[256,1024]{1,0:T(8,128)(2,1)} %get-tuple-element.229), channel_id=1, source_target_pairs={{0,2},{1,3},{2,0},{3,1},{4,6},{5,7},{6,4},{7,5},{8,10},{9,11},{10,... | collective-permute-start | bytes 1572872 | tf_op jit(solution)/shard_map/ppermute | solution.py:30
  506.5 47.9 %collective-permute-start.58 = (bf16[256,1024]{1,0:T(8,128)(2,1)S(1)}, bf16[256,1024]{1,0:T(8,128)(2,1)S(1)}, u32[]{:S(2)}, u32[]{:S(2)}) collective-permute-start(bf16[256,1024]{1,0:T(8,128)(2,1)S(1)} %get-tuple-element.282), channel_id=1, source_target_pairs={{0,1},{1,2},{2,3},{3,0},{4,5},{5,6},{6,7},{7,4},{8,9},{9,10},{10,1... | collective-permute-start | bytes 1572872 | tf_op jit(solution)/shard_map/ppermute | solution.py:30
  519.0 77.3 %collective-permute-start.47 = (bf16[2,1024,256]{2,1,0:T(8,128)(2,1)S(1)}, bf16[2,1024,256]{2,1,0:T(8,128)(2,1)S(1)}, u32[]{:S(2)}, u32[]{:S(2)}) collective-permute-start(bf16[2,1024,256]{2,1,0:T(8,128)(2,1)S(1)} %slice.234), channel_id=1, source_target_pairs={{0,16},{4,20},{8,24},{12,28},{16,0},{20,4},{24,8},{28,12},{1,17},{... | collective-permute-start | bytes 3145736 | tf_op jit(solution)/shard_map/ppermute | solution.py:25
  519.6 77.5 %collective-permute-start.48 = (bf16[2,1024,256]{2,1,0:T(8,128)(2,1)S(1)}, bf16[2,1024,256]{2,1,0:T(8,128)(2,1)S(1)}, u32[]{:S(2)}, u32[]{:S(2)}) collective-permute-start(bf16[2,1024,256]{2,1,0:T(8,128)(2,1)S(1)} %slice.235), channel_id=1, source_target_pairs={{0,8},{4,12},{8,0},{12,4},{16,24},{20,28},{24,16},{28,20},{1,9},{5... | collective-permute-start | bytes 3145736 | tf_op jit(solution)/shard_map/ppermute | solution.py:25
  552.4 43.9 %collective-permute-start.55 = (bf16[256,384]{1,0:T(8,128)(2,1)S(1)}, bf16[256,384]{1,0:T(8,128)(2,1)S(1)}, u32[]{:S(2)}, u32[]{:S(2)}) collective-permute-start(bf16[256,384]{1,0:T(8,128)(2,1)S(1)} %get-tuple-element.235), channel_id=1, source_target_pairs={{0,3},{1,0},{2,1},{3,2},{4,7},{5,4},{6,5},{7,6},{8,11},{9,8},{10,9... | collective-permute-start | bytes 589832 | tf_op jit(solution)/shard_map/ppermute | solution.py:30
  552.8 43.4 %collective-permute-start.51 = (bf16[256,1024]{1,0:T(8,128)(2,1)S(1)}, bf16[256,1024]{1,0:T(8,128)(2,1)S(1)}, u32[]{:S(2)}, u32[]{:S(2)}) collective-permute-start(bf16[256,1024]{1,0:T(8,128)(2,1)S(1)} %copy-done.58), channel_id=1, source_target_pairs={{0,1},{1,2},{2,3},{3,0},{4,5},{5,6},{6,7},{7,4},{8,9},{9,10},{10,1... | collective-permute-start | bytes 1572872 | tf_op jit(solution)/shard_map/ppermute | solution.py:30
  554.4 36.4 %collective-permute-start.59 = (bf16[256,1024]{1,0:T(8,128)(2,1)S(1)}, bf16[256,1024]{1,0:T(8,128)(2,1)S(1)}, u32[]{:S(2)}, u32[]{:S(2)}) collective-permute-start(bf16[256,1024]{1,0:T(8,128)(2,1)S(1)} %copy-done.59), channel_id=1, source_target_pairs={{0,2},{1,3},{2,0},{3,1},{4,6},{5,7},{6,4},{7,5},{8,10},{9,11},{10,... | collective-permute-start | bytes 1572872 | tf_op jit(solution)/shard_map/ppermute | solution.py:30
  (120 other events, 1590.9 us)
